TPU v7x, 256 devices: a whole 4x4x8 slice. The times are simulated.
256 devices in a mesh: dp: 32 (over x, z), tensor: 8 (over y, core).
Axes of the slice: x: 4, y: 4, z: 8, core: 2. Of those that a mesh axis runs over, the one named last changes fastest.
Arguments:
- queries: bfloat16 [8192, 4096], P('dp', 'tensor'), may hold values from -64 to 64
- keys: bfloat16 [32768, 4096], P('dp', 'tensor'), may hold values from -16 to 16
- values: bfloat16 [32768, 4096], P('dp', 'tensor'), may hold values from -6 to 6
- out_weight: bfloat16 [4096, 8192], P('tensor', 'dp'), may hold values from -0.75 to 0.75
- grad_out: bfloat16 [8192, 8192], P(('dp', 'tensor')), may hold values from -1.5 to 1.5
- neighbour_owner: int32 [128, 2], P('dp'), may hold values from 0 to 31, all different within a row; in each aligned block of 4 rows (0 to 3, 4 to 7, ...) no two rows name the same one
- neighbour_local: int32 [128, 2], P('dp'), may hold values from 0 to 7
Outputs:
- attended_out: bfloat16 [8192, 8192], P(('dp', 'tensor'))
- grad_queries: bfloat16 [8192, 4096], P('dp', 'tensor')
- grad_keys: float32 [32768, 4096], P('dp', 'tensor')
- grad_values: float32 [32768, 4096], P('dp', 'tensor')
Inputs may be any that keep to these rules, and one draw needn't show every extreme that they name: `neighbour_owner`: among the groups of one index of dp, each owner is named at most 1 times, and exactly 1 times somewhere; the 2 owners of a group differ.
All inputs are finite; a program needn't handle non-finite values.
Results may differ from a plain program's by a relative error of at most 0.04.
Values may be sent and summed in bfloat16 or wider, within the bound.
A program may use at most 128 MiB of HBM per device.

v0:
```python
import jax
import jax.numpy as jnp
from jax import lax
from jax.sharding import PartitionSpec as P

HD = 128
GROUP = 64
NLEN = 128
NB_DEV = 8


def split_heads(tensor, head_width):
    return tensor.reshape(tensor.shape[:-1] + (tensor.shape[-1] // head_width, head_width))


def partial_attend(query_rows, key_rows, value_rows, score_scale):
    scores = (
        jnp.einsum(
            "...qhd,...khd->...hqk", query_rows, key_rows, preferred_element_type=jnp.float32
        )
        * score_scale
    )
    peak_value = jnp.max(scores, axis=-1)
    exponent = jnp.exp(scores - peak_value[..., None])
    exp_total = jnp.sum(exponent, axis=-1)
    weighted = jnp.einsum(
        "...hqk,...khd->...hqd",
        exponent.astype(jnp.bfloat16),
        value_rows,
        preferred_element_type=jnp.float32,
    )
    return (peak_value, exp_total, weighted)


def combine_parts(peak_value, exp_total, weighted):
    top_peak = jnp.max(peak_value, axis=1, keepdims=True)
    factor = jnp.exp(peak_value - top_peak)
    denominator = jnp.sum(factor * exp_total, axis=1)
    merged = jnp.sum(factor[..., None] * weighted, axis=1) / denominator[..., None]
    return (merged, top_peak[:, 0] + jnp.log(denominator))


def attend_grads(query_rows, key_rows, value_rows, upstream, log_total, inner_term, score_scale):
    scores = (
        jnp.einsum(
            "...qhd,...khd->...hqk", query_rows, key_rows, preferred_element_type=jnp.float32
        )
        * score_scale
    )
    back_prob = jnp.exp(scores - log_total[..., None])
    grad_value = jnp.einsum(
        "...hqk,...qhd->...khd",
        back_prob.astype(jnp.bfloat16),
        upstream,
        preferred_element_type=jnp.float32,
    ).astype(jnp.bfloat16)
    grad_probs = jnp.einsum(
        "...qhd,...khd->...hqk", upstream, value_rows, preferred_element_type=jnp.float32
    )
    grad_scores = (back_prob * (grad_probs - inner_term[..., None])).astype(jnp.bfloat16)
    grad_key = (
        jnp.einsum(
            "...hqk,...qhd->...khd", grad_scores, query_rows, preferred_element_type=jnp.float32
        )
        * score_scale
    ).astype(jnp.bfloat16)
    grad_query = (
        jnp.einsum(
            "...hqk,...khd->...qhd", grad_scores, key_rows, preferred_element_type=jnp.float32
        )
        * score_scale
    )
    return (grad_key, grad_value, grad_query)


def shards(queries, keys, values, out_weight, grad_out, neighbour_owner, neighbour_local):
    score_scale = HD ** (-0.5)
    dp_size = lax.axis_size("dp")
    group_count, per_group = neighbour_owner.shape
    use_count = group_count * per_group
    capacity = max(1, 2 * use_count // dp_size)
    slot_total = dp_size * capacity
    tok_rows, head_cols = queries.shape
    owners = neighbour_owner.reshape(-1)
    local_ids = neighbour_local.reshape(-1)
    order_ids = jnp.arange(use_count)
    matches = (owners[:, None] == owners[None, :]) & (order_ids[None, :] < order_ids[:, None])
    slot_rank = jnp.sum(matches.astype(jnp.int32), axis=1)
    slot_index = owners * capacity + slot_rank
    key_table = keys.reshape(NB_DEV, NLEN, head_cols)
    value_table = values.reshape(NB_DEV, NLEN, head_cols)
    query_use = jnp.repeat(queries.reshape(group_count, GROUP, head_cols), per_group, axis=0)
    request = (
        jnp.zeros((slot_total,), jnp.int32).at[slot_index].set(local_ids).reshape(dp_size, capacity)
    )
    full_weight = lax.all_gather(out_weight, "dp", axis=1, tiled=True)

    def pick_slots(buffer):
        return buffer.reshape((slot_total,) + buffer.shape[2:])[slot_index]

    def place_slots(items):
        filled = jnp.zeros((slot_total,) + items.shape[1:], items.dtype).at[slot_index].set(items)
        return filled.reshape((dp_size, capacity) + items.shape[1:])

    owner_ids = lax.all_to_all(request, "dp", split_axis=0, concat_axis=0, tiled=True)
    rows_keys, rows_values = (
        lax.all_to_all(key_table[owner_ids], "dp", split_axis=0, concat_axis=0, tiled=True),
        lax.all_to_all(value_table[owner_ids], "dp", split_axis=0, concat_axis=0, tiled=True),
    )
    use_keys = split_heads(pick_slots(rows_keys), HD)
    use_values = split_heads(pick_slots(rows_values), HD)
    use_peak, use_total, use_weighted = partial_attend(
        split_heads(query_use, HD), use_keys, use_values, score_scale
    )
    pair_shape = (group_count, per_group)
    merged, log_total = combine_parts(
        use_peak.reshape(pair_shape + use_peak.shape[1:]),
        use_total.reshape(pair_shape + use_total.shape[1:]),
        use_weighted.reshape(pair_shape + use_weighted.shape[1:]),
    )
    context = merged.transpose(0, 2, 1, 3).reshape(tok_rows, head_cols).astype(jnp.bfloat16)
    attended_out = lax.psum_scatter(
        jnp.dot(context, full_weight, preferred_element_type=jnp.float32).astype(jnp.bfloat16),
        "tensor",
        scatter_dimension=0,
        tiled=True,
    )
    upstream = lax.dot_general(
        lax.all_gather(grad_out, "tensor", axis=0, tiled=True),
        full_weight,
        (((1,), (1,)), ((), ())),
        preferred_element_type=jnp.float32,
    ).astype(jnp.bfloat16)
    inner_term = jnp.sum(
        split_heads(upstream.astype(jnp.float32) * context.astype(jnp.float32), HD), axis=-1
    )
    inner_groups = inner_term.reshape(group_count, GROUP, -1).transpose(0, 2, 1)
    inner_use = jnp.repeat(inner_groups, per_group, axis=0)
    log_use = jnp.repeat(log_total, per_group, axis=0)
    upstream_use = jnp.repeat(upstream.reshape(group_count, GROUP, head_cols), per_group, axis=0)
    grad_key, grad_value, query_grad = attend_grads(
        split_heads(query_use, HD),
        use_keys,
        use_values,
        split_heads(upstream_use, HD),
        log_use,
        inner_use,
        score_scale,
    )
    query_grad_use = query_grad.reshape(use_count, GROUP, head_cols)
    owner_key_grads, owner_value_grads = (
        lax.all_to_all(
            place_slots(grad_key.reshape(use_count, NLEN, head_cols)),
            "dp",
            split_axis=0,
            concat_axis=0,
            tiled=True,
        ),
        lax.all_to_all(
            place_slots(grad_value.reshape(use_count, NLEN, head_cols)),
            "dp",
            split_axis=0,
            concat_axis=0,
            tiled=True,
        ),
    )
    grad_queries = jnp.sum(query_grad_use.reshape(group_count, per_group, GROUP, head_cols), axis=1)
    grad_queries = grad_queries.reshape(tok_rows, head_cols).astype(jnp.bfloat16)
    flat_ids = owner_ids.reshape(-1)
    key_terms = owner_key_grads.reshape(slot_total, NLEN, head_cols).astype(jnp.float32)
    value_terms = owner_value_grads.reshape(slot_total, NLEN, head_cols).astype(jnp.float32)
    grad_keys = jnp.zeros((NB_DEV, NLEN, head_cols), jnp.float32).at[flat_ids].add(key_terms)
    grad_values = jnp.zeros((NB_DEV, NLEN, head_cols), jnp.float32).at[flat_ids].add(value_terms)
    return (
        attended_out,
        grad_queries,
        grad_keys.reshape(keys.shape),
        grad_values.reshape(values.shape),
    )


def solution(mesh):
    return jax.shard_map(
        shards,
        mesh=mesh,
        in_specs=(
            P("dp", "tensor"),
            P("dp", "tensor"),
            P("dp", "tensor"),
            P("tensor", "dp"),
            P(("dp", "tensor"), None),
            P("dp", None),
            P("dp", None),
        ),
        out_specs=(
            P(("dp", "tensor"), None),
            P("dp", "tensor"),
            P("dp", "tensor"),
            P("dp", "tensor"),
        ),
        check_vma=False,
    )
```

profile of v0, /device:TPU:6, one launch (start us, length us, event | category | flops | bytes accessed | tf_op | source)
XLA Modules:
  0.0 540.2 jit_solution(6543540278713650892)
XLA Ops:
  10.6 19.3 %all_to_all.32 = s32[32,1,1]{2,1,0:T(1,128)S(1)} all-to-all(s32[32,1,1]{2,1,0:T(1,128)S(1)} %copy.99), channel_id=1, replica_groups=mesh['dp'=32,'tensor'=8] {'dp'}, dimensions={0} | all-to-all | bytes 256 | tf_op jit(solution)/shard_map/all_to_all | solution.py:105
  29.9 1.6 fusion.26
  31.5 2.7 gather_fusion
  34.3 6.8 %all-to-all-start.1 = ((bf16[32,1,128,512]{3,2,1,0:T(8,128)(2,1)}), bf16[32,1,128,512]{3,2,1,0:T(8,128)(2,1)}, u32[]{:S(2)}, u32[]{:S(2)}) async-start(bf16[32,1,128,512]{3,2,1,0:T(8,128)(2,1)} %bitcast.94), calls=%async_computation.1 | async-start | bytes 8388608 | tf_op jit(solution)/shard_map/all_to_all | solution.py:107
  41.9 2.8 gather_fusion.2
  44.6 100.2 %all-to-all-done.1 = bf16[32,1,128,512]{3,2,1,0:T(8,128)(2,1)} async-done(((bf16[32,1,128,512]{3,2,1,0:T(8,128)(2,1)}), bf16[32,1,128,512]{3,2,1,0:T(8,128)(2,1)}, u32[]{:S(2)}, u32[]{:S(2)}) %all-to-all-start.1) | async-done | bytes 4194336 | tf_op jit(solution)/shard_map/all_to_all | solution.py:107
  144.8 7.2 %all-to-all-start.2 = ((bf16[32,1,128,512]{3,2,1,0:T(8,128)(2,1)}), bf16[32,1,128,512]{3,2,1,0:T(8,128)(2,1)}, u32[]{:S(2)}, u32[]{:S(2)}) async-start(bf16[32,1,128,512]{3,2,1,0:T(8,128)(2,1)} %bitcast.93), calls=%async_computation.2 | async-start | bytes 8388608 | tf_op jit(solution)/shard_map/all_to_all | solution.py:108
  153.0 2.9 gather_fusion.1
  156.6 120.3 %all-to-all-done.2 = bf16[32,1,128,512]{3,2,1,0:T(8,128)(2,1)} async-done(((bf16[32,1,128,512]{3,2,1,0:T(8,128)(2,1)}), bf16[32,1,128,512]{3,2,1,0:T(8,128)(2,1)}, u32[]{:S(2)}, u32[]{:S(2)}) %all-to-all-start.2) | async-done | bytes 4194336 | tf_op jit(solution)/shard_map/all_to_all | solution.py:108
  276.9 2.8 gather_fusion.3
  280.3 1.5 fusion.28
  284.8 7.7 %convert_multiply_fusion = (f32[256,512]{1,0:T(8,128)}, bf16[256,512]{1,0:T(8,128)(2,1)S(1)}) fusion(bf16[32,8,4,128]{3,2,1,0:T(4,128)(2,1)} %bitcast.106, bf16[256,8192]{1,0:T(8,128)(2,1)} %all-gather.5.cloned.1.call-done, bf16[512,8192]{1,0:T(8,128)(2,1)} %all-gather.3.cloned.1.call-done), kind=kOutput, calls=%fused_computation.31 | convolution fusion | flops 2148007936 | bytes 13631488 | tf_op jit(solution)/shard_map/dot_general | solution.py:128
  292.6 2.0 reshape.171
  296.9 2.0 reshape_reshape.11
  298.9 1.7 fusion.3
  301.4 2.5 multiply_convert_fusion
  303.9 1.5 copy.113
  305.4 2.4 broadcast.85.clone
  307.9 2.9 scatter_fusion
  310.8 7.0 %all-to-all-start.3 = ((bf16[32,1,128,512]{3,2,1,0:T(8,128)(2,1)}), bf16[32,1,128,512]{3,2,1,0:T(8,128)(2,1)}, u32[]{:S(2)}, u32[]{:S(2)}) async-start(bf16[32,1,128,512]{3,2,1,0:T(8,128)(2,1)} %bitcast.92), calls=%async_computation.4 | async-start | bytes 8388608 | tf_op jit(solution)/shard_map/all_to_all | solution.py:152
  317.8 1.8 convolution_convert_fusion.1
  319.6 1.5 copy.116
  321.1 2.4 broadcast.85.clone.1
  323.6 2.9 scatter_fusion.2
  326.5 85.2 %all-to-all-done.3 = bf16[32,1,128,512]{3,2,1,0:T(8,128)(2,1)} async-done(((bf16[32,1,128,512]{3,2,1,0:T(8,128)(2,1)}), bf16[32,1,128,512]{3,2,1,0:T(8,128)(2,1)}, u32[]{:S(2)}, u32[]{:S(2)}) %all-to-all-start.3) | async-done | bytes 4194336 | tf_op jit(solution)/shard_map/all_to_all | solution.py:152
  411.6 8.7 %all-to-all-start.4 = ((bf16[32,1,128,512]{3,2,1,0:T(8,128)(2,1)}), bf16[32,1,128,512]{3,2,1,0:T(8,128)(2,1)}, u32[]{:S(2)}, u32[]{:S(2)}) async-start(bf16[32,1,128,512]{3,2,1,0:T(8,128)(2,1)} %bitcast.91), calls=%async_computation.5 | async-start | bytes 8388608 | tf_op jit(solution)/shard_map/all_to_all | solution.py:159
  420.4 7.7 %convolution_convert_fusion = bf16[256,8192]{1,0:T(8,128)(2,1)} fusion(bf16[512,8192]{1,0:T(8,128)(2,1)} %all-gather.3.cloned.1.call-done, bf16[32,8,4,128]{3,2,1,0:T(4,128)(2,1)S(1)} %bitcast.107), kind=kOutput, calls=%fused_computation.9 | convolution fusion | flops 2149580800 | bytes 12845056 | tf_op jit(solution)/shard_map/dot_general | solution.py:123
  431.9 6.6 %bitcast_convert_fusion.1 = f32[32,128,512]{2,1,0:T(8,128)} fusion(bf16[32,1,128,512]{3,2,1,0:T(8,128)(2,1)} %all-to-all-done.3), kind=kLoop, calls=%fused_computation.11 | loop fusion | flops 2097152 | bytes 12582912 | tf_op jit(solution)/shard_map/convert_element_type | solution.py:170
  438.7 12.0 %scatter_fusion.1 = f32[8,128,512]{2,1,0:T(8,128)S(1)} fusion(f32[8,128,512]{2,1,0:T(8,128)S(1)} %broadcast.82.clone, s32[32]{0:T(128)S(1)} %fusion.23, f32[32,128,512]{2,1,0:T(8,128)} %bitcast_convert_fusion.1), kind=kCustom, calls=%fused_computation.6 | custom fusion | flops 2097152 | bytes 25165952 | tf_op jit(solution)/shard_map/scatter-add | solution.py:172
  450.7 63.1 %all-to-all-done.4 = bf16[32,1,128,512]{3,2,1,0:T(8,128)(2,1)} async-done(((bf16[32,1,128,512]{3,2,1,0:T(8,128)(2,1)}), bf16[32,1,128,512]{3,2,1,0:T(8,128)(2,1)}, u32[]{:S(2)}, u32[]{:S(2)}) %all-to-all-start.4) | async-done | bytes 4194336 | tf_op jit(solution)/shard_map/all_to_all | solution.py:159
  513.9 6.6 %bitcast_convert_fusion = f32[32,128,512]{2,1,0:T(8,128)} fusion(bf16[32,1,128,512]{3,2,1,0:T(8,128)(2,1)} %all-to-all-done.4), kind=kLoop, calls=%fused_computation.10 | loop fusion | flops 2097152 | bytes 12582912 | tf_op jit(solution)/shard_map/convert_element_type | solution.py:171
  520.7 11.6 %scatter_fusion.3 = f32[8,128,512]{2,1,0:T(8,128)S(1)} fusion(f32[8,128,512]{2,1,0:T(8,128)S(1)} %broadcast.82.clone.1, s32[32]{0:T(128)S(1)} %fusion.23, f32[32,128,512]{2,1,0:T(8,128)} %bitcast_convert_fusion), kind=kCustom, calls=%fused_computation.8 | custom fusion | flops 2097152 | bytes 25165952 | tf_op jit(solution)/shard_map/scatter-add | solution.py:173
  (69 shorter events, 18.2 us)
Async XLA Ops:
  7.2 24.4 %copy-start = (bf16[1024,512]{1,0:T(8,128)(2,1)S(1)}, bf16[1024,512]{1,0:T(8,128)(2,1)}, u32[]{:S(2)}) copy-start(bf16[1024,512]{1,0:T(8,128)(2,1)} %param.8) | copy-start | bytes 3145732
  7.2 277.6 %all-gather.5.cloned.1.call-start = ((), (), s32[]{:S(2)}) async-start(), calls=%async_computation.8 | async-start | bytes 4718592 | tf_op jit(solution)/shard_map/all_gather | solution.py:129
  9.9 143.1 %copy-start.10 = (s32[8]{0:T(128)}, s32[8]{0:T(128)S(1)}, u32[]{:S(2)}) copy-start(s32[8]{0:T(128)S(1)} %fusion.22) | copy-start | bytes 100
  34.3 7.6 %copy-start.4 = (bf16[1024,512]{1,0:T(8,128)(2,1)S(1)}, bf16[1024,512]{1,0:T(8,128)(2,1)}, u32[]{:S(2)}) copy-start(bf16[1024,512]{1,0:T(8,128)(2,1)} %param.9) | copy-start | bytes 3145732
  34.3 110.6 %all-to-all-start.1 = ((bf16[32,1,128,512]{3,2,1,0:T(8,128)(2,1)}), bf16[32,1,128,512]{3,2,1,0:T(8,128)(2,1)}, u32[]{:S(2)}, u32[]{:S(2)}) async-start(bf16[32,1,128,512]{3,2,1,0:T(8,128)(2,1)} %bitcast.94), calls=%async_computation.1 | async-start | bytes 8388608 | tf_op jit(solution)/shard_map/all_to_all | solution.py:107
  41.1 243.7 %all-gather.3.cloned.1.call-start = ((), (), s32[]{:S(2)}) async-start(), calls=%async_computation.6 | async-start | bytes 8650752 | tf_op jit(solution)/shard_map/all_gather | solution.py:96
  144.8 7.2 %copy-start.8 = (bf16[256,512]{1,0:T(8,128)(2,1)S(1)}, bf16[256,512]{1,0:T(8,128)(2,1)}, u32[]{:S(2)}) copy-start(bf16[256,512]{1,0:T(8,128)(2,1)} %param.7) | copy-start | bytes 786436
  144.8 132.0 %all-to-all-start.2 = ((bf16[32,1,128,512]{3,2,1,0:T(8,128)(2,1)}), bf16[32,1,128,512]{3,2,1,0:T(8,128)(2,1)}, u32[]{:S(2)}, u32[]{:S(2)}) async-start(bf16[32,1,128,512]{3,2,1,0:T(8,128)(2,1)} %bitcast.93), calls=%async_computation.2 | async-start | bytes 8388608 | tf_op jit(solution)/shard_map/all_to_all | solution.py:108
  300.6 0.8 copy-start.6
  301.4 6.4 %copy-start.11 = (s32[8]{0:T(128)S(1)}, s32[8]{0:T(128)}, u32[]{:S(2)}) copy-start(s32[8]{0:T(128)} %copy-done.10) | copy-start | bytes 100
  310.8 7.0 %copy-start.5 = (bf16[8,64,4,128]{3,2,1,0:T(4,128)(2,1)S(1)}, bf16[8,64,4,128]{3,2,1,0:T(4,128)(2,1)}, u32[]{:S(2)}) copy-start(bf16[8,64,4,128]{3,2,1,0:T(4,128)(2,1)} %reshape_reshape.11) | copy-start | bytes 1572868
  310.8 100.9 %all-to-all-start.3 = ((bf16[32,1,128,512]{3,2,1,0:T(8,128)(2,1)}), bf16[32,1,128,512]{3,2,1,0:T(8,128)(2,1)}, u32[]{:S(2)}, u32[]{:S(2)}) async-start(bf16[32,1,128,512]{3,2,1,0:T(8,128)(2,1)} %bitcast.92), calls=%async_computation.4 | async-start | bytes 8388608 | tf_op jit(solution)/shard_map/all_to_all | solution.py:152
  411.6 8.7 %copy-start.9 = (bf16[4,64,4,128]{3,2,1,0:T(4,128)(2,1)S(1)}, bf16[4,64,4,128]{3,2,1,0:T(4,128)(2,1)}, u32[]{:S(2)}) copy-start(bf16[4,64,4,128]{3,2,1,0:T(4,128)(2,1)} %copy.105) | copy-start | bytes 786436
  411.6 102.2 %all-to-all-start.4 = ((bf16[32,1,128,512]{3,2,1,0:T(8,128)(2,1)}), bf16[32,1,128,512]{3,2,1,0:T(8,128)(2,1)}, u32[]{:S(2)}, u32[]{:S(2)}) async-start(bf16[32,1,128,512]{3,2,1,0:T(8,128)(2,1)} %bitcast.91), calls=%async_computation.5 | async-start | bytes 8388608 | tf_op jit(solution)/shard_map/all_to_all | solution.py:159
  420.3 112.0 %reduce-scatter.2.cloned.1.call-start = ((), (), s32[]{:S(2)}) async-start(), calls=%async_computation.7 | async-start | bytes 4718592 | tf_op jit(solution)/shard_map/reduce_scatter | solution.py:122
  428.1 0.7 copy-start.12
  428.1 1.0 copy-start.7
  450.7 63.2 %copy-start.3 = (f32[8,128,512]{2,1,0:T(8,128)}, f32[8,128,512]{2,1,0:T(8,128)S(1)}, u32[]{:S(2)}) copy-start(f32[8,128,512]{2,1,0:T(8,128)S(1)} %scatter_fusion.1) | copy-start | bytes 6291460
  520.7 12.9 %copy-start.1 = (bf16[1024,512]{1,0:T(8,128)(2,1)S(1)}, bf16[1024,512]{1,0:T(8,128)(2,1)}, u32[]{:S(2)}) copy-start(bf16[1024,512]{1,0:T(8,128)(2,1)} %param.8) | copy-start | bytes 3145732
  532.3 1.3 copy-start.2
Sparse Core Ops, SparseCore 0:
  9.9 37.5 all-gather.4
  50.0 225.6 all-gather.2
  428.2 41.9 reduce-scatter.1
where the time goes:
time: 544 us; the launch traced here: 540 us
  waiting for transfers between devices  370 us (68%)
  other arithmetic  41.7 us (8%)
  local copies, waits for them, and re-layouts  40.2 us (7%)
  starting transfers between devices  29.8 us (5%)
  matrix products  24.8 us (5%)
  blocking collectives  19.3 us (4%)
  between operations  14.1 us (3%)
    all_to_all x1, waiting for transfers between devices, shards(): lax.all_to_all(value_table[owner_ids], 'dp', split_axis=0, concat_axis=0,...  120 us
    all_to_all x1, waiting for transfers between devices, shards(): lax.all_to_all(key_table[owner_ids], 'dp', split_axis=0, concat_axis=0, t...  100 us
    all_to_all x1, waiting for transfers between devices, shards(): lax.all_to_all(place_slots(grad_key.reshape(use_count, NLEN, head_cols)),...  85.2 us
    all_to_all x1, waiting for transfers between devices, shards(): lax.all_to_all(place_slots(grad_value.reshape(use_count, NLEN, head_cols)...  63.1 us
    scatter-add x2, other arithmetic, shards(): jnp.zeros((NB_DEV, NLEN, head_cols), jnp.float32).at[flat_ids]  23.6 us
    all_to_all x1, blocking collectives, shards(): lax.all_to_all(request, 'dp', split_axis=0, concat_axis=0, tiled=True)  19.3 us
  transfers between devices with their start and end apart: 7, of which 4 were waited for; matrix products, arithmetic and copies ran while one was open for 15% of the time, Pallas kernels for 0%

commit v1 on v0

v1 whole, which is shorter than its diff:
```python
import jax
import jax.numpy as jnp
from jax import lax
from jax.experimental import pallas as pl
from jax.experimental.pallas import tpu as pltpu
from jax.sharding import PartitionSpec as P

X, Z, Y, C = 4, 8, 4, 2
HD = 128
GROUP = 64
NLEN = 128
NB_DEV = 8
TOK = 256
SCALE = HD**-0.5
LOW = -1e30
BF = jnp.bfloat16
F32 = jnp.float32
VMEM = pl.BlockSpec(memory_space=pltpu.VMEM)
SMEM = pl.BlockSpec(memory_space=pltpu.SMEM)
LIMIT = 60 * 1024 * 1024


def place():
    dp, t = lax.axis_index("dp"), lax.axis_index("tensor")
    return lax.div(dp, Z), lax.rem(dp, Z), lax.div(t, C), lax.rem(t, C)


def device(x, z, y, c):
    return (x * Z + z, y * C + c)


def step_from(i, by, n):
    return lax.rem(i + (by + n), n)


def columns(i, width):
    return pl.ds(pl.multiple_of(i * width, width), width)


def enter(peers):
    barrier = pltpu.get_barrier_semaphore()
    for peer in peers:
        pl.semaphore_signal(barrier, inc=1, device_id=peer, device_id_type=pl.DeviceIdType.MESH)
    pl.semaphore_wait(barrier, len(peers))


class Copies:
    def __init__(self, send, recv):
        self.send, self.recv, self.count, self.started = send, recv, 0, []

    def take(self, n=1):
        first = self.count
        self.count += n
        return first

    def make(self, sem, src, dst, to):
        return pltpu.make_async_remote_copy(
            src_ref=src,
            dst_ref=dst,
            send_sem=self.send.at[sem],
            recv_sem=self.recv.at[sem],
            device_id=to,
            device_id_type=pl.DeviceIdType.MESH,
        )

    def start(self, src, dst, to):
        copy = self.make(self.take(), src, dst, to)
        copy.start()
        self.started.append(copy)
        return copy

    def finish(self):
        for copy in self.started:
            copy.wait_send()


class Gather:
    def __init__(self, copies, first, view, hops, where):
        self.copies, self.first, self.view, self.hops, self.where = copies, first, view, hops, where
        self.sent = [[], []]

    def step(self, s):
        x, z, y, c = self.where
        for way, sign in ((0, 1), (1, -1)):
            if 0 < s <= self.hops[way]:
                self.sent[way][s - 1].wait_recv()
            if s < self.hops[way]:
                block = step_from(z, -sign * s, Z)
                src = self.first if s == 0 else self.view(block)
                to = device(x, step_from(z, sign, Z), y, c)
                self.sent[way].append(self.copies.start(src, self.view(block), to))


class Scatter:
    def __init__(self, copies, part, held, hops, where):
        self.copies, self.part, self.held, self.hops, self.where = copies, part, held, hops, where
        self.sent = [[], []]

    def step(self, s):
        x, z, y, c = self.where
        for way, sign in ((0, 1), (1, -1)):
            n = self.hops[way]
            if 0 < s <= n:
                self.sent[way][s - 1].wait_recv()
            if s < n:
                goal = step_from(z, sign * (n - s), Z)
                if s == 0:
                    src = self.part(goal)
                else:
                    src = self.held(way, s - 1)
                    src[...] = (src[...].astype(F32) + self.part(goal)[...].astype(F32)).astype(BF)
                to = device(x, step_from(z, sign, Z), y, c)
                self.sent[way].append(self.copies.start(src, self.held(way, s), to))

    def total(self):
        z = self.where[1]
        total = self.part(z)[...].astype(F32)
        for way in (0, 1):
            total += self.held(way, self.hops[way] - 1)[...].astype(F32)
        return total


HOPS = ((4, 3), (3, 4))


def spread_kernel(
    q_ref, k_ref, v_ref, w_ref, g_ref,
    qall, ktab, vtab, wf, upall,
    gfull, upp, upr, send, recv, local,
):
    where = x, z, y, c = place()
    t = y * C + c
    depth = w_ref.shape[0] // 4
    width = w_ref.shape[1]
    span = Z * width
    xs = [step_from(x, i, X) for i in range(X)]
    ys = [step_from(y, i, Y) for i in range(Y)]
    other = 1 - c
    enter(
        [device(xs[i], z, y, c) for i in (1, 2, 3)]
        + [device(x, step_from(z, i, Z), y, c) for i in (1, -1)]
        + [device(x, z, ys[i], c) for i in (1, 2, 3)]
        + [device(x, z, y, other)]
    )
    copies = Copies(send, recv)
    kept = []

    def keep(src, dst):
        copy = pltpu.make_async_copy(src, dst, local.at[len(kept)])
        copy.start()
        kept.append(copy)

    keep(g_ref.at[:, columns(x, span)], gfull.at[x, t])
    keep(q_ref.at[:, columns(x, HD)], qall.at[z, x])
    keep(k_ref.at[:, columns(x, HD)], ktab.at[x])
    keep(v_ref.at[:, columns(x, HD)], vtab.at[x])
    keep(w_ref, wf.at[:, columns(z, width)])

    g_in = [
        copies.start(g_ref.at[:, columns(xs[i], span)], gfull.at[x, t], device(xs[i], z, y, c))
        for i in (1, 3, 2)
    ]

    def weight_piece(i):
        rows = pl.ds(i * depth, depth)
        return Gather(
            copies, w_ref.at[rows], lambda b: wf.at[rows, columns(b, width)], HOPS[i % 2], where
        )

    def piece(ref, i):
        return Gather(copies, ref.at[z, i], lambda b: ref.at[b, i], HOPS[i % 2], where)

    pieces = [weight_piece(i) for i in range(4)]
    pieces += [piece(qall, i) for i in range(X)]
    pieces += [piece(upall, i) for i in range(X)]

    table_in, q_in, g_y, g_core, up_in = [], [], {}, {}, {}

    def before(wave):
        if wave == 4:
            for copy in q_in:
                copy.wait_recv()
            kept[1].wait()
        if 8 <= wave < 8 + X:
            i = wave - 8
            for copy in up_in[i]:
                copy.wait_recv()
            total = upp[i, :, columns(x, HD)].astype(F32)
            for j in range(3):
                total += upr[i, j].astype(F32)
            upall[z, i] = total.astype(BF)

    def after(wave):
        if wave == 0:
            for i in (1, 3, 2):
                q_in.append(
                    copies.start(
                        q_ref.at[:, columns(xs[i], HD)], qall.at[z, x], device(xs[i], z, y, c)
                    )
                )
            kept[0].wait()
            for copy in g_in:
                copy.wait_recv()
            for i in range(X):
                block = gfull.at[i, t]
                g_y[i] = [copies.start(block, block, device(x, z, ys[j], c)) for j in (1, 3, 2)]
                g_core[i] = [copies.start(block, block, device(x, z, y, other))]
            for i in (1, 3, 2):
                for src, dst in ((k_ref, ktab), (v_ref, vtab)):
                    table_in.append(
                        copies.start(
                            src.at[:, columns(xs[i], HD)], dst.at[x], device(xs[i], z, y, c)
                        )
                    )
        if 3 <= wave < 3 + X:
            i = wave - 3
            for copy, j in zip(g_y[i], (-1, -3, -2)):
                copy.wait_recv()
                block = gfull.at[i, step_from(y, j, Y) * C + c]
                g_core[i].append(copies.start(block, block, device(x, z, y, other)))
        if 7 <= wave < 7 + X:
            i = wave - 7
            if wave == 7:
                kept[4].wait()
            for copy in g_core[i]:
                copy.wait_recv()
            rows = gfull[i].reshape(TOK, span)
            upp[i] = lax.dot_general(
                rows, wf[...], (((1,), (1,)), ((), ())), preferred_element_type=F32
            ).astype(BF)
            up_in[i] = [
                copies.start(
                    upp.at[i, :, columns(xs[j], HD)], upr.at[i, j - 1], device(xs[j], z, y, c)
                )
                for j in (1, 3, 2)
            ]

    for wave in range(len(pieces) + 4):
        before(wave)
        for i, one in enumerate(pieces):
            if 0 <= wave - i <= 4:
                one.step(wave - i)
        after(wave)
    for copy in table_in:
        copy.wait_recv()
    for copy in kept[2:4]:
        copy.wait()
    copies.finish()


def spread(queries, keys, values, out_weight, grad_out):
    depth, width = out_weight.shape
    rows, head_cols = keys.shape
    return pl.pallas_call(
        spread_kernel,
        out_shape=(
            jax.ShapeDtypeStruct((Z, X, TOK, HD), BF),
            jax.ShapeDtypeStruct((X, rows, HD), BF),
            jax.ShapeDtypeStruct((X, rows, HD), BF),
            jax.ShapeDtypeStruct((depth, Z * width), BF),
            jax.ShapeDtypeStruct((Z, X, TOK, HD), BF),
        ),
        in_specs=[VMEM] * 5,
        out_specs=[VMEM] * 5,
        scratch_shapes=[
            pltpu.VMEM((X, Y * C, grad_out.shape[0], Z * width), BF),
            pltpu.VMEM((X, TOK, head_cols), BF),
            pltpu.VMEM((X, X - 1, TOK, HD), BF),
            pltpu.SemaphoreType.DMA((140,)),
            pltpu.SemaphoreType.DMA((140,)),
            pltpu.SemaphoreType.DMA((8,)),
        ],
        compiler_params=pltpu.CompilerParams(
            collective_id=0, has_side_effects=True, vmem_limit_bytes=LIMIT
        ),
        name="spread",
    )(queries, keys, values, out_weight, grad_out)


def list_uses(ids, groups, names):
    z = lax.rem(lax.axis_index("dp"), Z)

    def add(i, n):
        owner = ids[2 * i]
        dp, group = lax.shift_right_logical(i, 3), lax.shift_right_logical(i, 1) & 3
        groups[n] = (dp & 7) * 16 + lax.shift_right_logical(dp, 3) * 4 + group
        names[n] = lax.shift_right_logical(owner, 3) * NB_DEV + ids[2 * i + 1]
        return n + ((owner & 7) == z).astype(jnp.int32)

    n = lax.fori_loop(0, X * Z * 8, add, jnp.int32(0), unroll=8)
    last = jnp.maximum(n - 1, 0)
    groups[n] = groups[last]
    names[n] = names[last]
    return n


def pair_rows(ref, a, b, size):
    return [ref[pl.ds(pl.multiple_of(i * size, size), size), :] for i in (a, b)]


def pair_scores(first, second, both, left):
    product = lax.dot_general(
        jnp.concatenate([first, second], axis=0),
        both,
        (((1,), (1,)), ((), ())),
        preferred_element_type=F32,
    )
    return jnp.where(left, product[:NLEN], product[NLEN:])


def merge(one, two):
    peak = jnp.maximum(one[0], two[0])
    f, g = jnp.exp(one[0] - peak), jnp.exp(two[0] - peak)
    return peak, f * one[1] + g * two[1], f * one[2] + g * two[2]


def stats_kernel(ids, qall, upall, ktab, vtab, stats, groups, names):
    n = list_uses(ids, groups, names)
    stats[0] = jnp.full(stats.shape[1:], LOW, F32)
    stats[1] = jnp.zeros(stats.shape[1:], F32)
    stats[2] = jnp.zeros(stats.shape[1:], F32)
    left = lax.broadcasted_iota(jnp.int32, (1, 2 * GROUP), 1) < GROUP

    def pair(p, carry):
        a, b = 2 * p, 2 * p + 1
        ga, gb, na, nb = groups[a], groups[b], names[a], names[b]
        qq = jnp.concatenate(pair_rows(qall, ga, gb, GROUP), axis=0)
        uu = jnp.concatenate(pair_rows(upall, ga, gb, GROUP), axis=0)
        scores = pair_scores(*pair_rows(ktab, na, nb, NLEN), qq, left) * SCALE
        grad_probs = pair_scores(*pair_rows(vtab, na, nb, NLEN), uu, left)
        peak = jnp.max(scores, axis=0, keepdims=True)
        exponent = jnp.exp(scores - peak)
        total = jnp.sum(exponent, axis=0, keepdims=True)
        inner = jnp.sum(exponent * grad_probs, axis=0, keepdims=True)
        real = left | (b < n)
        new = (
            jnp.where(real, peak, LOW),
            jnp.where(real, total, 0.0),
            jnp.where(real, inner, 0.0),
        )
        for g, mine in ((ga, left), (gb, jnp.logical_not(left))):
            old = tuple(stats[i, pl.ds(g, 1), :] for i in range(3))
            merged = merge(old, new)
            for i in range(3):
                stats[i, pl.ds(g, 1), :] = jnp.where(mine, merged[i], old[i])
        return carry

    lax.fori_loop(0, (n + 1) // 2, pair, 0)


def stats_of_uses(ids, qall, upall, ktab, vtab):
    return pl.pallas_call(
        stats_kernel,
        out_shape=jax.ShapeDtypeStruct((3, 16 * Z, 2 * GROUP), F32),
        in_specs=[SMEM] + [VMEM] * 4,
        out_specs=VMEM,
        scratch_shapes=[pltpu.SMEM((264,), jnp.int32), pltpu.SMEM((264,), jnp.int32)],
        compiler_params=pltpu.CompilerParams(vmem_limit_bytes=LIMIT),
        name="stats",
    )(ids, qall, upall, ktab, vtab)


def totals_kernel(stats, out, held, send, recv):
    x, z, y, c = place()
    zs = [step_from(z, i, Z) for i in range(Z)]
    order = (1, 7, 2, 6, 3, 5, 4)
    enter([device(x, zs[i], y, c) for i in order])
    copies = Copies(send, recv)
    sent = [
        copies.start(
            stats.at[:, columns(zs[i], 16), :], held.at[i - 1], device(x, zs[i], y, c)
        )
        for i in order
    ]
    own = pl.ds(pl.multiple_of(z * 16, 16), 16)
    state = tuple(stats[i, own, :] for i in range(3))
    for copy, i in zip(sent, order):
        copy.wait_recv()
        state = merge(state, tuple(held[i - 1, j] for j in range(3)))
    state = merge(state, tuple(pltpu.roll(v, GROUP, 1) for v in state))
    out[0, own, :] = state[0] + jnp.log(state[1])
    out[1, own, :] = state[2] / state[1]
    back = out.at[:, own, :]
    sent = [copies.start(back, back, device(x, zs[i], y, c)) for i in order]
    for copy in sent:
        copy.wait_recv()
    copies.finish()


def totals(stats):
    return pl.pallas_call(
        totals_kernel,
        out_shape=jax.ShapeDtypeStruct((2,) + stats.shape[1:], F32),
        in_specs=[VMEM],
        out_specs=VMEM,
        scratch_shapes=[
            pltpu.VMEM((Z - 1, 3, 16, 2 * GROUP), F32),
            pltpu.SemaphoreType.DMA((16,)),
            pltpu.SemaphoreType.DMA((16,)),
        ],
        compiler_params=pltpu.CompilerParams(
            collective_id=1, has_side_effects=True, vmem_limit_bytes=LIMIT
        ),
        name="totals",
    )(stats)


def grads_kernel(
    ids, qall, upall, ktab, vtab, sums, ctx, gq, dkey, dvalue, groups, names, dk, dv
):
    n = list_uses(ids, groups, names)
    for ref in (ctx, gq, dk, dv):
        rows = 512

        @pl.loop(0, ref.shape[0] // rows)
        def _(i, ref=ref):
            ref[pl.ds(pl.multiple_of(i * rows, rows), rows), :] = jnp.zeros((rows, HD), ref.dtype)

    left = lax.broadcasted_iota(jnp.int32, (1, 2 * GROUP), 1) < GROUP
    zero = jnp.zeros((), BF)

    def add(ref, i, size, value):
        at = pl.ds(pl.multiple_of(i * size, size), size)
        ref[at, :] = (ref[at, :].astype(F32) + value).astype(ref.dtype)

    def dot(a, b):
        return jnp.dot(a, b, preferred_element_type=F32)

    def pair(p, carry):
        a, b = 2 * p, 2 * p + 1
        ga, gb, na, nb = groups[a], groups[b], names[a], names[b]
        qq = jnp.concatenate(pair_rows(qall, ga, gb, GROUP), axis=0)
        uu = jnp.concatenate(pair_rows(upall, ga, gb, GROUP), axis=0)
        keys = pair_rows(ktab, na, nb, NLEN)
        values = pair_rows(vtab, na, nb, NLEN)
        scores = pair_scores(*keys, qq, left) * SCALE
        grad_probs = pair_scores(*values, uu, left)
        log_total = jnp.where(left, sums[0, pl.ds(ga, 1), :], sums[0, pl.ds(gb, 1), :])
        inner = jnp.where(left, sums[1, pl.ds(ga, 1), :], sums[1, pl.ds(gb, 1), :])
        real = left | (b < n)
        prob = jnp.where(real, jnp.exp(scores - log_total), 0.0)
        grad_scores = prob * (grad_probs - inner)
        prob_t = prob.T.astype(BF)
        grad_t = grad_scores.T.astype(BF)
        prob, grad_scores = prob.astype(BF), grad_scores.astype(BF)

        def halves(v):
            return jnp.concatenate([jnp.where(left, v, zero), jnp.where(left, zero, v)], axis=0)

        context = dot(prob_t, jnp.concatenate(values, axis=1))
        grad_q = dot(grad_t, jnp.concatenate(keys, axis=1)) * SCALE
        grad_v = dot(halves(prob), uu)
        grad_k = dot(halves(grad_scores), qq) * SCALE
        add(ctx, ga, GROUP, context[:GROUP, :HD])
        add(ctx, gb, GROUP, context[GROUP:, HD:])
        add(gq, ga, GROUP, grad_q[:GROUP, :HD])
        add(gq, gb, GROUP, grad_q[GROUP:, HD:])
        add(dv, na, NLEN, grad_v[:NLEN])
        add(dv, nb, NLEN, grad_v[NLEN:])
        add(dk, na, NLEN, grad_k[:NLEN])
        add(dk, nb, NLEN, grad_k[NLEN:])
        return carry

    lax.fori_loop(0, (n + 1) // 2, pair, 0)
    for src, dst in ((dk, dkey), (dv, dvalue)):
        rows = 512

        @pl.loop(0, src.shape[0] // rows)
        def _(i, src=src, dst=dst):
            at = pl.ds(pl.multiple_of(i * rows, rows), rows)
            dst[at, :] = src[at, :].astype(BF)


def grads_of_uses(ids, qall, upall, ktab, vtab, sums):
    tokens, rows = qall.shape[0], ktab.shape[0]
    return pl.pallas_call(
        grads_kernel,
        out_shape=(
            jax.ShapeDtypeStruct((tokens, HD), BF),
            jax.ShapeDtypeStruct((tokens, HD), BF),
            jax.ShapeDtypeStruct((rows, HD), BF),
            jax.ShapeDtypeStruct((rows, HD), BF),
        ),
        in_specs=[SMEM] + [VMEM] * 5,
        out_specs=[VMEM] * 4,
        scratch_shapes=[
            pltpu.SMEM((264,), jnp.int32),
            pltpu.SMEM((264,), jnp.int32),
            pltpu.VMEM((rows, HD), F32),
            pltpu.VMEM((rows, HD), F32),
        ],
        compiler_params=pltpu.CompilerParams(vmem_limit_bytes=LIMIT),
        name="grads",
    )(ids, qall, upall, ktab, vtab, sums)


def collect_kernel(
    ctx, gq, dkey, dvalue, wf,
    out, gq_out, dk_out, dv_out,
    held, ctx4, part, core_in, y_in, done, gq_done, send, recv, out_send, out_recv, local,
):
    where = x, z, y, c = place()
    t = y * C + c
    span = wf.shape[1]
    xs = [step_from(x, i, X) for i in range(X)]
    ys = [step_from(y, i, Y) for i in range(Y)]
    other = 1 - c
    enter(
        [device(xs[i], z, y, c) for i in (1, 2, 3)]
        + [device(x, step_from(z, i, Z), y, c) for i in (1, -1)]
        + [device(x, z, ys[i], c) for i in (1, 2, 3)]
        + [device(x, z, y, other)]
    )
    copies = Copies(send, recv)
    kept = []

    def keep(src, dst):
        copy = pltpu.make_async_copy(src, dst, local.at[len(kept)])
        copy.start()
        kept.append(copy)

    def piece(ref, i, n):
        return Scatter(
            copies,
            lambda b: ref.at[b, i],
            lambda way, s: held.at[n, 4 * way + s],
            HOPS[n % 2],
            where,
        )

    pieces = [piece(ctx, i, i) for i in range(X)]
    pieces += [piece(gq, xs[i], X + i) for i in range(X)]
    table_in, ctx_in, core_sent, y_sent, gq_sent = [], {}, {}, {}, []

    def tables():
        for src, dst in ((dkey, dk_out), (dvalue, dv_out)):
            keep(src.at[x], dst.at[:, columns(x, HD)])
            for i in (1, 3, 2):
                table_in.append(
                    copies.start(src.at[xs[i]], dst.at[:, columns(x, HD)], device(xs[i], z, y, c))
                )

    def share(i):
        mine = ctx4.at[i, :, columns(x, HD)]
        mine[...] = pieces[i].total().astype(BF)
        ctx_in[i] = [copies.start(mine, mine, device(xs[j], z, y, c)) for j in (1, 3, 2)]

    def multiply(i):
        for copy in ctx_in[i]:
            copy.wait_recv()
        for j in range(2):
            cols = pl.ds(j * (span // 2), span // 2)
            product = jnp.dot(ctx4[i], wf[:, cols], preferred_element_type=F32).astype(BF)
            part[i, :, :, :, cols] = product.reshape(Y, C, TOK // (Y * C), span // 2)
        core_sent[i] = copies.start(part.at[i, :, other], core_in.at[i], device(x, z, y, other))

    def join(i):
        core_sent[i].wait_recv()
        core_in[i] = (core_in[i].astype(F32) + part[i, :, c].astype(F32)).astype(BF)
        y_sent[i] = [
            copies.start(core_in.at[i, ys[j]], y_in.at[i, j - 1], device(x, z, ys[j], c))
            for j in (1, 3, 2)
        ]

    def total(i):
        for copy in y_sent[i]:
            copy.wait_recv()
        value = core_in[i, y].astype(F32)
        for j in range(3):
            value += y_in[i, j].astype(F32)
        done[i] = value.astype(BF)
        goal = out.at[:, columns(x, span)]

        @pl.when(x == i)
        def _():
            copy = pltpu.make_async_copy(done.at[i], goal, local.at[7])
            copy.start()
            copy.wait()

        @pl.when(x != i)
        def _():
            sem = step_from(i - x, 0, X)
            pltpu.make_async_remote_copy(
                src_ref=done.at[i],
                dst_ref=goal,
                send_sem=out_send.at[sem],
                recv_sem=out_recv.at[sem],
                device_id=device(i, z, y, c),
                device_id_type=pl.DeviceIdType.MESH,
            ).start()

    def queries(i):
        gq_done[i] = pieces[X + i].total().astype(BF)
        goal = gq_out.at[:, columns(x, HD)]
        if i == 0:
            keep(gq_done.at[i], goal)
        else:
            gq_sent.append(copies.start(gq_done.at[i], goal, device(xs[i], z, y, c)))

    def last_hop(n):
        return n + 4

    for wave in range(12):
        for n, one in enumerate(pieces):
            if 0 <= wave - n <= 4:
                one.step(wave - n)
        if wave == 0:
            tables()
        for stage, ref in enumerate((share, multiply, join, total)):
            i = wave - 4 - stage
            if 0 <= i < X:
                ref(i)
        if 8 <= wave:
            queries(wave - 8)
    for copy in table_in + gq_sent:
        copy.wait_recv()
    for i in (1, 2, 3):
        copy = pltpu.make_async_remote_copy(
            src_ref=done.at[0],
            dst_ref=out.at[:, columns(xs[i], span)],
            send_sem=out_send.at[i],
            recv_sem=out_recv.at[i],
            device_id=device(xs[i], z, y, c),
            device_id_type=pl.DeviceIdType.MESH,
        )
        copy.wait_recv()
        copy.wait_send()
    for copy in kept:
        copy.wait()
    copies.finish()


def collect(ctx, gq, dkey, dvalue, wf):
    head_cols, span = wf.shape
    rows = dkey.shape[1]
    slots = TOK // (Y * C)
    return pl.pallas_call(
        collect_kernel,
        out_shape=(
            jax.ShapeDtypeStruct((slots, X * span), BF),
            jax.ShapeDtypeStruct((TOK, head_cols), BF),
            jax.ShapeDtypeStruct((rows, head_cols), BF),
            jax.ShapeDtypeStruct((rows, head_cols), BF),
        ),
        in_specs=[VMEM] * 5,
        out_specs=[VMEM] * 4,
        scratch_shapes=[
            pltpu.VMEM((2 * X, 8, TOK, HD), BF),
            pltpu.VMEM((X, TOK, head_cols), BF),
            pltpu.VMEM((X, Y, C, slots, span), BF),
            pltpu.VMEM((X, Y, slots, span), BF),
            pltpu.VMEM((X, Y - 1, slots, span), BF),
            pltpu.VMEM((X, slots, span), BF),
            pltpu.VMEM((X, TOK, HD), BF),
            pltpu.SemaphoreType.DMA((120,)),
            pltpu.SemaphoreType.DMA((120,)),
            pltpu.SemaphoreType.DMA((4,)),
            pltpu.SemaphoreType.DMA((4,)),
            pltpu.SemaphoreType.DMA((8,)),
        ],
        compiler_params=pltpu.CompilerParams(
            collective_id=2, has_side_effects=True, vmem_limit_bytes=LIMIT
        ),
        name="collect",
    )(ctx, gq, dkey, dvalue, wf)


def shards(queries, keys, values, out_weight, grad_out, neighbour_owner, neighbour_local):
    ids = jnp.stack([neighbour_owner, neighbour_local], axis=-1).reshape(1, -1)
    ids = lax.all_gather(ids, "dp", axis=0, tiled=True).reshape(-1)
    qall, ktab, vtab, wf, upall = spread(queries, keys, values, out_weight, grad_out)
    qall, upall = (a.reshape(Z * X * TOK, HD) for a in (qall, upall))
    ktab, vtab = (a.reshape(X * keys.shape[0], HD) for a in (ktab, vtab))
    sums = totals(stats_of_uses(ids, qall, upall, ktab, vtab))
    ctx, gq, dkey, dvalue = grads_of_uses(ids, qall, upall, ktab, vtab, sums)
    ctx, gq = (a.reshape(Z, X, TOK, HD) for a in (ctx, gq))
    dkey, dvalue = (a.reshape((X,) + keys.shape[:1] + (HD,)) for a in (dkey, dvalue))
    out, grad_queries, grad_keys, grad_values = collect(ctx, gq, dkey, dvalue, wf)
    return out, grad_queries, grad_keys.astype(F32), grad_values.astype(F32)


def solution(mesh):
    return jax.shard_map(
        shards,
        mesh=mesh,
        in_specs=(
            P("dp", "tensor"),
            P("dp", "tensor"),
            P("dp", "tensor"),
            P("tensor", "dp"),
            P(("dp", "tensor"), None),
            P("dp", None),
            P("dp", None),
        ),
        out_specs=(
            P(("dp", "tensor"), None),
            P("dp", "tensor"),
            P("dp", "tensor"),
            P("dp", "tensor"),
        ),
        check_vma=False,
    )
```

time: 544 us -> 270 us (0.50)
  waiting for transfers between devices: 370 us -> 0 us
  Pallas kernels: 0 us -> 218 us
  local copies, waits for them, and re-layouts: 40.2 us -> 2.87 us
  other arithmetic: 41.7 us -> 5.92 us
  starting transfers between devices: 29.8 us -> 0 us
  matrix products: 24.8 us -> 0 us
  blocking collectives: 19.3 us -> 40 us
  between operations: 14.1 us -> 0.68 us
    all_to_all x4 -> x0, waiting for transfers between devices: 369 us -> none  [the longest x1 120 us: shards(): lax.all_to_all(value_table[owner_ids], 'dp', split_axis=0, concat_axis=0,...]
    pallas_call x0 -> x5, Pallas kernels: none -> 218 us  [the longest x1 96.3 us: spread(): pl.pallas_call(spread_kernel, out_shape=(jax.ShapeDtypeStruct((Z, X, TOK,...]
    all_gather x0 -> x1, blocking collectives: none -> 40 us  [shards(): ids = lax.all_gather(ids, 'dp', axis=0, tiled=True).reshape(-1)]
    all_to_all x4 -> x0, starting transfers between devices: 29.7 us -> none  [the longest x1 8.68 us: shards(): lax.all_to_all(place_slots(grad_value.reshape(use_count, NLEN, head_cols)...]
    dot_general x8 -> x0, matrix products: 24.8 us -> none  [the longest x1 7.74 us: shards(): lax.dot_general(lax.all_gather(grad_out, 'tensor', axis=0, tiled=True), f...]
    scatter-add x2 -> x0, other arithmetic: 23.6 us -> none  [shards(): jnp.zeros((NB_DEV, NLEN, head_cols), jnp.float32).at[flat_ids]]
    all_to_all x1 -> x0, blocking collectives: 19.3 us -> none  [shards(): lax.all_to_all(request, 'dp', split_axis=0, concat_axis=0, tiled=True)]
    gather x6 -> x0, local copies, waits for them, and re-layouts: 12.5 us -> none  [the longest x4 6.99 us: pick_slots(): return buffer.reshape((slot_total,) + buffer.shape[2:])[slot_index]]
  transfers between devices with their start and end apart: 7 -> 0, of which waited for: 4 -> 0; matrix products, arithmetic and copies ran while one was open for 15% -> 0% of each run, Pallas kernels for 0% -> 0%
where the time goes in v1:
time: 270 us; the launch traced here: 268 us
  Pallas kernels  218 us (81%)
  blocking collectives  40 us (15%)
  other arithmetic  5.92 us (2%)
  local copies, waits for them, and re-layouts  2.87 us (1%)
    pallas_call x1, Pallas kernels, spread(): pl.pallas_call(spread_kernel, out_shape=(jax.ShapeDtypeStruct((Z, X, TOK,...  96.3 us
    pallas_call x1, Pallas kernels, collect(): pl.pallas_call(collect_kernel, out_shape=(jax.ShapeDtypeStruct((slots, X...  80.2 us
    all_gather x1, blocking collectives, shards(): ids = lax.all_gather(ids, 'dp', axis=0, tiled=True).reshape(-1)  40 us
    pallas_call x1, Pallas kernels, totals(): pl.pallas_call(totals_kernel, out_shape=jax.ShapeDtypeStruct((2,) + stats...  18.9 us
    pallas_call x1, Pallas kernels, grads_of_uses(): pl.pallas_call(grads_kernel, out_shape=(jax.ShapeDtypeStruct((tokens, HD)...  14.2 us
    pallas_call x1, Pallas kernels, stats_of_uses(): pl.pallas_call(stats_kernel, out_shape=jax.ShapeDtypeStruct((3, 16 * Z, 2...  8.43 us

profile of v1, /device:TPU:6, one launch (start us, length us, event | category | flops | bytes accessed | tf_op | source)
XLA Modules:
  0.0 267.5 jit_solution(7088087386477628737)
XLA Ops:
  0.6 0.7 pad_add_fusion
  1.3 0.1 copy.13
  1.4 0.1 reshape.48
  1.5 40.0 %all-gather = s32[32,1,16]{2,1,0:T(1,128)S(1)} all-gather(s32[1,1,16]{2,1,0:T(1,128)S(1)} %reshape.48), channel_id=1, replica_groups=mesh['dp'=32,'tensor'=8] {'dp'}, dimensions={0}, use_global_device_ids=true | all-gather | bytes 2112 | tf_op jit(solution)/shard_map/all_gather | solution.py:670
  41.5 0.5 broadcast.3
  42.0 0.7 reduce.3
  42.7 0.7 reshape.39.ids
  43.4 96.3 %spread.1 = (bf16[8,4,256,128]{3,2,1,0:T(8,128)(2,1)}, bf16[4,1024,128]{2,1,0:T(8,128)(2,1)}, bf16[4,1024,128]{2,1,0:T(8,128)(2,1)}, bf16[512,2048]{1,0:T(8,128)(2,1)}, bf16[8,4,256,128]{3,2,1,0:T(8,128)(2,1)}) custom-call(bf16[256,512]{1,0:T(8,128)(2,1)} %q_ref.1, bf16[1024,512]{1,0:T(8,128)(2,1)} %k_ref.1, bf16[1024,512]{1,0:T(8,128)(2,1)} %v_ref.1, ...), custom_call_target="tpu_custom_call" | custom-call | tf_op jit(solution)/shard_map/spread/pallas_call | solution.py:254
  139.6 8.4 %stats.1 = f32[3,128,128]{2,1,0:T(8,128)} custom-call(s32[512]{0:T(512)} %reshape.39.ids, bf16[8192,128]{1,0:T(8,128)(2,1)} %bitcast.10, bf16[8192,128]{1,0:T(8,128)(2,1)} %bitcast.12, bf16[4096,128]{1,0:T(8,128)(2,1)} %bitcast.14, bf16[4096,128]{1,0:T(8,128)(2,1)} %bitcast.16), custom_call_target="tpu_custom_call" | custom-call | tf_op jit(solution)/shard_map/stats/pallas_call | solution.py:352
  148.1 18.9 %totals.1.sums = f32[2,128,128]{2,1,0:T(8,128)} custom-call(f32[3,128,128]{2,1,0:T(8,128)} %stats.1), custom_call_target="tpu_custom_call" | custom-call | tf_op jit(solution)/shard_map/totals/pallas_call | solution.py:391
  167.0 14.2 %grads.1 = (bf16[8192,128]{1,0:T(8,128)(2,1)}, bf16[8192,128]{1,0:T(8,128)(2,1)}, bf16[4096,128]{1,0:T(8,128)(2,1)}, bf16[4096,128]{1,0:T(8,128)(2,1)}) custom-call(s32[512]{0:T(512)} %reshape.39.ids, bf16[8192,128]{1,0:T(8,128)(2,1)} %bitcast.11, bf16[8192,128]{1,0:T(8,128)(2,1)} %bitcast.13, bf16[4096,128]{1,0:T(8,128)(2,1)} %bitcast.15, ...), custom_call_target="tpu_custom_call" | custom-call | tf_op jit(solution)/shard_map/grads/pallas_call | solution.py:476
  181.2 80.2 %collect.1 = (bf16[32,8192]{1,0:T(8,128)(2,1)}, bf16[256,512]{1,0:T(8,128)(2,1)}, bf16[1024,512]{1,0:T(8,128)(2,1)}, bf16[1024,512]{1,0:T(8,128)(2,1)}) custom-call(bf16[8,4,256,128]{3,2,1,0:T(8,128)(2,1)} %bitcast.18, bf16[8,4,256,128]{3,2,1,0:T(8,128)(2,1)} %bitcast.19, bf16[4,1024,128]{2,1,0:T(8,128)(2,1)} %bitcast.20, bf16[4,1024,128]{2,1,0:T(8,128)(2,1)} %bitcast.21, ...), custom_call_target="tpu_custom_call" | custom-call | tf_op jit(solution)/shard_map/collect/pallas_call | solution.py:637
  261.5 0.0 copy-start
  261.5 2.9 %convert_element_type.6 = f32[1024,512]{1,0:T(8,128)} convert(bf16[1024,512]{1,0:T(8,128)(2,1)} %get-tuple-element.28) | non-fusion elementwise | flops 524288 | bytes 3145728 | tf_op jit(solution)/shard_map/convert_element_type | solution.py:679
  264.4 0.0 copy-done
  264.4 0.0 copy-start.1
  264.4 0.0 copy-start.2
  264.4 1.6 convert_element_type.7
  266.0 0.0 copy-done.1
  266.0 0.8 copy.16
  266.8 0.0 copy-done.2
  266.8 0.7 copy.17
Async XLA Ops:
  261.5 2.9 %copy-start = (bf16[1024,512]{1,0:T(8,128)(2,1)S(1)}, bf16[1024,512]{1,0:T(8,128)(2,1)}, u32[]{:S(2)}) copy-start(bf16[1024,512]{1,0:T(8,128)(2,1)} %get-tuple-element.29) | copy-start | bytes 3145732
  264.4 1.6 copy-start.1
  264.4 2.4 copy-start.2

commit v2 on v1

--- a/solution.py
+++ b/solution.py
@@ -124,8 +124,8 @@
 
 
 def spread_kernel(
-    q_ref, k_ref, v_ref, w_ref, g_ref,
-    qall, ktab, vtab, wf, upall,
+    ids_ref, q_ref, k_ref, v_ref, w_ref, g_ref,
+    idall, qall, ktab, vtab, wf, upall,
     gfull, upp, upr, send, recv, local,
 ):
     where = x, z, y, c = place()
@@ -155,6 +155,7 @@
     keep(k_ref.at[:, columns(x, HD)], ktab.at[x])
     keep(v_ref.at[:, columns(x, HD)], vtab.at[x])
     keep(w_ref, wf.at[:, columns(z, width)])
+    keep(ids_ref, idall.at[z, x])
 
     g_in = [
         copies.start(g_ref.at[:, columns(xs[i], span)], gfull.at[x, t], device(xs[i], z, y, c))
@@ -170,77 +171,112 @@
     def piece(ref, i):
         return Gather(copies, ref.at[z, i], lambda b: ref.at[b, i], HOPS[i % 2], where)
 
-    pieces = [weight_piece(i) for i in range(4)]
-    pieces += [piece(qall, i) for i in range(X)]
-    pieces += [piece(upall, i) for i in range(X)]
-
+    weights = [weight_piece(i) for i in range(4)]
+    asked = [piece(qall, i) for i in range(X)]
+    asked.append(
+        Gather(copies, idall.at[z], lambda b: idall.at[b], HOPS[0], where),
+    )
+    upstream = [piece(upall, i) for i in range(X)]
     table_in, q_in, g_y, g_core, up_in = [], [], {}, {}, {}
 
-    def before(wave):
-        if wave == 4:
-            for copy in q_in:
-                copy.wait_recv()
-            kept[1].wait()
-        if 8 <= wave < 8 + X:
-            i = wave - 8
-            for copy in up_in[i]:
-                copy.wait_recv()
-            total = upp[i, :, columns(x, HD)].astype(F32)
-            for j in range(3):
-                total += upr[i, j].astype(F32)
-            upall[z, i] = total.astype(BF)
-
-    def after(wave):
-        if wave == 0:
-            for i in (1, 3, 2):
-                q_in.append(
-                    copies.start(
-                        q_ref.at[:, columns(xs[i], HD)], qall.at[z, x], device(xs[i], z, y, c)
-                    )
-                )
-            kept[0].wait()
-            for copy in g_in:
-                copy.wait_recv()
-            for i in range(X):
-                block = gfull.at[i, t]
-                g_y[i] = [copies.start(block, block, device(x, z, ys[j], c)) for j in (1, 3, 2)]
-                g_core[i] = [copies.start(block, block, device(x, z, y, other))]
-            for i in (1, 3, 2):
-                for src, dst in ((k_ref, ktab), (v_ref, vtab)):
-                    table_in.append(
-                        copies.start(
-                            src.at[:, columns(xs[i], HD)], dst.at[x], device(xs[i], z, y, c)
-                        )
-                    )
-        if 3 <= wave < 3 + X:
-            i = wave - 3
-            for copy, j in zip(g_y[i], (-1, -3, -2)):
-                copy.wait_recv()
-                block = gfull.at[i, step_from(y, j, Y) * C + c]
-                g_core[i].append(copies.start(block, block, device(x, z, y, other)))
-        if 7 <= wave < 7 + X:
-            i = wave - 7
-            if wave == 7:
-                kept[4].wait()
-            for copy in g_core[i]:
-                copy.wait_recv()
-            rows = gfull[i].reshape(TOK, span)
-            upp[i] = lax.dot_general(
-                rows, wf[...], (((1,), (1,)), ((), ())), preferred_element_type=F32
-            ).astype(BF)
-            up_in[i] = [
-                copies.start(
-                    upp.at[i, :, columns(xs[j], HD)], upr.at[i, j - 1], device(xs[j], z, y, c)
-                )
-                for j in (1, 3, 2)
-            ]
-
-    for wave in range(len(pieces) + 4):
-        before(wave)
-        for i, one in enumerate(pieces):
-            if 0 <= wave - i <= 4:
-                one.step(wave - i)
-        after(wave)
+    def step(pieces, s):
+        for one in pieces:
+            one.step(s)
+
+    def send_queries():
+        for i in (1, 3, 2):
+            to = device(xs[i], z, y, c)
+            q_in.append(copies.start(q_ref.at[:, columns(xs[i], HD)], qall.at[z, x], to))
+            q_in.append(copies.start(ids_ref, idall.at[z, x], to))
+
+    def send_table(src, dst):
+        for i in (1, 3, 2):
+            to = device(xs[i], z, y, c)
+            table_in.append(copies.start(src.at[:, columns(xs[i], HD)], dst.at[x], to))
+
+    def send_rows():
+        kept[0].wait()
+        for copy in g_in:
+            copy.wait_recv()
+        for i in range(X):
+            block = gfull.at[i, t]
+            g_y[i] = [copies.start(block, block, device(x, z, ys[j], c)) for j in (1, 3, 2)]
+            g_core[i] = [copies.start(block, block, device(x, z, y, other))]
+
+    def hand_over(i):
+        for copy, j in zip(g_y[i], (-1, -3, -2)):
+            copy.wait_recv()
+            block = gfull.at[i, step_from(y, j, Y) * C + c]
+            g_core[i].append(copies.start(block, block, device(x, z, y, other)))
+
+    def multiply(i):
+        for copy in g_core[i]:
+            copy.wait_recv()
+        rows = gfull[i].reshape(TOK, span)
+        upp[i] = lax.dot_general(
+            rows, wf[...], (((1,), (1,)), ((), ())), preferred_element_type=F32
+        ).astype(BF)
+        up_in[i] = [
+            copies.start(
+                upp.at[i, :, columns(xs[j], HD)], upr.at[i, j - 1], device(xs[j], z, y, c)
+            )
+            for j in (1, 3, 2)
+        ]
+
+    def total(i):
+        for copy in up_in[i]:
+            copy.wait_recv()
+        value = upp[i, :, columns(x, HD)].astype(F32)
+        for j in range(3):
+            value += upr[i, j].astype(F32)
+        upall[z, i] = value.astype(BF)
+        upstream[i].step(0)
+
+    step(weights, 0)
+    send_queries()
+    step(weights, 1)
+    send_rows()
+    step(weights, 2)
+    for copy in q_in:
+        copy.wait_recv()
+    kept[1].wait()
+    kept[5].wait()
+    send_table(k_ref, ktab)
+    step(weights, 3)
+    step(asked, 0)
+    hand_over(0)
+    step(weights, 4)
+    kept[4].wait()
+    multiply(0)
+    hand_over(1)
+    step(asked, 1)
+    multiply(1)
+    hand_over(2)
+    step(asked, 2)
+    multiply(2)
+    hand_over(3)
+    total(0)
+    total(1)
+    step(asked, 3)
+    multiply(3)
+    step(upstream[:1], 1)
+    total(2)
+    send_table(v_ref, vtab)
+    step(upstream[1:2], 1)
+    step(asked, 4)
+    step(upstream[:1], 2)
+    total(3)
+    step(upstream[1:2], 2)
+    step(upstream[2:3], 1)
+    step(upstream[:1], 3)
+    step(upstream[3:], 1)
+    step(upstream[1:2], 3)
+    step(upstream[2:3], 2)
+    step(upstream[:1], 4)
+    step(upstream[3:], 2)
+    step(upstream[1:2], 4)
+    step(upstream[2:], 3)
+    step(upstream[2:], 4)
     for copy in table_in:
         copy.wait_recv()
     for copy in kept[2:4]:
@@ -248,43 +284,44 @@
     copies.finish()
 
 
-def spread(queries, keys, values, out_weight, grad_out):
+def spread(ids, queries, keys, values, out_weight, grad_out):
     depth, width = out_weight.shape
     rows, head_cols = keys.shape
     return pl.pallas_call(
         spread_kernel,
         out_shape=(
+            jax.ShapeDtypeStruct((Z, X) + ids.shape, jnp.int32),
             jax.ShapeDtypeStruct((Z, X, TOK, HD), BF),
             jax.ShapeDtypeStruct((X, rows, HD), BF),
             jax.ShapeDtypeStruct((X, rows, HD), BF),
             jax.ShapeDtypeStruct((depth, Z * width), BF),
             jax.ShapeDtypeStruct((Z, X, TOK, HD), BF),
         ),
-        in_specs=[VMEM] * 5,
-        out_specs=[VMEM] * 5,
+        in_specs=[VMEM] * 6,
+        out_specs=[VMEM] * 6,
         scratch_shapes=[
             pltpu.VMEM((X, Y * C, grad_out.shape[0], Z * width), BF),
             pltpu.VMEM((X, TOK, head_cols), BF),
             pltpu.VMEM((X, X - 1, TOK, HD), BF),
-            pltpu.SemaphoreType.DMA((140,)),
-            pltpu.SemaphoreType.DMA((140,)),
+            pltpu.SemaphoreType.DMA((152,)),
+            pltpu.SemaphoreType.DMA((152,)),
             pltpu.SemaphoreType.DMA((8,)),
         ],
         compiler_params=pltpu.CompilerParams(
             collective_id=0, has_side_effects=True, vmem_limit_bytes=LIMIT
         ),
         name="spread",
-    )(queries, keys, values, out_weight, grad_out)
+    )(ids, queries, keys, values, out_weight, grad_out)
 
 
 def list_uses(ids, groups, names):
     z = lax.rem(lax.axis_index("dp"), Z)
 
     def add(i, n):
-        owner = ids[2 * i]
-        dp, group = lax.shift_right_logical(i, 3), lax.shift_right_logical(i, 1) & 3
-        groups[n] = (dp & 7) * 16 + lax.shift_right_logical(dp, 3) * 4 + group
-        names[n] = lax.shift_right_logical(owner, 3) * NB_DEV + ids[2 * i + 1]
+        dp_z, dp_x = lax.shift_right_logical(i, 5), lax.shift_right_logical(i, 3) & 3
+        owner, name = (ids[dp_z, dp_x, 0, 2 * (i & 7) + j] for j in (0, 1))
+        groups[n] = lax.shift_right_logical(i, 1)
+        names[n] = lax.shift_right_logical(owner, 3) * NB_DEV + name
         return n + ((owner & 7) == z).astype(jnp.int32)
 
     n = lax.fori_loop(0, X * Z * 8, add, jnp.int32(0), unroll=8)
@@ -597,21 +634,36 @@
         else:
             gq_sent.append(copies.start(gq_done.at[i], goal, device(xs[i], z, y, c)))
 
-    def last_hop(n):
-        return n + 4
-
-    for wave in range(12):
-        for n, one in enumerate(pieces):
-            if 0 <= wave - n <= 4:
-                one.step(wave - n)
-        if wave == 0:
-            tables()
-        for stage, ref in enumerate((share, multiply, join, total)):
-            i = wave - 4 - stage
-            if 0 <= i < X:
-                ref(i)
-        if 8 <= wave:
-            queries(wave - 8)
+    def step(pieces, s):
+        for one in pieces:
+            one.step(s)
+
+    contexts, grads = pieces[:X], pieces[X:]
+    step(contexts, 0)
+    tables()
+    for s in (1, 2, 3):
+        step(contexts, s)
+    step(grads, 0)
+    for i in range(X):
+        contexts[i].step(4)
+        share(i)
+    step(grads, 1)
+    multiply(0)
+    multiply(1)
+    join(0)
+    multiply(2)
+    join(1)
+    step(grads, 2)
+    multiply(3)
+    join(2)
+    join(3)
+    step(grads, 3)
+    total(0)
+    for i in range(X):
+        grads[i].step(4)
+        queries(i)
+    for i in (1, 2, 3):
+        total(i)
     for copy in table_in + gq_sent:
         copy.wait_recv()
     for i in (1, 2, 3):
@@ -667,8 +719,8 @@
 
 def shards(queries, keys, values, out_weight, grad_out, neighbour_owner, neighbour_local):
     ids = jnp.stack([neighbour_owner, neighbour_local], axis=-1).reshape(1, -1)
-    ids = lax.all_gather(ids, "dp", axis=0, tiled=True).reshape(-1)
-    qall, ktab, vtab, wf, upall = spread(queries, keys, values, out_weight, grad_out)
+    ids = jnp.pad(ids, ((0, 0), (0, 128 - ids.shape[1])))
+    ids, qall, ktab, vtab, wf, upall = spread(ids, queries, keys, values, out_weight, grad_out)
     qall, upall = (a.reshape(Z * X * TOK, HD) for a in (qall, upall))
     ktab, vtab = (a.reshape(X * keys.shape[0], HD) for a in (ktab, vtab))
     sums = totals(stats_of_uses(ids, qall, upall, ktab, vtab))

time: 270 us -> 211 us (0.78)
  blocking collectives: 40 us -> 0 us
  Pallas kernels: 218 us -> 202 us
    all_gather x1 -> x0, blocking collectives: 40 us -> none  [shards(): ids = lax.all_gather(ids, 'dp', axis=0, tiled=True).reshape(-1)]
    pallas_call x1, Pallas kernels: 96.3 us -> 80.4 us  [spread(): pl.pallas_call(spread_kernel, out_shape=(jax.ShapeDtypeStruct((Z, X) + id...]
    pallas_call x1, Pallas kernels: 80.2 us -> 72.6 us  [collect(): pl.pallas_call(collect_kernel, out_shape=(jax.ShapeDtypeStruct((slots, X...]
    pallas_call x1, Pallas kernels: 14.2 us -> 21.3 us  [grads_of_uses(): pl.pallas_call(grads_kernel, out_shape=(jax.ShapeDtypeStruct((tokens, HD)...]
    pallas_call x1, Pallas kernels: 8.43 us -> 12.6 us  [stats_of_uses(): pl.pallas_call(stats_kernel, out_shape=jax.ShapeDtypeStruct((3, 16 * Z, 2...]
    pallas_call x1, Pallas kernels: 18.9 us -> 15.4 us  [totals(): pl.pallas_call(totals_kernel, out_shape=jax.ShapeDtypeStruct((2,) + stats...]
where the time goes in v2:
time: 211 us; the launch traced here: 210 us
  Pallas kernels  202 us (96%)
  other arithmetic  5.24 us (2%)
  local copies, waits for them, and re-layouts  2.22 us (1%)
    pallas_call x1, Pallas kernels, spread(): pl.pallas_call(spread_kernel, out_shape=(jax.ShapeDtypeStruct((Z, X) + id...  80.4 us
    pallas_call x1, Pallas kernels, collect(): pl.pallas_call(collect_kernel, out_shape=(jax.ShapeDtypeStruct((slots, X...  72.6 us
    pallas_call x1, Pallas kernels, grads_of_uses(): pl.pallas_call(grads_kernel, out_shape=(jax.ShapeDtypeStruct((tokens, HD)...  21.3 us
    pallas_call x1, Pallas kernels, totals(): pl.pallas_call(totals_kernel, out_shape=jax.ShapeDtypeStruct((2,) + stats...  15.4 us
    pallas_call x1, Pallas kernels, stats_of_uses(): pl.pallas_call(stats_kernel, out_shape=jax.ShapeDtypeStruct((3, 16 * Z, 2...  12.6 us
    convert_element_type x2, other arithmetic, shards(): return (out, grad_queries, grad_keys.astype(F32), grad_values.astype(F32))  4.54 us

profile of v2, /device:TPU:6, one launch (start us, length us, event | category | flops | bytes accessed | tf_op | source)
XLA Modules:
  0.0 210.4 jit_solution(10016229205740131228)
XLA Ops:
  0.6 0.7 pad_add_fusion
  1.3 0.1 copy.12
  1.4 0.1 reshape.35
  1.5 0.5 pad.4.ids_ref
  2.0 80.4 %spread.1 = (s32[8,4,1,128]{3,2,1,0:T(1,128)}, bf16[8,4,256,128]{3,2,1,0:T(8,128)(2,1)}, bf16[4,1024,128]{2,1,0:T(8,128)(2,1)}, bf16[4,1024,128]{2,1,0:T(8,128)(...) custom-call(s32[1,128]{1,0:T(1,128)} %pad.4.ids_ref, bf16[256,512]{1,0:T(8,128)(2,1)} %q_ref.1, ...), custom_call_target="tpu_custom_call" | custom-call | tf_op jit(solution)/shard_map/spread/pallas_call | solution.py:290
  82.4 12.6 %stats.1 = f32[3,128,128]{2,1,0:T(8,128)} custom-call(s32[8,4,1,128]{3,2,1,0:T(1,128)} %get-tuple-element.18.ids, bf16[8192,128]{1,0:T(8,128)(2,1)} %bitcast.10, bf16[8192,128]{1,0:T(8,128)(2,1)} %bitcast.12, bf16[4096,128]{1,0:T(8,128)(2,1)} %bitcast.14, bf16[4096,128]{1,0:T(8,128)(2,1)} %bitcast.16), custom_call_target="tpu_custom_call" | custom-call | tf_op jit(solution)/shard_map/stats/pallas_call | solution.py:389
  95.0 15.4 %totals.1.sums = f32[2,128,128]{2,1,0:T(8,128)} custom-call(f32[3,128,128]{2,1,0:T(8,128)} %stats.1), custom_call_target="tpu_custom_call" | custom-call | tf_op jit(solution)/shard_map/totals/pallas_call | solution.py:428
  110.4 21.3 %grads.1 = (bf16[8192,128]{1,0:T(8,128)(2,1)}, bf16[8192,128]{1,0:T(8,128)(2,1)}, bf16[4096,128]{1,0:T(8,128)(2,1)}, bf16[4096,128]{1,0:T(8,128)(2,1)}) custom-call(s32[8,4,1,128]{3,2,1,0:T(1,128)} %get-tuple-element.18.ids, bf16[8192,128]{1,0:T(8,128)(2,1)} %bitcast.11, bf16[8192,128]{1,0:T(8,128)(2,1)} %bitcast.13, bf16[4096,128]{1,0:T(8,128)(2,1)} %bitcast.15, ...), custom_call_target="tpu_custom_call" | custom-call | tf_op jit(solution)/shard_map/grads/pallas_call | solution.py:513
  131.7 72.6 %collect.1 = (bf16[32,8192]{1,0:T(8,128)(2,1)}, bf16[256,512]{1,0:T(8,128)(2,1)}, bf16[1024,512]{1,0:T(8,128)(2,1)}, bf16[1024,512]{1,0:T(8,128)(2,1)}) custom-call(bf16[8,4,256,128]{3,2,1,0:T(8,128)(2,1)} %bitcast.18, bf16[8,4,256,128]{3,2,1,0:T(8,128)(2,1)} %bitcast.19, bf16[4,1024,128]{2,1,0:T(8,128)(2,1)} %bitcast.20, bf16[4,1024,128]{2,1,0:T(8,128)(2,1)} %bitcast.21, ...), custom_call_target="tpu_custom_call" | custom-call | tf_op jit(solution)/shard_map/collect/pallas_call | solution.py:689
  204.3 0.0 copy-start
  204.4 2.9 %convert_element_type.6 = f32[1024,512]{1,0:T(8,128)} convert(bf16[1024,512]{1,0:T(8,128)(2,1)} %get-tuple-element.30) | non-fusion elementwise | flops 524288 | bytes 3145728 | tf_op jit(solution)/shard_map/convert_element_type | solution.py:731
  207.3 0.0 copy-done
  207.3 0.0 copy-start.1
  207.3 0.0 copy-start.2
  207.3 1.6 convert_element_type.7
  208.9 0.0 copy-done.1
  208.9 0.8 copy.15
  209.7 0.0 copy-done.2
  209.7 0.7 copy.16
Async XLA Ops:
  204.3 2.9 %copy-start = (bf16[1024,512]{1,0:T(8,128)(2,1)S(1)}, bf16[1024,512]{1,0:T(8,128)(2,1)}, u32[]{:S(2)}) copy-start(bf16[1024,512]{1,0:T(8,128)(2,1)} %get-tuple-element.31) | copy-start | bytes 3145732
  207.3 1.6 copy-start.1
  207.3 2.4 %copy-start.2 = (bf16[256,512]{1,0:T(8,128)(2,1)S(1)}, bf16[256,512]{1,0:T(8,128)(2,1)}, u32[]{:S(2)}) copy-start(bf16[256,512]{1,0:T(8,128)(2,1)} %get-tuple-element.37) | copy-start | bytes 786436

commit v3 on v2

--- a/solution.py
+++ b/solution.py
@@ -17,7 +17,7 @@
 F32 = jnp.float32
 VMEM = pl.BlockSpec(memory_space=pltpu.VMEM)
 SMEM = pl.BlockSpec(memory_space=pltpu.SMEM)
-LIMIT = 60 * 1024 * 1024
+LIMIT = 28 * 1024 * 1024
 
 
 def place():
@@ -75,52 +75,59 @@
 
 
 class Gather:
-    def __init__(self, copies, first, view, hops, where):
-        self.copies, self.first, self.view, self.hops, self.where = copies, first, view, hops, where
+    def __init__(self, copies, first, view, hops, ring, arrived=None):
+        self.copies, self.first, self.view, self.hops = copies, first, view, hops
+        self.place, self.size, self.sides = ring
+        self.arrived = arrived
         self.sent = [[], []]
 
     def step(self, s):
-        x, z, y, c = self.where
         for way, sign in ((0, 1), (1, -1)):
+            block = step_from(self.place, -sign * s, self.size)
             if 0 < s <= self.hops[way]:
                 self.sent[way][s - 1].wait_recv()
             if s < self.hops[way]:
-                block = step_from(z, -sign * s, Z)
                 src = self.first if s == 0 else self.view(block)
-                to = device(x, step_from(z, sign, Z), y, c)
-                self.sent[way].append(self.copies.start(src, self.view(block), to))
+                self.sent[way].append(self.copies.start(src, self.view(block), self.sides[way]))
+            if self.arrived is not None and 0 < s <= self.hops[way]:
+                self.arrived(block)
 
 
 class Scatter:
-    def __init__(self, copies, part, held, hops, where):
-        self.copies, self.part, self.held, self.hops, self.where = copies, part, held, hops, where
+    def __init__(self, copies, part, held, hops, ring):
+        self.copies, self.part, self.held, self.hops = copies, part, held, hops
+        self.place, self.size, self.sides = ring
         self.sent = [[], []]
 
     def step(self, s):
-        x, z, y, c = self.where
         for way, sign in ((0, 1), (1, -1)):
             n = self.hops[way]
             if 0 < s <= n:
                 self.sent[way][s - 1].wait_recv()
             if s < n:
-                goal = step_from(z, sign * (n - s), Z)
+                goal = step_from(self.place, sign * (n - s), self.size)
                 if s == 0:
                     src = self.part(goal)
                 else:
                     src = self.held(way, s - 1)
                     src[...] = (src[...].astype(F32) + self.part(goal)[...].astype(F32)).astype(BF)
-                to = device(x, step_from(z, sign, Z), y, c)
-                self.sent[way].append(self.copies.start(src, self.held(way, s), to))
+                self.sent[way].append(self.copies.start(src, self.held(way, s), self.sides[way]))
 
     def total(self):
-        z = self.where[1]
-        total = self.part(z)[...].astype(F32)
+        total = self.part(self.place)[...].astype(F32)
         for way in (0, 1):
             total += self.held(way, self.hops[way] - 1)[...].astype(F32)
         return total
 
 
+def rings(x, z, y, c):
+    along_z = z, Z, tuple(device(x, step_from(z, i, Z), y, c) for i in (1, -1))
+    along_y = y, Y, tuple(device(x, z, step_from(y, i, Y), c) for i in (1, -1))
+    return along_z, along_y
+
+
 HOPS = ((4, 3), (3, 4))
+HOPS_Y = ((2, 1), (1, 2))
 
 
 def spread_kernel(
@@ -128,19 +135,19 @@
     idall, qall, ktab, vtab, wf, upall,
     gfull, upp, upr, send, recv, local,
 ):
-    where = x, z, y, c = place()
+    x, z, y, c = place()
     t = y * C + c
     depth = w_ref.shape[0] // 4
     width = w_ref.shape[1]
     span = Z * width
     xs = [step_from(x, i, X) for i in range(X)]
-    ys = [step_from(y, i, Y) for i in range(Y)]
-    other = 1 - c
+    along_z, along_y = rings(x, z, y, c)
+    sibling = device(x, z, y, 1 - c)
     enter(
         [device(xs[i], z, y, c) for i in (1, 2, 3)]
-        + [device(x, step_from(z, i, Z), y, c) for i in (1, -1)]
-        + [device(x, z, ys[i], c) for i in (1, 2, 3)]
-        + [device(x, z, y, other)]
+        + list(along_z[2])
+        + list(along_y[2])
+        + [sibling]
     )
     copies = Copies(send, recv)
     kept = []
@@ -165,19 +172,19 @@
     def weight_piece(i):
         rows = pl.ds(i * depth, depth)
         return Gather(
-            copies, w_ref.at[rows], lambda b: wf.at[rows, columns(b, width)], HOPS[i % 2], where
+            copies, w_ref.at[rows], lambda b: wf.at[rows, columns(b, width)], HOPS[i % 2], along_z
         )
 
     def piece(ref, i):
-        return Gather(copies, ref.at[z, i], lambda b: ref.at[b, i], HOPS[i % 2], where)
+        return Gather(copies, ref.at[z, i], lambda b: ref.at[b, i], HOPS[i % 2], along_z)
 
     weights = [weight_piece(i) for i in range(4)]
     asked = [piece(qall, i) for i in range(X)]
     asked.append(
-        Gather(copies, idall.at[z], lambda b: idall.at[b], HOPS[0], where),
+        Gather(copies, idall.at[z], lambda b: idall.at[b], HOPS[0], along_z),
     )
     upstream = [piece(upall, i) for i in range(X)]
-    table_in, q_in, g_y, g_core, up_in = [], [], {}, {}, {}
+    table_in, q_in, g_core, up_in = [], [], {}, {}
 
     def step(pieces, s):
         for one in pieces:
@@ -194,27 +201,32 @@
             to = device(xs[i], z, y, c)
             table_in.append(copies.start(src.at[:, columns(xs[i], HD)], dst.at[x], to))
 
-    def send_rows():
-        kept[0].wait()
-        for copy in g_in:
-            copy.wait_recv()
-        for i in range(X):
-            block = gfull.at[i, t]
-            g_y[i] = [copies.start(block, block, device(x, z, ys[j], c)) for j in (1, 3, 2)]
-            g_core[i] = [copies.start(block, block, device(x, z, y, other))]
-
-    def hand_over(i):
-        for copy, j in zip(g_y[i], (-1, -3, -2)):
-            copy.wait_recv()
-            block = gfull.at[i, step_from(y, j, Y) * C + c]
-            g_core[i].append(copies.start(block, block, device(x, z, y, other)))
+    def hand_over(i, block):
+        block = gfull.at[i, block * C + c]
+        g_core[i].append(copies.start(block, block, sibling))
+
+    def rows_piece(i):
+        return Gather(
+            copies,
+            gfull.at[i, t],
+            lambda b: gfull.at[i, b * C + c],
+            HOPS_Y[i % 2],
+            along_y,
+            lambda b: hand_over(i, b),
+        )
+
+    rows = [rows_piece(i) for i in range(X)]
+
+    def send_rows(i):
+        rows[i].step(0)
+        g_core[i] = []
+        hand_over(i, y)
 
     def multiply(i):
         for copy in g_core[i]:
             copy.wait_recv()
-        rows = gfull[i].reshape(TOK, span)
         upp[i] = lax.dot_general(
-            rows, wf[...], (((1,), (1,)), ((), ())), preferred_element_type=F32
+            gfull[i].reshape(TOK, span), wf[...], (((1,), (1,)), ((), ())), preferred_element_type=F32
         ).astype(BF)
         up_in[i] = [
             copies.start(
@@ -235,48 +247,46 @@
     step(weights, 0)
     send_queries()
     step(weights, 1)
-    send_rows()
+    kept[0].wait()
+    for copy in g_in:
+        copy.wait_recv()
+    send_rows(0)
+    send_rows(1)
     step(weights, 2)
     for copy in q_in:
         copy.wait_recv()
     kept[1].wait()
     kept[5].wait()
+    step(rows[:1], 1)
+    step(weights[:2], 3)
+    step(rows[1:2], 1)
+    send_rows(2)
+    send_rows(3)
+    step(weights[2:], 3)
+    step(asked, 0)
     send_table(k_ref, ktab)
-    step(weights, 3)
-    step(asked, 0)
-    hand_over(0)
+    step(rows[:2], 2)
     step(weights, 4)
     kept[4].wait()
     multiply(0)
-    hand_over(1)
-    step(asked, 1)
+    step(asked[:2], 1)
     multiply(1)
-    hand_over(2)
+    step(rows[2:3], 1)
+    step(asked[2:], 1)
+    step(rows[3:], 1)
     step(asked, 2)
+    step(rows[2:], 2)
     multiply(2)
-    hand_over(3)
     total(0)
+    multiply(3)
     total(1)
     step(asked, 3)
-    multiply(3)
-    step(upstream[:1], 1)
     total(2)
+    total(3)
     send_table(v_ref, vtab)
-    step(upstream[1:2], 1)
     step(asked, 4)
-    step(upstream[:1], 2)
-    total(3)
-    step(upstream[1:2], 2)
-    step(upstream[2:3], 1)
-    step(upstream[:1], 3)
-    step(upstream[3:], 1)
-    step(upstream[1:2], 3)
-    step(upstream[2:3], 2)
-    step(upstream[:1], 4)
-    step(upstream[3:], 2)
-    step(upstream[1:2], 4)
-    step(upstream[2:], 3)
-    step(upstream[2:], 4)
+    for s in (1, 2, 3, 4):
+        step(upstream, s)
     for copy in table_in:
         copy.wait_recv()
     for copy in kept[2:4]:
@@ -534,19 +544,20 @@
 def collect_kernel(
     ctx, gq, dkey, dvalue, wf,
     out, gq_out, dk_out, dv_out,
-    held, ctx4, part, core_in, y_in, done, gq_done, send, recv, out_send, out_recv, local,
+    held, ctx4, ctx_other, wf_other, part, y_held, done, gq_done,
+    send, recv, out_send, out_recv, local,
 ):
-    where = x, z, y, c = place()
-    t = y * C + c
-    span = wf.shape[1]
+    x, z, y, c = place()
+    head_cols, span = wf.shape
+    slots = TOK // (Y * C)
     xs = [step_from(x, i, X) for i in range(X)]
-    ys = [step_from(y, i, Y) for i in range(Y)]
-    other = 1 - c
+    along_z, along_y = rings(x, z, y, c)
+    sibling = device(x, z, y, 1 - c)
     enter(
         [device(xs[i], z, y, c) for i in (1, 2, 3)]
-        + [device(x, step_from(z, i, Z), y, c) for i in (1, -1)]
-        + [device(x, z, ys[i], c) for i in (1, 2, 3)]
-        + [device(x, z, y, other)]
+        + list(along_z[2])
+        + list(along_y[2])
+        + [sibling]
     )
     copies = Copies(send, recv)
     kept = []
@@ -562,50 +573,58 @@
             lambda b: ref.at[b, i],
             lambda way, s: held.at[n, 4 * way + s],
             HOPS[n % 2],
-            where,
+            along_z,
         )
 
-    pieces = [piece(ctx, i, i) for i in range(X)]
-    pieces += [piece(gq, xs[i], X + i) for i in range(X)]
-    table_in, ctx_in, core_sent, y_sent, gq_sent = [], {}, {}, {}, []
-
-    def tables():
-        for src, dst in ((dkey, dk_out), (dvalue, dv_out)):
-            keep(src.at[x], dst.at[:, columns(x, HD)])
-            for i in (1, 3, 2):
-                table_in.append(
-                    copies.start(src.at[xs[i]], dst.at[:, columns(x, HD)], device(xs[i], z, y, c))
-                )
+    def out_piece(i):
+        return Scatter(
+            copies,
+            lambda b: part.at[i, b],
+            lambda way, s: y_held.at[i, 2 * way + s],
+            HOPS_Y[i % 2],
+            along_y,
+        )
+
+    contexts = [piece(ctx, i, i) for i in range(X)]
+    grads = [piece(gq, xs[i], X + i) for i in range(X)]
+    outs = [out_piece(i) for i in range(X)]
+    table_in, ctx_in, core_in, gq_sent = [], {}, {}, []
+
+    def step(pieces, s):
+        for one in pieces:
+            one.step(s)
+
+    def send_table(src, dst):
+        keep(src.at[x], dst.at[:, columns(x, HD)])
+        for i in (1, 3, 2):
+            table_in.append(
+                copies.start(src.at[xs[i]], dst.at[:, columns(x, HD)], device(xs[i], z, y, c))
+            )
 
     def share(i):
-        mine = ctx4.at[i, :, columns(x, HD)]
-        mine[...] = pieces[i].total().astype(BF)
+        mine = ctx4.at[i, :, :, :, columns(x, HD)]
+        mine[...] = contexts[i].total().astype(BF).reshape(Y, C, slots, HD)
         ctx_in[i] = [copies.start(mine, mine, device(xs[j], z, y, c)) for j in (1, 3, 2)]
 
-    def multiply(i):
+    def swap(i):
         for copy in ctx_in[i]:
             copy.wait_recv()
+        core_in[i] = copies.start(ctx4.at[i, :, 1 - c], ctx_other.at[i], sibling)
+
+    def multiply(i):
+        core_in[i].wait_recv()
+        mine = ctx4[i, :, c].reshape(Y * slots, head_cols)
+        others = ctx_other[i].reshape(Y * slots, head_cols)
         for j in range(2):
             cols = pl.ds(j * (span // 2), span // 2)
-            product = jnp.dot(ctx4[i], wf[:, cols], preferred_element_type=F32).astype(BF)
-            part[i, :, :, :, cols] = product.reshape(Y, C, TOK // (Y * C), span // 2)
-        core_sent[i] = copies.start(part.at[i, :, other], core_in.at[i], device(x, z, y, other))
-
-    def join(i):
-        core_sent[i].wait_recv()
-        core_in[i] = (core_in[i].astype(F32) + part[i, :, c].astype(F32)).astype(BF)
-        y_sent[i] = [
-            copies.start(core_in.at[i, ys[j]], y_in.at[i, j - 1], device(x, z, ys[j], c))
-            for j in (1, 3, 2)
-        ]
-
-    def total(i):
-        for copy in y_sent[i]:
-            copy.wait_recv()
-        value = core_in[i, y].astype(F32)
-        for j in range(3):
-            value += y_in[i, j].astype(F32)
-        done[i] = value.astype(BF)
+            product = jnp.dot(mine, wf[:, cols], preferred_element_type=F32)
+            product += jnp.dot(others, wf_other[:, cols], preferred_element_type=F32)
+            part[i, :, :, cols] = product.astype(BF).reshape(Y, slots, span // 2)
+        outs[i].step(0)
+
+    def finish_out(i):
+        outs[i].step(2)
+        done[i] = outs[i].total().astype(BF)
         goal = out.at[:, columns(x, span)]
 
         @pl.when(x == i)
@@ -627,43 +646,46 @@
             ).start()
 
     def queries(i):
-        gq_done[i] = pieces[X + i].total().astype(BF)
+        gq_done[i] = grads[i].total().astype(BF)
         goal = gq_out.at[:, columns(x, HD)]
         if i == 0:
             keep(gq_done.at[i], goal)
         else:
             gq_sent.append(copies.start(gq_done.at[i], goal, device(xs[i], z, y, c)))
 
-    def step(pieces, s):
-        for one in pieces:
-            one.step(s)
-
-    contexts, grads = pieces[:X], pieces[X:]
     step(contexts, 0)
-    tables()
+    weight_in = copies.start(wf, wf_other, sibling)
+    send_table(dkey, dk_out)
+    send_table(dvalue, dv_out)
     for s in (1, 2, 3):
         step(contexts, s)
     step(grads, 0)
     for i in range(X):
         contexts[i].step(4)
         share(i)
-    step(grads, 1)
+    weight_in.wait_recv()
+    swap(0)
+    step(grads[:2], 1)
     multiply(0)
+    swap(1)
+    step(grads[2:], 1)
     multiply(1)
-    join(0)
+    swap(2)
+    step(grads[:2], 2)
     multiply(2)
-    join(1)
-    step(grads, 2)
+    swap(3)
+    step(grads[2:], 2)
     multiply(3)
-    join(2)
-    join(3)
+    step(outs[:2], 1)
     step(grads, 3)
-    total(0)
+    finish_out(0)
+    finish_out(1)
+    step(outs[2:], 1)
     for i in range(X):
         grads[i].step(4)
         queries(i)
-    for i in (1, 2, 3):
-        total(i)
+    finish_out(2)
+    finish_out(3)
     for copy in table_in + gq_sent:
         copy.wait_recv()
     for i in (1, 2, 3):
@@ -698,10 +720,11 @@
         out_specs=[VMEM] * 4,
         scratch_shapes=[
             pltpu.VMEM((2 * X, 8, TOK, HD), BF),
-            pltpu.VMEM((X, TOK, head_cols), BF),
-            pltpu.VMEM((X, Y, C, slots, span), BF),
+            pltpu.VMEM((X, Y, C, slots, head_cols), BF),
+            pltpu.VMEM((X, Y, slots, head_cols), BF),
+            pltpu.VMEM((head_cols, span), BF),
             pltpu.VMEM((X, Y, slots, span), BF),
-            pltpu.VMEM((X, Y - 1, slots, span), BF),
+            pltpu.VMEM((X, 4, slots, span), BF),
             pltpu.VMEM((X, slots, span), BF),
             pltpu.VMEM((X, TOK, HD), BF),
             pltpu.SemaphoreType.DMA((120,)),

time: 211 us -> 190 us (0.900); the launches traced: 210 us -> 187 us
  Pallas kernels: 202 us -> 175 us
  local copies, waits for them, and re-layouts: 2.22 us -> 7.07 us
    pallas_call x1, Pallas kernels: 21.3 us -> 10.5 us  [grads_of_uses(): pl.pallas_call(grads_kernel, out_shape=(jax.ShapeDtypeStruct((tokens, HD)...]
    pallas_call x1, Pallas kernels: 72.6 us -> 65.5 us  [collect(): pl.pallas_call(collect_kernel, out_shape=(jax.ShapeDtypeStruct((slots, X...]
    pallas_call x1, Pallas kernels: 80.4 us -> 73.5 us  [spread(): pl.pallas_call(spread_kernel, out_shape=(jax.ShapeDtypeStruct((Z, X) + id...]
    pallas_call x1, Pallas kernels: 12.6 us -> 6.58 us  [stats_of_uses(): pl.pallas_call(stats_kernel, out_shape=jax.ShapeDtypeStruct((3, 16 * Z, 2...]
    unnamed x8 -> x12, local copies, waits for them, and re-layouts: 1.51 us -> 6.88 us
    pallas_call x1, Pallas kernels: 15.4 us -> 19.1 us  [totals(): pl.pallas_call(totals_kernel, out_shape=jax.ShapeDtypeStruct((2,) + stats...]
where the time goes in v3:
time: 190 us; the launch traced here: 187 us
  Pallas kernels  175 us (92%)
  local copies, waits for them, and re-layouts  7.07 us (4%)
  other arithmetic  3.92 us (2%)
    pallas_call x1, Pallas kernels, spread(): pl.pallas_call(spread_kernel, out_shape=(jax.ShapeDtypeStruct((Z, X) + id...  73.5 us
    pallas_call x1, Pallas kernels, collect(): pl.pallas_call(collect_kernel, out_shape=(jax.ShapeDtypeStruct((slots, X...  65.5 us
    pallas_call x1, Pallas kernels, totals(): pl.pallas_call(totals_kernel, out_shape=jax.ShapeDtypeStruct((2,) + stats...  19.1 us
    pallas_call x1, Pallas kernels, grads_of_uses(): pl.pallas_call(grads_kernel, out_shape=(jax.ShapeDtypeStruct((tokens, HD)...  10.5 us
    unnamed x12, local copies, waits for them, and re-layouts  6.88 us
    pallas_call x1, Pallas kernels, stats_of_uses(): pl.pallas_call(stats_kernel, out_shape=jax.ShapeDtypeStruct((3, 16 * Z, 2...  6.58 us

profile of v3, /device:TPU:6, one launch (start us, length us, event | category | flops | bytes accessed | tf_op | source)
XLA Modules:
  0.0 186.9 jit_solution(18123549055010124847)
XLA Ops:
  0.6 0.7 pad_add_fusion
  1.3 0.1 copy.12
  1.4 0.1 reshape.35
  1.5 0.0 copy-start
  1.5 1.2 copy-done
  2.8 0.0 copy-start.1
  2.8 1.2 copy-done.1
  4.0 0.0 copy-start.2
  4.0 1.0 copy-done.2
  5.0 0.0 copy-start.3
  5.0 0.9 copy-done.3
  6.0 0.0 copy-start.4
  6.0 0.9 copy-done.4
  6.9 73.5 %spread.1 = (s32[8,4,1,128]{3,2,1,0:T(1,128)S(1)}, bf16[8,4,256,128]{3,2,1,0:T(8,128)(2,1)S(1)}, bf16[4,1024,128]{2,1,0:T(8,128)(2,1)S(1)}, bf16[4,1024,128]{2,1...) custom-call(s32[1,128]{1,0:T(1,128)S(1)} %pad.4.ids_ref, ...), custom_call_target="tpu_custom_call" | custom-call | tf_op jit(solution)/shard_map/spread/pallas_call | solution.py:300
  80.5 6.6 %stats.1 = f32[3,128,128]{2,1,0:T(8,128)S(1)} custom-call(s32[8,4,1,128]{3,2,1,0:T(1,128)S(1)} %get-tuple-element.18.ids, bf16[8192,128]{1,0:T(8,128)(2,1)S(1)} %bitcast.10, bf16[8192,128]{1,0:T(8,128)(2,1)S(1)} %bitcast.12, bf16[4096,128]{1,0:T(8,128)(2,1)S(1)} %bitcast.14, bf16[4096,128]{1,0:T(8,128)(2,1)S(1)} %bitcast.16), custom_call_target="tpu_custom_call" | custom-call | tf_op jit(solution)/shard_map/stats/pallas_call | solution.py:399
  87.1 19.1 %totals.1.sums = f32[2,128,128]{2,1,0:T(8,128)S(1)} custom-call(f32[3,128,128]{2,1,0:T(8,128)S(1)} %stats.1), custom_call_target="tpu_custom_call" | custom-call | tf_op jit(solution)/shard_map/totals/pallas_call | solution.py:438
  106.2 10.5 %grads.1 = (bf16[8192,128]{1,0:T(8,128)(2,1)S(1)}, bf16[8192,128]{1,0:T(8,128)(2,1)S(1)}, bf16[4096,128]{1,0:T(8,128)(2,1)S(1)}, bf16[4096,128]{1,0:T(8,128)(2,1)S(1)}) custom-call(s32[8,4,1,128]{3,2,1,0:T(1,128)S(1)} %get-tuple-element.18.ids, bf16[8192,128]{1,0:T(8,128)(2,1)S(1)} %bitcast.11, bf16[8192,128]{1,0:T(8,128)(2,1)S(1)} %bitcast.13, ...), custom_call_target="tpu_custom_call" | custom-call | tf_op jit(solution)/shard_map/grads/pallas_call | solution.py:523
  116.7 65.5 %collect.1 = (bf16[32,8192]{1,0:T(8,128)(2,1)S(1)}, bf16[256,512]{1,0:T(8,128)(2,1)S(1)}, bf16[1024,512]{1,0:T(8,128)(2,1)S(1)}, bf16[1024,512]{1,0:T(8,128)(2,1)S(1)}) custom-call(bf16[8,4,256,128]{3,2,1,0:T(8,128)(2,1)S(1)} %bitcast.18, bf16[8,4,256,128]{3,2,1,0:T(8,128)(2,1)S(1)} %bitcast.19, bf16[4,1024,128]{2,1,0:T(8,128)(2,1)S(1)} %bitcast.20, ...), custom_call_target="tpu_custom_call" | custom-call | tf_op jit(solution)/shard_map/collect/pallas_call | solution.py:711
  182.2 1.6 convert_element_type.6
  183.8 1.6 convert_element_type.7
  185.4 0.8 copy.15
  186.2 0.7 copy.16
  (1 shorter events, 0.0 us)
Async XLA Ops:
  1.5 1.2 copy-start
  2.8 1.2 copy-start.1
  4.0 1.0 copy-start.2
  5.0 0.9 copy-start.3
  6.0 0.9 copy-start.4

commit v4 on v3

v4 whole, which is shorter than its diff:
```python
import functools

import jax
import jax.numpy as jnp
from jax import lax
from jax.experimental import pallas as pl
from jax.experimental.pallas import tpu as pltpu
from jax.sharding import PartitionSpec as P

X, Z, Y, C = 4, 8, 4, 2
HD = 128
GROUP = 64
NLEN = 128
NB_DEV = 8
TOK = 256
SCALE = HD**-0.5
LOW = -1e30
BF = jnp.bfloat16
F32 = jnp.float32
VMEM = pl.BlockSpec(memory_space=pltpu.VMEM)
SMEM = pl.BlockSpec(memory_space=pltpu.SMEM)
HBM = pl.BlockSpec(memory_space=pltpu.HBM)
LIMIT = 28 * 1024 * 1024


def place():
    dp, t = lax.axis_index("dp"), lax.axis_index("tensor")
    return lax.div(dp, Z), lax.rem(dp, Z), lax.div(t, C), lax.rem(t, C)


def device(x, z, y, c):
    return (x * Z + z, y * C + c)


def step_from(i, by, n):
    return lax.rem(i + (by + n), n)


def columns(i, width):
    return pl.ds(pl.multiple_of(i * width, width), width)


def enter(peers):
    barrier = pltpu.get_barrier_semaphore()
    for peer in peers:
        pl.semaphore_signal(barrier, inc=1, device_id=peer, device_id_type=pl.DeviceIdType.MESH)
    pl.semaphore_wait(barrier, len(peers))


class Copies:
    def __init__(self, send, recv):
        self.send, self.recv, self.count, self.started = send, recv, 0, []

    def take(self, n=1):
        first = self.count
        self.count += n
        return first

    def make(self, sem, src, dst, to):
        return pltpu.make_async_remote_copy(
            src_ref=src,
            dst_ref=dst,
            send_sem=self.send.at[sem],
            recv_sem=self.recv.at[sem],
            device_id=to,
            device_id_type=pl.DeviceIdType.MESH,
        )

    def start(self, src, dst, to):
        copy = self.make(self.take(), src, dst, to)
        copy.start()
        self.started.append(copy)
        return copy

    def finish(self):
        for copy in self.started:
            copy.wait_send()


class Gather:
    def __init__(self, copies, first, view, hops, ring, arrived=None):
        self.copies, self.first, self.view, self.hops = copies, first, view, hops
        self.place, self.size, self.sides = ring
        self.arrived = arrived
        self.sent = [[], []]

    def step(self, s):
        for way, sign in ((0, 1), (1, -1)):
            block = step_from(self.place, -sign * s, self.size)
            if 0 < s <= self.hops[way]:
                self.sent[way][s - 1].wait_recv()
            if s < self.hops[way]:
                src = self.first if s == 0 else self.view(block)
                self.sent[way].append(self.copies.start(src, self.view(block), self.sides[way]))
            if self.arrived is not None and 0 < s <= self.hops[way]:
                self.arrived(block)


class Scatter:
    def __init__(self, copies, first, value, held, hops, ring):
        self.copies, self.first, self.value, self.held, self.hops = copies, first, value, held, hops
        self.place, self.size, self.sides = ring
        self.sent = [[], []]

    def step(self, s):
        for way, sign in ((0, 1), (1, -1)):
            n = self.hops[way]
            if 0 < s <= n:
                self.sent[way][s - 1].wait_recv()
            if s < n:
                goal = step_from(self.place, sign * (n - s), self.size)
                if s == 0:
                    src = self.first(way, goal)
                else:
                    src = self.held(way, s - 1)
                    src[...] = (src[...].astype(F32) + self.value(goal)).astype(BF)
                self.sent[way].append(self.copies.start(src, self.held(way, s), self.sides[way]))

    def total(self):
        total = self.value(self.place)
        for way in (0, 1):
            total += self.held(way, self.hops[way] - 1)[...].astype(F32)
        return total


def rings(x, z, y, c):
    along_z = z, Z, tuple(device(x, step_from(z, i, Z), y, c) for i in (1, -1))
    along_y = y, Y, tuple(device(x, z, step_from(y, i, Y), c) for i in (1, -1))
    return along_z, along_y


HOPS = ((4, 3), (3, 4))
HOPS_Y = ((2, 1), (1, 2))


def start_local(local, kept, src, dst):
    copy = pltpu.make_async_copy(src, dst, local.at[len(kept)])
    copy.start()
    kept.append(copy)


def step_all(pieces, s):
    for one in pieces:
        one.step(s)


def weight_piece(copies, first, wf, width, i, along_z):
    depth = wf.shape[0] // 2
    rows = pl.ds(i * depth, depth)
    return Gather(
        copies, first, lambda b: wf.at[rows, columns(b, width)], HOPS[i % 2], along_z
    )


def spread_kernel(
    ids_ref, q_ref, k_ref, v_ref, w_ref, g_ref,
    idall, qall, ktab, vtab, wf, gfull,
    send, recv, local,
):
    x, z, y, c = place()
    t = y * C + c
    width = w_ref.shape[1]
    depth = w_ref.shape[0] // 4
    span = Z * width
    xs = [step_from(x, i, X) for i in range(X)]
    along_z, along_y = rings(x, z, y, c)
    sibling = device(x, z, y, 1 - c)
    enter(
        [device(xs[i], z, y, c) for i in (1, 2, 3)]
        + list(along_z[2])
        + list(along_y[2])
        + [sibling]
    )
    copies = Copies(send, recv)
    kept = []

    def keep(src, dst):
        start_local(local, kept, src, dst)

    table_in, q_in, g_core = [], [], {}

    def piece(ref, i):
        return Gather(copies, ref.at[z, i], lambda b: ref.at[b, i], HOPS[i % 2], along_z)

    weights = [
        weight_piece(copies, w_ref.at[pl.ds(i * depth, depth)], wf, width, i, along_z)
        for i in range(2)
    ]
    asked = [piece(qall, i) for i in range(X)]
    asked.append(Gather(copies, idall.at[z], lambda b: idall.at[b], HOPS[0], along_z))

    def send_table(src, dst):
        for i in (1, 3, 2):
            to = device(xs[i], z, y, c)
            table_in.append(copies.start(src.at[:, columns(xs[i], HD)], dst.at[x], to))

    def hand_over(i, block):
        block = gfull.at[i, block * C + c]
        g_core[i].append(copies.start(block, block, sibling))

    def rows_piece(i):
        return Gather(
            copies,
            gfull.at[i, t],
            lambda b: gfull.at[i, b * C + c],
            HOPS_Y[i % 2],
            along_y,
            lambda b: hand_over(i, b),
        )

    rows = [rows_piece(i) for i in range(X)]

    def send_rows(i):
        rows[i].step(0)
        g_core[i] = []
        hand_over(i, y)

    for i in (1, 3, 2):
        to = device(xs[i], z, y, c)
        q_in.append(copies.start(q_ref.at[:, columns(xs[i], HD)], qall.at[z, x], to))
        q_in.append(copies.start(ids_ref, idall.at[z, x], to))
    step_all(weights, 0)
    g_in = [
        copies.start(g_ref.at[:, columns(xs[i], span)], gfull.at[x, t], device(xs[i], z, y, c))
        for i in (1, 3, 2)
    ]
    keep(q_ref.at[:, columns(x, HD)], qall.at[z, x])
    keep(ids_ref, idall.at[z, x])
    keep(g_ref.at[:, columns(x, span)], gfull.at[x, t])
    keep(w_ref.at[pl.ds(0, 2 * depth)], wf.at[:, columns(z, width)])
    keep(k_ref.at[:, columns(x, HD)], ktab.at[x])
    keep(v_ref.at[:, columns(x, HD)], vtab.at[x])
    step_all(weights, 1)
    for copy in q_in:
        copy.wait_recv()
    for copy in kept[:2]:
        copy.wait()
    step_all(asked, 0)
    send_table(k_ref, ktab)
    send_table(v_ref, vtab)
    step_all(weights, 2)
    kept[2].wait()
    for copy in g_in:
        copy.wait_recv()
    send_rows(0)
    send_rows(1)
    step_all(asked, 1)
    step_all(weights, 3)
    step_all(rows[:2], 1)
    send_rows(2)
    send_rows(3)
    step_all(asked, 2)
    step_all(rows[:2], 2)
    step_all(weights, 4)
    step_all(asked, 3)
    step_all(rows[2:], 1)
    step_all(rows[2:], 2)
    step_all(asked, 4)
    for i in range(X):
        for copy in g_core[i]:
            copy.wait_recv()
    for copy in table_in:
        copy.wait_recv()
    for copy in kept[3:]:
        copy.wait()
    copies.finish()


def spread(ids, queries, keys, values, out_weight, grad_out):
    depth, width = out_weight.shape
    rows = keys.shape[0]
    return pl.pallas_call(
        spread_kernel,
        out_shape=(
            jax.ShapeDtypeStruct((Z, X) + ids.shape, jnp.int32),
            jax.ShapeDtypeStruct((Z, X, TOK, HD), BF),
            jax.ShapeDtypeStruct((X, rows, HD), BF),
            jax.ShapeDtypeStruct((X, rows, HD), BF),
            jax.ShapeDtypeStruct((depth // 2, Z * width), BF),
            jax.ShapeDtypeStruct((X, Y * C, grad_out.shape[0], Z * width), BF),
        ),
        in_specs=[VMEM] + [HBM] * 5,
        out_specs=[VMEM] * 6,
        scratch_shapes=[
            pltpu.SemaphoreType.DMA((96,)),
            pltpu.SemaphoreType.DMA((96,)),
            pltpu.SemaphoreType.DMA((8,)),
        ],
        compiler_params=pltpu.CompilerParams(
            collective_id=0, has_side_effects=True, vmem_limit_bytes=LIMIT
        ),
        name="spread",
    )(ids, queries, keys, values, out_weight, grad_out)


def list_uses(ids, groups, names):
    z = lax.rem(lax.axis_index("dp"), Z)

    def add(i, n):
        dp_z, dp_x = lax.shift_right_logical(i, 5), lax.shift_right_logical(i, 3) & 3
        owner, name = (ids[dp_z, dp_x, 0, 2 * (i & 7) + j] for j in (0, 1))
        groups[n] = lax.shift_right_logical(i, 1)
        names[n] = lax.shift_right_logical(owner, 3) * NB_DEV + name
        return n + ((owner & 7) == z).astype(jnp.int32)

    n = lax.fori_loop(0, X * Z * 8, add, jnp.int32(0), unroll=8)
    last = jnp.maximum(n - 1, 0)
    groups[n] = groups[last]
    names[n] = names[last]
    return n


def pair_rows(ref, a, b, size):
    return [ref[pl.ds(pl.multiple_of(i * size, size), size), :] for i in (a, b)]


def pair_scores(first, second, both, left):
    product = lax.dot_general(
        jnp.concatenate([first, second], axis=0),
        both,
        (((1,), (1,)), ((), ())),
        preferred_element_type=F32,
    )
    return jnp.where(left, product[:NLEN], product[NLEN:])


def merge(one, two):
    peak = jnp.maximum(one[0], two[0])
    return peak, jnp.exp(one[0] - peak) * one[1] + jnp.exp(two[0] - peak) * two[1]


def clear(ref, rows=512):
    @pl.loop(0, ref.shape[0] // rows)
    def _(i):
        ref[pl.ds(pl.multiple_of(i * rows, rows), rows), :] = jnp.zeros((rows, HD), ref.dtype)


def add_rows(ref, i, size, value):
    at = pl.ds(pl.multiple_of(i * size, size), size)
    ref[at, :] = (ref[at, :].astype(F32) + value).astype(ref.dtype)


def attend_kernel(ids, qall, ktab, vtab, logs, ctx, groups, names, stats):
    n = list_uses(ids, groups, names)
    stats[0] = jnp.full(stats.shape[1:], LOW, F32)
    stats[1] = jnp.zeros(stats.shape[1:], F32)
    clear(ctx)
    left = lax.broadcasted_iota(jnp.int32, (1, 2 * GROUP), 1) < GROUP

    def scores_of(ga, gb, na, nb):
        qq = jnp.concatenate(pair_rows(qall, ga, gb, GROUP), axis=0)
        return pair_scores(*pair_rows(ktab, na, nb, NLEN), qq, left) * SCALE

    def measure(p, carry):
        a, b = 2 * p, 2 * p + 1
        ga, gb, na, nb = groups[a], groups[b], names[a], names[b]
        scores = scores_of(ga, gb, na, nb)
        peak = jnp.max(scores, axis=0, keepdims=True)
        total = jnp.sum(jnp.exp(scores - peak), axis=0, keepdims=True)
        real = left | (b < n)
        new = jnp.where(real, peak, LOW), jnp.where(real, total, 0.0)
        for g, mine in ((ga, left), (gb, jnp.logical_not(left))):
            old = tuple(stats[i, pl.ds(g, 1), :] for i in range(2))
            merged = merge(old, new)
            for i in range(2):
                stats[i, pl.ds(g, 1), :] = jnp.where(mine, merged[i], old[i])
        return carry

    def weigh(p, carry):
        a, b = 2 * p, 2 * p + 1
        ga, gb, na, nb = groups[a], groups[b], names[a], names[b]
        scores = scores_of(ga, gb, na, nb)
        log_total = jnp.where(left, logs[pl.ds(ga, 1), :], logs[pl.ds(gb, 1), :])
        prob = jnp.where(left | (b < n), jnp.exp(scores - log_total), 0.0)
        values = pair_rows(vtab, na, nb, NLEN)
        context = jnp.dot(
            prob.T.astype(BF), jnp.concatenate(values, axis=1), preferred_element_type=F32
        )
        add_rows(ctx, ga, GROUP, context[:GROUP, :HD])
        add_rows(ctx, gb, GROUP, context[GROUP:, HD:])
        return carry

    lax.fori_loop(0, (n + 1) // 2, measure, 0)
    state = stats[0], stats[1]
    peak, total = merge(state, tuple(pltpu.roll(v, GROUP, 1) for v in state))
    logs[...] = jnp.where(total > 0.0, peak + jnp.log(jnp.maximum(total, 1e-30)), LOW)
    lax.fori_loop(0, (n + 1) // 2, weigh, 0)


def attend(ids, qall, ktab, vtab):
    return pl.pallas_call(
        attend_kernel,
        out_shape=(
            jax.ShapeDtypeStruct((16 * Z, 2 * GROUP), F32),
            jax.ShapeDtypeStruct(qall.shape, BF),
        ),
        in_specs=[SMEM] + [VMEM] * 3,
        out_specs=[VMEM] * 2,
        scratch_shapes=[
            pltpu.SMEM((264,), jnp.int32),
            pltpu.SMEM((264,), jnp.int32),
            pltpu.VMEM((2, 16 * Z, 2 * GROUP), F32),
        ],
        compiler_params=pltpu.CompilerParams(vmem_limit_bytes=LIMIT),
        name="attend",
    )(ids, qall, ktab, vtab)


def project_kernel(
    logs, ctx, wa, w_ref, gfull,
    sums, upall, out,
    wb, wo, logs_in, upp, upr, staged, held, ctx4, ctx_other, part, y_held, done,
    send, recv, out_send, out_recv, local,
):
    x, z, y, c = place()
    half, span = wa.shape
    width = w_ref.shape[1]
    depth = half // 2
    head_cols = 2 * half
    slots = TOK // (Y * C)
    xs = [step_from(x, i, X) for i in range(X)]
    zs = [step_from(z, i, Z) for i in range(Z)]
    order = (4, 3, 5, 2, 6, 1, 7)
    along_z, along_y = rings(x, z, y, c)
    sibling = device(x, z, y, 1 - c)
    enter(
        [device(xs[i], z, y, c) for i in (1, 2, 3)]
        + [device(x, zs[i], y, c) for i in order]
        + list(along_y[2])
        + [sibling]
    )
    copies = Copies(send, recv)
    kept = []
    left = lax.broadcasted_iota(jnp.int32, (1, 2 * GROUP), 1) < GROUP
    own = pl.ds(pl.multiple_of(z * 16, 16), 16)
    up_in, ctx_in, core_in = {}, {}, {}

    def tell(ref):
        return [copies.start(ref, ref, device(x, zs[i], y, c)) for i in order]

    def send_logs():
        return [
            copies.start(logs.at[columns(zs[i], 16)], logs_in.at[i - 1], device(x, zs[i], y, c))
            for i in order
        ]

    def merge_logs():
        parts = [logs[own, :]] + [logs_in[i] for i in range(Z - 1)]
        peak = functools.reduce(jnp.maximum, parts)
        total = sum(jnp.exp(v - peak) for v in parts)
        sums[0, own, :] = peak + jnp.log(total)

    def multiply_rows(i, w, at):
        upp[i, :, at] = lax.dot_general(
            gfull[i].reshape(TOK, span),
            w[...],
            (((1,), (1,)), ((), ())),
            preferred_element_type=F32,
        ).astype(BF)

    def send_up(i):
        up_in[i] = [
            copies.start(
                upp.at[i, :, columns(xs[j], HD)], upr.at[i, j - 1], device(xs[j], z, y, c)
            )
            for j in (1, 3, 2)
        ]

    def total_up(i):
        for copy in up_in[i]:
            copy.wait_recv()
        value = upp[i, :, columns(x, HD)].astype(F32)
        for j in range(3):
            value += upr[i, j].astype(F32)
        upall[z, i] = value.astype(BF)
        upstream[i].step(0)

    def scaled(b, i):
        rows = []
        for j in range(2):
            at = [pl.ds(b * 16 + i * 4 + 2 * j + k, 1) for k in (0, 1)]
            factor = [jnp.exp(logs[r, :] - sums[0, r, :]) for r in at]
            factor = jnp.broadcast_to(jnp.where(left, *factor), (2 * GROUP, HD))
            rows.append(factor.T)
        return jnp.concatenate(rows, axis=0) * ctx[b, i].astype(F32)

    def context_piece(i):
        def first(way, b):
            staged[i, way] = scaled(b, i).astype(BF)
            return staged.at[i, way]

        return Scatter(
            copies,
            first,
            lambda b: scaled(b, i),
            lambda way, s: held.at[i, 4 * way + s],
            HOPS[i % 2],
            along_z,
        )

    def out_piece(i):
        return Scatter(
            copies,
            lambda way, b: part.at[i, b],
            lambda b: part[i, b].astype(F32),
            lambda way, s: y_held.at[i, 2 * way + s],
            HOPS_Y[i % 2],
            along_y,
        )

    weights = [
        weight_piece(copies, w_ref.at[pl.ds(half + i * depth, depth)], wb, width, i, along_z)
        for i in range(2)
    ]
    contexts = [context_piece(i) for i in range(X)]
    outs = [out_piece(i) for i in range(X)]
    upstream = [
        Gather(copies, upall.at[z, i], lambda b, i=i: upall.at[b, i], HOPS[i % 2], along_z)
        for i in range(X)
    ]

    def share(i):
        context = contexts[i].total().astype(BF)
        mine = ctx4.at[i, :, :, :, columns(x, HD)]
        mine[...] = context.reshape(Y, C, slots, HD)
        ctx_in[i] = [copies.start(mine, mine, device(xs[j], z, y, c)) for j in (1, 3, 2)]

    def inner(i):
        context = ctx4[i, :, :, :, columns(x, HD)].reshape(TOK, HD)
        product = upall[z, i].astype(F32) * context.astype(F32)
        for j in range(2):
            rows = product[j * 2 * GROUP : (j + 1) * 2 * GROUP]
            row = jnp.sum(rows.T, axis=0, keepdims=True)
            turned = pltpu.roll(row, GROUP, 1)
            at = z * 16 + i * 4 + 2 * j
            sums[1, pl.ds(at, 1), :] = jnp.where(left, row, turned)
            sums[1, pl.ds(at + 1, 1), :] = jnp.where(left, turned, row)

    def swap(i):
        for copy in ctx_in[i]:
            copy.wait_recv()
        core_in[i] = copies.start(ctx4.at[i, :, 1 - c], ctx_other.at[i], sibling)

    def multiply(i):
        core_in[i].wait_recv()
        terms = (
            (ctx4[i, :, c].reshape(Y * slots, head_cols), wa, wb),
            (ctx_other[i].reshape(Y * slots, head_cols), wo.at[0], wo.at[1]),
        )
        for j in range(2):
            cols = pl.ds(j * (span // 2), span // 2)
            product = 0.0
            for rows, first, second in terms:
                product += jnp.dot(rows[:, :half], first[:, cols], preferred_element_type=F32)
                product += jnp.dot(rows[:, half:], second[:, cols], preferred_element_type=F32)
            part[i, :, :, cols] = product.astype(BF).reshape(Y, slots, span // 2)
        outs[i].step(0)

    def finish_out(i):
        outs[i].step(2)
        done[i] = outs[i].total().astype(BF)
        goal = out.at[:, columns(x, span)]

        @pl.when(x == i)
        def _():
            copy = pltpu.make_async_copy(done.at[i], goal, local.at[7])
            copy.start()
            copy.wait()

        @pl.when(x != i)
        def _():
            sem = step_from(i - x, 0, X)
            pltpu.make_async_remote_copy(
                src_ref=done.at[i],
                dst_ref=goal,
                send_sem=out_send.at[sem],
                recv_sem=out_recv.at[sem],
                device_id=device(i, z, y, c),
                device_id_type=pl.DeviceIdType.MESH,
            ).start()

    logs_sent = send_logs()
    step_all(weights, 0)
    wa_in = copies.start(wa, wo.at[0], sibling)
    start_local(local, kept, w_ref.at[pl.ds(half, half)], wb.at[:, columns(z, width)])
    multiply_rows(0, wa, pl.ds(0, half))
    multiply_rows(1, wa, pl.ds(0, half))
    step_all(weights, 1)
    for copy in logs_sent:
        copy.wait_recv()
    merge_logs()
    logs_back = tell(sums.at[0, own])
    multiply_rows(2, wa, pl.ds(0, half))
    multiply_rows(3, wa, pl.ds(0, half))
    step_all(weights, 2)
    step_all(weights, 3)
    for copy in logs_back:
        copy.wait_recv()
    step_all(contexts, 0)
    step_all(weights, 4)
    kept[0].wait()
    wb_in = copies.start(wb, wo.at[1], sibling)
    multiply_rows(0, wb, pl.ds(half, half))
    send_up(0)
    step_all(contexts[:2], 1)
    multiply_rows(1, wb, pl.ds(half, half))
    send_up(1)
    step_all(contexts[2:], 1)
    multiply_rows(2, wb, pl.ds(half, half))
    send_up(2)
    step_all(contexts[:2], 2)
    multiply_rows(3, wb, pl.ds(half, half))
    send_up(3)
    step_all(contexts[2:], 2)
    step_all(contexts, 3)
    total_up(0)
    total_up(1)
    for i in range(X):
        contexts[i].step(4)
        share(i)
    total_up(2)
    total_up(3)
    wa_in.wait_recv()
    wb_in.wait_recv()
    swap(0)
    step_all(upstream, 1)
    multiply(0)
    swap(1)
    for i in range(X):
        inner(i)
    inner_back = tell(sums.at[1, own])
    multiply(1)
    swap(2)
    step_all(upstream, 2)
    multiply(2)
    swap(3)
    multiply(3)
    step_all(outs[:2], 1)
    step_all(upstream, 3)
    finish_out(0)
    finish_out(1)
    step_all(outs[2:], 1)
    step_all(upstream, 4)
    finish_out(2)
    finish_out(3)
    for copy in inner_back:
        copy.wait_recv()
    for i in (1, 2, 3):
        copy = pltpu.make_async_remote_copy(
            src_ref=done.at[0],
            dst_ref=out.at[:, columns(xs[i], span)],
            send_sem=out_send.at[i],
            recv_sem=out_recv.at[i],
            device_id=device(xs[i], z, y, c),
            device_id_type=pl.DeviceIdType.MESH,
        )
        copy.wait_recv()
        copy.wait_send()
    copies.finish()


def project(logs, ctx, wa, out_weight, gfull):
    half, span = wa.shape
    slots = TOK // (Y * C)
    return pl.pallas_call(
        project_kernel,
        out_shape=(
            jax.ShapeDtypeStruct((2,) + logs.shape, F32),
            jax.ShapeDtypeStruct(ctx.shape, BF),
            jax.ShapeDtypeStruct((slots, X * span), BF),
        ),
        in_specs=[VMEM] * 3 + [HBM] + [VMEM],
        out_specs=[VMEM] * 3,
        scratch_shapes=[
            pltpu.VMEM((half, span), BF),
            pltpu.VMEM((2, half, span), BF),
            pltpu.VMEM((Z - 1, 16, 2 * GROUP), F32),
            pltpu.VMEM((X, TOK, 2 * half), BF),
            pltpu.VMEM((X, X - 1, TOK, HD), BF),
            pltpu.VMEM((X, 2, TOK, HD), BF),
            pltpu.VMEM((X, 8, TOK, HD), BF),
            pltpu.VMEM((X, Y, C, slots, 2 * half), BF),
            pltpu.VMEM((X, Y, slots, 2 * half), BF),
            pltpu.VMEM((X, Y, slots, span), BF),
            pltpu.VMEM((X, 4, slots, span), BF),
            pltpu.VMEM((X, slots, span), BF),
            pltpu.SemaphoreType.DMA((144,)),
            pltpu.SemaphoreType.DMA((144,)),
            pltpu.SemaphoreType.DMA((4,)),
            pltpu.SemaphoreType.DMA((4,)),
            pltpu.SemaphoreType.DMA((8,)),
        ],
        compiler_params=pltpu.CompilerParams(
            collective_id=1, has_side_effects=True, vmem_limit_bytes=LIMIT
        ),
        name="project",
    )(logs, ctx, wa, out_weight, gfull)


def grads_kernel(
    ids, qall, upall, ktab, vtab, sums, gq, dkey, dvalue, groups, names, dk, dv
):
    n = list_uses(ids, groups, names)
    for ref in (gq, dk, dv):
        clear(ref)

    left = lax.broadcasted_iota(jnp.int32, (1, 2 * GROUP), 1) < GROUP
    zero = jnp.zeros((), BF)

    def dot(a, b):
        return jnp.dot(a, b, preferred_element_type=F32)

    def pair(p, carry):
        a, b = 2 * p, 2 * p + 1
        ga, gb, na, nb = groups[a], groups[b], names[a], names[b]
        qq = jnp.concatenate(pair_rows(qall, ga, gb, GROUP), axis=0)
        uu = jnp.concatenate(pair_rows(upall, ga, gb, GROUP), axis=0)
        keys = pair_rows(ktab, na, nb, NLEN)
        values = pair_rows(vtab, na, nb, NLEN)
        scores = pair_scores(*keys, qq, left) * SCALE
        grad_probs = pair_scores(*values, uu, left)
        log_total = jnp.where(left, sums[0, pl.ds(ga, 1), :], sums[0, pl.ds(gb, 1), :])
        inner = jnp.where(left, sums[1, pl.ds(ga, 1), :], sums[1, pl.ds(gb, 1), :])
        real = left | (b < n)
        prob = jnp.where(real, jnp.exp(scores - log_total), 0.0)
        grad_scores = prob * (grad_probs - inner)
        grad_t = grad_scores.T.astype(BF)
        prob, grad_scores = prob.astype(BF), grad_scores.astype(BF)

        def halves(v):
            return jnp.concatenate([jnp.where(left, v, zero), jnp.where(left, zero, v)], axis=0)

        grad_q = dot(grad_t, jnp.concatenate(keys, axis=1)) * SCALE
        grad_v = dot(halves(prob), uu)
        grad_k = dot(halves(grad_scores), qq) * SCALE
        add_rows(gq, ga, GROUP, grad_q[:GROUP, :HD])
        add_rows(gq, gb, GROUP, grad_q[GROUP:, HD:])
        add_rows(dv, na, NLEN, grad_v[:NLEN])
        add_rows(dv, nb, NLEN, grad_v[NLEN:])
        add_rows(dk, na, NLEN, grad_k[:NLEN])
        add_rows(dk, nb, NLEN, grad_k[NLEN:])
        return carry

    lax.fori_loop(0, (n + 1) // 2, pair, 0)
    for src, dst in ((dk, dkey), (dv, dvalue)):
        rows = 512

        @pl.loop(0, src.shape[0] // rows)
        def _(i, src=src, dst=dst):
            at = pl.ds(pl.multiple_of(i * rows, rows), rows)
            dst[at, :] = src[at, :].astype(BF)


def grads_of_uses(ids, qall, upall, ktab, vtab, sums):
    tokens, rows = qall.shape[0], ktab.shape[0]
    return pl.pallas_call(
        grads_kernel,
        out_shape=(
            jax.ShapeDtypeStruct((tokens, HD), BF),
            jax.ShapeDtypeStruct((rows, HD), BF),
            jax.ShapeDtypeStruct((rows, HD), BF),
        ),
        in_specs=[SMEM] + [VMEM] * 5,
        out_specs=[VMEM] * 3,
        scratch_shapes=[
            pltpu.SMEM((264,), jnp.int32),
            pltpu.SMEM((264,), jnp.int32),
            pltpu.VMEM((rows, HD), F32),
            pltpu.VMEM((rows, HD), F32),
        ],
        compiler_params=pltpu.CompilerParams(vmem_limit_bytes=LIMIT),
        name="grads",
    )(ids, qall, upall, ktab, vtab, sums)


def collect_kernel(
    gq, dkey, dvalue, gq_out, dk_out, dv_out, held, gq_done, send, recv, local
):
    x, z, y, c = place()
    xs = [step_from(x, i, X) for i in range(X)]
    along_z, _ = rings(x, z, y, c)
    enter([device(xs[i], z, y, c) for i in (1, 2, 3)] + list(along_z[2]))
    copies = Copies(send, recv)
    kept, table_in, gq_sent = [], [], []

    def piece(i):
        return Scatter(
            copies,
            lambda way, b: gq.at[b, xs[i]],
            lambda b: gq[b, xs[i]].astype(F32),
            lambda way, s: held.at[i, 4 * way + s],
            HOPS[i % 2],
            along_z,
        )

    grads = [piece(i) for i in range(X)]
    step_all(grads, 0)
    for src, dst in ((dkey, dk_out), (dvalue, dv_out)):
        goal = dst.at[:, columns(x, HD)]
        for i in (1, 3, 2):
            table_in.append(copies.start(src.at[xs[i]], goal, device(xs[i], z, y, c)))
        start_local(local, kept, src.at[x], goal)
    for s in (1, 2, 3):
        step_all(grads, s)
    for i in (1, 2, 3, 0):
        grads[i].step(4)
        gq_done[i] = grads[i].total().astype(BF)
        goal = gq_out.at[:, columns(x, HD)]
        if i == 0:
            start_local(local, kept, gq_done.at[i], goal)
        else:
            gq_sent.append(copies.start(gq_done.at[i], goal, device(xs[i], z, y, c)))
    for copy in table_in + gq_sent:
        copy.wait_recv()
    for copy in kept:
        copy.wait()
    copies.finish()


def collect(gq, dkey, dvalue):
    rows = dkey.shape[1]
    return pl.pallas_call(
        collect_kernel,
        out_shape=(
            jax.ShapeDtypeStruct((TOK, X * HD), BF),
            jax.ShapeDtypeStruct((rows, X * HD), BF),
            jax.ShapeDtypeStruct((rows, X * HD), BF),
        ),
        in_specs=[VMEM] * 3,
        out_specs=[VMEM] * 3,
        scratch_shapes=[
            pltpu.VMEM((X, 8, TOK, HD), BF),
            pltpu.VMEM((X, TOK, HD), BF),
            pltpu.SemaphoreType.DMA((40,)),
            pltpu.SemaphoreType.DMA((40,)),
            pltpu.SemaphoreType.DMA((8,)),
        ],
        compiler_params=pltpu.CompilerParams(
            collective_id=2, has_side_effects=True, vmem_limit_bytes=LIMIT
        ),
        name="collect",
    )(gq, dkey, dvalue)


def shards(queries, keys, values, out_weight, grad_out, neighbour_owner, neighbour_local):
    ids = jnp.stack([neighbour_owner, neighbour_local], axis=-1).reshape(1, -1)
    ids = jnp.pad(ids, ((0, 0), (0, 128 - ids.shape[1])))
    ids, qall, ktab, vtab, wa, gfull = spread(ids, queries, keys, values, out_weight, grad_out)
    qall = qall.reshape(Z * X * TOK, HD)
    ktab, vtab = (a.reshape(X * keys.shape[0], HD) for a in (ktab, vtab))
    logs, ctx = attend(ids, qall, ktab, vtab)
    sums, upall, out = project(logs, ctx.reshape(Z, X, TOK, HD), wa, out_weight, gfull)
    upall = upall.reshape(Z * X * TOK, HD)
    gq, dkey, dvalue = grads_of_uses(ids, qall, upall, ktab, vtab, sums)
    dkey, dvalue = (a.reshape((X,) + keys.shape[:1] + (HD,)) for a in (dkey, dvalue))
    grad_queries, grad_keys, grad_values = collect(gq.reshape(Z, X, TOK, HD), dkey, dvalue)
    return out, grad_queries, grad_keys.astype(F32), grad_values.astype(F32)


def solution(mesh):
    return jax.shard_map(
        shards,
        mesh=mesh,
        in_specs=(
            P("dp", "tensor"),
            P("dp", "tensor"),
            P("dp", "tensor"),
            P("tensor", "dp"),
            P(("dp", "tensor"), None),
            P("dp", None),
            P("dp", None),
        ),
        out_specs=(
            P(("dp", "tensor"), None),
            P("dp", "tensor"),
            P("dp", "tensor"),
            P("dp", "tensor"),
        ),
        check_vma=False,
    )
```

time: 190 us -> 202 us (1.063)
  Pallas kernels: 175 us -> 189 us
    pallas_call x3, Pallas kernels: 91.1 us -> 134 us  [the longest x1 90 us: project(): pl.pallas_call(project_kernel, out_shape=(jax.ShapeDtypeStruct((2,) + log...]
    pallas_call x1, Pallas kernels: 73.5 us -> 45.1 us  [spread(): pl.pallas_call(spread_kernel, out_shape=(jax.ShapeDtypeStruct((Z, X) + id...]
    unnamed x12 -> x14, local copies, waits for them, and re-layouts: 6.88 us -> 6.89 us
where the time goes in v4:
time: 202 us; the launch traced here: 201 us
  Pallas kernels  189 us (94%)
  local copies, waits for them, and re-layouts  7.08 us (4%)
  other arithmetic  3.92 us (2%)
    pallas_call x1, Pallas kernels, project(): pl.pallas_call(project_kernel, out_shape=(jax.ShapeDtypeStruct((2,) + log...  90 us
    pallas_call x1, Pallas kernels, spread(): pl.pallas_call(spread_kernel, out_shape=(jax.ShapeDtypeStruct((Z, X) + id...  45.1 us
    pallas_call x1, Pallas kernels, collect(): pl.pallas_call(collect_kernel, out_shape=(jax.ShapeDtypeStruct((TOK, X *...  31.7 us
    pallas_call x1, Pallas kernels, attend(): pl.pallas_call(attend_kernel, out_shape=(jax.ShapeDtypeStruct((16 * Z, 2...  11.9 us
    pallas_call x1, Pallas kernels, grads_of_uses(): pl.pallas_call(grads_kernel, out_shape=(jax.ShapeDtypeStruct((tokens, HD)...  10.1 us
    unnamed x14, local copies, waits for them, and re-layouts  6.89 us

profile of v4, /device:TPU:6, one launch (start us, length us, event | category | flops | bytes accessed | tf_op | source)
XLA Modules:
  0.0 200.6 jit_solution(8584356770972146193)
XLA Ops:
  0.6 0.7 pad_add_fusion
  1.3 0.1 copy.12
  1.4 0.1 reshape.35
  1.5 0.0 copy-start
  1.5 1.2 copy-done
  2.8 0.0 copy-start.1
  2.8 1.2 copy-done.1
  4.0 0.0 copy-start.2
  4.0 0.9 copy-done.2
  4.9 0.0 copy-start.4
  4.9 1.0 copy-done.4
  6.0 0.0 copy-start.5
  6.0 0.9 copy-done.5
  6.9 45.1 %spread.1 = (s32[8,4,1,128]{3,2,1,0:T(1,128)S(1)}, bf16[8,4,256,128]{3,2,1,0:T(8,128)(2,1)S(1)}, bf16[4,1024,128]{2,1,0:T(8,128)(2,1)S(1)}, bf16[4,1024,128]{2,1...) custom-call(s32[1,128]{1,0:T(1,128)S(1)} %pad.4.ids_ref, ...), custom_call_target="tpu_custom_call" | custom-call | tf_op jit(solution)/shard_map/spread/pallas_call | solution.py:272
  52.1 0.0 copy-start.3
  52.1 11.9 %attend.1 = (f32[128,128]{1,0:T(8,128)S(1)}, bf16[8192,128]{1,0:T(8,128)(2,1)S(1)}) custom-call(s32[8,4,1,128]{3,2,1,0:T(1,128)S(1)} %get-tuple-element.21.ids, bf16[8192,128]{1,0:T(8,128)(2,1)S(1)} %bitcast.10, bf16[4096,128]{1,0:T(8,128)(2,1)S(1)} %bitcast.12, bf16[4096,128]{1,0:T(8,128)(2,1)S(1)} %bitcast.14), custom_call_target="tpu_custom_call" | custom-call | tf_op jit(solution)/shard_map/attend/pallas_call | solution.py:391
  64.0 0.0 copy-done.3
  64.0 90.0 %project.1 = (f32[2,128,128]{2,1,0:T(8,128)S(1)}, bf16[8,4,256,128]{3,2,1,0:T(8,128)(2,1)S(1)}, bf16[32,8192]{1,0:T(8,128)(2,1)S(1)}) custom-call(f32[128,128]{1,0:T(8,128)S(1)} %get-tuple-element.25.logs, bf16[8,4,256,128]{3,2,1,0:T(8,128)(2,1)S(1)} %bitcast.18, bf16[256,2048]{1,0:T(8,128)(2,1)S(1)} %get-tuple-element.27.wa, ...), custom_call_target="tpu_custom_call" | custom-call | tf_op jit(solution)/shard_map/project/pallas_call | solution.py:665
  154.0 10.1 %grads.1 = (bf16[8192,128]{1,0:T(8,128)(2,1)S(1)}, bf16[4096,128]{1,0:T(8,128)(2,1)S(1)}, bf16[4096,128]{1,0:T(8,128)(2,1)S(1)}) custom-call(s32[8,4,1,128]{3,2,1,0:T(1,128)S(1)} %get-tuple-element.21.ids, bf16[8192,128]{1,0:T(8,128)(2,1)S(1)} %bitcast.11, bf16[8192,128]{1,0:T(8,128)(2,1)S(1)} %bitcast.16, bf16[4096,128]{1,0:T(8,128)(2,1)S(1)} %bitcast.13, ...), custom_call_target="tpu_custom_call" | custom-call | tf_op jit(solution)/shard_map/grads/pallas_call | solution.py:756
  164.1 31.7 %collect.1 = (bf16[256,512]{1,0:T(8,128)(2,1)S(1)}, bf16[1024,512]{1,0:T(8,128)(2,1)S(1)}, bf16[1024,512]{1,0:T(8,128)(2,1)S(1)}) custom-call(bf16[8,4,256,128]{3,2,1,0:T(8,128)(2,1)S(1)} %bitcast.17, bf16[4,1024,128]{2,1,0:T(8,128)(2,1)S(1)} %bitcast.19, bf16[4,1024,128]{2,1,0:T(8,128)(2,1)S(1)} %bitcast.20), custom_call_target="tpu_custom_call" | custom-call | tf_op jit(solution)/shard_map/collect/pallas_call | solution.py:822
  195.9 1.6 convert_element_type.6
  197.5 1.6 convert_element_type.7
  199.1 0.8 copy.15
  199.9 0.7 copy.16
  (1 shorter events, 0.0 us)
Async XLA Ops:
  1.5 1.2 copy-start
  2.8 1.2 copy-start.1
  4.0 0.9 copy-start.2
  4.9 1.0 copy-start.4
  6.0 0.9 copy-start.5
  52.1 11.9 %copy-start.3 = (bf16[512,256]{1,0:T(8,128)(2,1)S(1)}, bf16[512,256]{1,0:T(8,128)(2,1)}, u32[]{:S(2)}) copy-start(bf16[512,256]{1,0:T(8,128)(2,1)} %w_ref.3) | copy-start | bytes 786436

commit v5 on v4

--- a/solution.py
+++ b/solution.py
@@ -1,5 +1,3 @@
-import functools
-
 import jax
 import jax.numpy as jnp
 from jax import lax
@@ -21,6 +19,7 @@
 SMEM = pl.BlockSpec(memory_space=pltpu.SMEM)
 HBM = pl.BlockSpec(memory_space=pltpu.HBM)
 LIMIT = 28 * 1024 * 1024
+PAIRS, GRAD_PAIRS = 8, 4
 
 
 def place():
@@ -97,8 +96,8 @@
 
 
 class Scatter:
-    def __init__(self, copies, first, value, held, hops, ring):
-        self.copies, self.first, self.value, self.held, self.hops = copies, first, value, held, hops
+    def __init__(self, copies, first, join, held, hops, ring):
+        self.copies, self.first, self.join, self.held, self.hops = copies, first, join, held, hops
         self.place, self.size, self.sides = ring
         self.sent = [[], []]
 
@@ -113,13 +112,25 @@
                     src = self.first(way, goal)
                 else:
                     src = self.held(way, s - 1)
-                    src[...] = (src[...].astype(F32) + self.value(goal)).astype(BF)
+                    self.join(src, goal)
                 self.sent[way].append(self.copies.start(src, self.held(way, s), self.sides[way]))
 
+    def arrived(self):
+        return [self.held(way, self.hops[way] - 1) for way in (0, 1)]
+
+
+class Sum(Scatter):
+    def __init__(self, copies, part, held, hops, ring):
+        def join(ref, goal):
+            ref[...] = (ref[...].astype(F32) + part(goal)[...].astype(F32)).astype(BF)
+
+        super().__init__(copies, lambda way, b: part(b), join, held, hops, ring)
+        self.part = part
+
     def total(self):
-        total = self.value(self.place)
-        for way in (0, 1):
-            total += self.held(way, self.hops[way] - 1)[...].astype(F32)
+        total = self.part(self.place)[...].astype(F32)
+        for ref in self.arrived():
+            total += ref[...].astype(F32)
         return total
 
 
@@ -142,14 +153,6 @@
 def step_all(pieces, s):
     for one in pieces:
         one.step(s)
-
-
-def weight_piece(copies, first, wf, width, i, along_z):
-    depth = wf.shape[0] // 2
-    rows = pl.ds(i * depth, depth)
-    return Gather(
-        copies, first, lambda b: wf.at[rows, columns(b, width)], HOPS[i % 2], along_z
-    )
 
 
 def spread_kernel(
@@ -182,10 +185,13 @@
     def piece(ref, i):
         return Gather(copies, ref.at[z, i], lambda b: ref.at[b, i], HOPS[i % 2], along_z)
 
-    weights = [
-        weight_piece(copies, w_ref.at[pl.ds(i * depth, depth)], wf, width, i, along_z)
-        for i in range(2)
-    ]
+    def weight_piece(i):
+        rows = pl.ds(i * depth, depth)
+        return Gather(
+            copies, w_ref.at[rows], lambda b: wf.at[rows, columns(b, width)], HOPS[i % 2], along_z
+        )
+
+    weights = [weight_piece(i) for i in range(4)]
     asked = [piece(qall, i) for i in range(X)]
     asked.append(Gather(copies, idall.at[z], lambda b: idall.at[b], HOPS[0], along_z))
 
@@ -227,10 +233,9 @@
     keep(q_ref.at[:, columns(x, HD)], qall.at[z, x])
     keep(ids_ref, idall.at[z, x])
     keep(g_ref.at[:, columns(x, span)], gfull.at[x, t])
-    keep(w_ref.at[pl.ds(0, 2 * depth)], wf.at[:, columns(z, width)])
+    keep(w_ref, wf.at[:, columns(z, width)])
     keep(k_ref.at[:, columns(x, HD)], ktab.at[x])
     keep(v_ref.at[:, columns(x, HD)], vtab.at[x])
-    step_all(weights, 1)
     for copy in q_in:
         copy.wait_recv()
     for copy in kept[:2]:
@@ -238,23 +243,24 @@
     step_all(asked, 0)
     send_table(k_ref, ktab)
     send_table(v_ref, vtab)
-    step_all(weights, 2)
+    step_all(weights, 1)
     kept[2].wait()
     for copy in g_in:
         copy.wait_recv()
     send_rows(0)
     send_rows(1)
     step_all(asked, 1)
-    step_all(weights, 3)
     step_all(rows[:2], 1)
     send_rows(2)
     send_rows(3)
+    step_all(weights, 2)
+    step_all(rows[:2], 2)
     step_all(asked, 2)
-    step_all(rows[:2], 2)
+    step_all(rows[2:], 1)
+    step_all(weights, 3)
+    step_all(rows[2:], 2)
+    step_all(asked, 3)
     step_all(weights, 4)
-    step_all(asked, 3)
-    step_all(rows[2:], 1)
-    step_all(rows[2:], 2)
     step_all(asked, 4)
     for i in range(X):
         for copy in g_core[i]:
@@ -276,14 +282,14 @@
             jax.ShapeDtypeStruct((Z, X, TOK, HD), BF),
             jax.ShapeDtypeStruct((X, rows, HD), BF),
             jax.ShapeDtypeStruct((X, rows, HD), BF),
-            jax.ShapeDtypeStruct((depth // 2, Z * width), BF),
+            jax.ShapeDtypeStruct((depth, Z * width), BF),
             jax.ShapeDtypeStruct((X, Y * C, grad_out.shape[0], Z * width), BF),
         ),
         in_specs=[VMEM] + [HBM] * 5,
         out_specs=[VMEM] * 6,
         scratch_shapes=[
-            pltpu.SemaphoreType.DMA((96,)),
-            pltpu.SemaphoreType.DMA((96,)),
+            pltpu.SemaphoreType.DMA((112,)),
+            pltpu.SemaphoreType.DMA((112,)),
             pltpu.SemaphoreType.DMA((8,)),
         ],
         compiler_params=pltpu.CompilerParams(
@@ -293,21 +299,42 @@
     )(ids, queries, keys, values, out_weight, grad_out)
 
 
-def list_uses(ids, groups, names):
+TAIL = 16
+LISTED = 256 + 32
+
+
+def list_uses(ids, uses):
     z = lax.rem(lax.axis_index("dp"), Z)
 
     def add(i, n):
         dp_z, dp_x = lax.shift_right_logical(i, 5), lax.shift_right_logical(i, 3) & 3
         owner, name = (ids[dp_z, dp_x, 0, 2 * (i & 7) + j] for j in (0, 1))
-        groups[n] = lax.shift_right_logical(i, 1)
-        names[n] = lax.shift_right_logical(owner, 3) * NB_DEV + name
+        uses[n] = lax.shift_right_logical(i, 1)
+        uses[LISTED + n] = lax.shift_right_logical(owner, 3) * NB_DEV + name
         return n + ((owner & 7) == z).astype(jnp.int32)
 
     n = lax.fori_loop(0, X * Z * 8, add, jnp.int32(0), unroll=8)
     last = jnp.maximum(n - 1, 0)
-    groups[n] = groups[last]
-    names[n] = names[last]
+    for i in range(2 * PAIRS - 1):
+        uses[n + i] = uses[last]
+        uses[LISTED + n + i] = uses[LISTED + last]
+    uses[2 * LISTED] = n
     return n
+
+
+def uses_at(uses, p, n, pairs):
+    lane = lax.broadcasted_iota(jnp.int32, (1, 2 * GROUP), 1)
+    out = []
+    for i in range(pairs):
+        a = 2 * (pairs * p + i)
+        b = a + 1
+        real = jnp.where(lane < GROUP, a, b) < n
+        out.append((uses[a], uses[b], uses[LISTED + a], uses[LISTED + b], real))
+    return out
+
+
+def turns(n, pairs):
+    return lax.div(n + (2 * pairs - 1), 2 * pairs)
 
 
 def pair_rows(ref, a, b, size):
@@ -340,8 +367,8 @@
     ref[at, :] = (ref[at, :].astype(F32) + value).astype(ref.dtype)
 
 
-def attend_kernel(ids, qall, ktab, vtab, logs, ctx, groups, names, stats):
-    n = list_uses(ids, groups, names)
+def attend_kernel(ids, qall, ktab, vtab, logs, ctx, uses, stats):
+    n = list_uses(ids, uses)
     stats[0] = jnp.full(stats.shape[1:], LOW, F32)
     stats[1] = jnp.zeros(stats.shape[1:], F32)
     clear(ctx)
@@ -352,39 +379,46 @@
         return pair_scores(*pair_rows(ktab, na, nb, NLEN), qq, left) * SCALE
 
     def measure(p, carry):
-        a, b = 2 * p, 2 * p + 1
-        ga, gb, na, nb = groups[a], groups[b], names[a], names[b]
-        scores = scores_of(ga, gb, na, nb)
-        peak = jnp.max(scores, axis=0, keepdims=True)
-        total = jnp.sum(jnp.exp(scores - peak), axis=0, keepdims=True)
-        real = left | (b < n)
-        new = jnp.where(real, peak, LOW), jnp.where(real, total, 0.0)
-        for g, mine in ((ga, left), (gb, jnp.logical_not(left))):
-            old = tuple(stats[i, pl.ds(g, 1), :] for i in range(2))
-            merged = merge(old, new)
-            for i in range(2):
-                stats[i, pl.ds(g, 1), :] = jnp.where(mine, merged[i], old[i])
+        pairs = uses_at(uses, p, n, PAIRS)
+        found = []
+        for ga, gb, na, nb, real in pairs:
+            scores = scores_of(ga, gb, na, nb)
+            peak = jnp.max(scores, axis=0, keepdims=True)
+            total = jnp.sum(jnp.exp(scores - peak), axis=0, keepdims=True)
+            found.append((jnp.where(real, peak, LOW), jnp.where(real, total, 0.0)))
+        for (ga, gb, *_), new in zip(pairs, found):
+            for g, mine in ((ga, left), (gb, jnp.logical_not(left))):
+                old = tuple(stats[i, pl.ds(g, 1), :] for i in range(2))
+                merged = merge(old, new)
+                for i in range(2):
+                    stats[i, pl.ds(g, 1), :] = jnp.where(mine, merged[i], old[i])
         return carry
 
     def weigh(p, carry):
-        a, b = 2 * p, 2 * p + 1
-        ga, gb, na, nb = groups[a], groups[b], names[a], names[b]
-        scores = scores_of(ga, gb, na, nb)
-        log_total = jnp.where(left, logs[pl.ds(ga, 1), :], logs[pl.ds(gb, 1), :])
-        prob = jnp.where(left | (b < n), jnp.exp(scores - log_total), 0.0)
-        values = pair_rows(vtab, na, nb, NLEN)
-        context = jnp.dot(
-            prob.T.astype(BF), jnp.concatenate(values, axis=1), preferred_element_type=F32
-        )
-        add_rows(ctx, ga, GROUP, context[:GROUP, :HD])
-        add_rows(ctx, gb, GROUP, context[GROUP:, HD:])
+        pairs = uses_at(uses, p, n, PAIRS)
+        found = []
+        for ga, gb, na, nb, real in pairs:
+            scores = scores_of(ga, gb, na, nb)
+            log_total = jnp.where(left, logs[pl.ds(ga, 1), :], logs[pl.ds(gb, 1), :])
+            prob = jnp.where(real, jnp.exp(scores - log_total), 0.0)
+            values = pair_rows(vtab, na, nb, NLEN)
+            found.append(
+                jnp.dot(
+                    prob.T.astype(BF),
+                    jnp.concatenate(values, axis=1),
+                    preferred_element_type=F32,
+                )
+            )
+        for (ga, gb, *_), context in zip(pairs, found):
+            add_rows(ctx, ga, GROUP, context[:GROUP, :HD])
+            add_rows(ctx, gb, GROUP, context[GROUP:, HD:])
         return carry
 
-    lax.fori_loop(0, (n + 1) // 2, measure, 0)
+    lax.fori_loop(0, turns(n, PAIRS), measure, 0)
     state = stats[0], stats[1]
     peak, total = merge(state, tuple(pltpu.roll(v, GROUP, 1) for v in state))
     logs[...] = jnp.where(total > 0.0, peak + jnp.log(jnp.maximum(total, 1e-30)), LOW)
-    lax.fori_loop(0, (n + 1) // 2, weigh, 0)
+    lax.fori_loop(0, turns(n, PAIRS), weigh, 0)
 
 
 def attend(ids, qall, ktab, vtab):
@@ -393,12 +427,11 @@
         out_shape=(
             jax.ShapeDtypeStruct((16 * Z, 2 * GROUP), F32),
             jax.ShapeDtypeStruct(qall.shape, BF),
+            jax.ShapeDtypeStruct((2 * LISTED + 64,), jnp.int32),
         ),
         in_specs=[SMEM] + [VMEM] * 3,
-        out_specs=[VMEM] * 2,
+        out_specs=[VMEM] * 2 + [SMEM],
         scratch_shapes=[
-            pltpu.SMEM((264,), jnp.int32),
-            pltpu.SMEM((264,), jnp.int32),
             pltpu.VMEM((2, 16 * Z, 2 * GROUP), F32),
         ],
         compiler_params=pltpu.CompilerParams(vmem_limit_bytes=LIMIT),
@@ -407,16 +440,13 @@
 
 
 def project_kernel(
-    logs, ctx, wa, w_ref, gfull,
+    logs, ctx, wf, gfull,
     sums, upall, out,
-    wb, wo, logs_in, upp, upr, staged, held, ctx4, ctx_other, part, y_held, done,
+    wf_other, upp, upr, staged, held, ctx4, ctx_other, part, y_held, done,
     send, recv, out_send, out_recv, local,
 ):
     x, z, y, c = place()
-    half, span = wa.shape
-    width = w_ref.shape[1]
-    depth = half // 2
-    head_cols = 2 * half
+    head_cols, span = wf.shape
     slots = TOK // (Y * C)
     xs = [step_from(x, i, X) for i in range(X)]
     zs = [step_from(z, i, Z) for i in range(Z)]
@@ -430,35 +460,17 @@
         + [sibling]
     )
     copies = Copies(send, recv)
-    kept = []
     left = lax.broadcasted_iota(jnp.int32, (1, 2 * GROUP), 1) < GROUP
     own = pl.ds(pl.multiple_of(z * 16, 16), 16)
     up_in, ctx_in, core_in = {}, {}, {}
 
-    def tell(ref):
-        return [copies.start(ref, ref, device(x, zs[i], y, c)) for i in order]
-
-    def send_logs():
-        return [
-            copies.start(logs.at[columns(zs[i], 16)], logs_in.at[i - 1], device(x, zs[i], y, c))
-            for i in order
-        ]
-
-    def merge_logs():
-        parts = [logs[own, :]] + [logs_in[i] for i in range(Z - 1)]
-        peak = functools.reduce(jnp.maximum, parts)
-        total = sum(jnp.exp(v - peak) for v in parts)
-        sums[0, own, :] = peak + jnp.log(total)
-
-    def multiply_rows(i, w, at):
-        upp[i, :, at] = lax.dot_general(
+    def multiply_rows(i):
+        upp[i] = lax.dot_general(
             gfull[i].reshape(TOK, span),
-            w[...],
+            wf[...],
             (((1,), (1,)), ((), ())),
             preferred_element_type=F32,
         ).astype(BF)
-
-    def send_up(i):
         up_in[i] = [
             copies.start(
                 upp.at[i, :, columns(xs[j], HD)], upr.at[i, j - 1], device(xs[j], z, y, c)
@@ -475,43 +487,65 @@
         upall[z, i] = value.astype(BF)
         upstream[i].step(0)
 
-    def scaled(b, i):
+    def mine(b, i):
+        rows = [logs[pl.ds(b * 16 + i * 4 + j, 1), :] for j in range(4)]
+        return ctx[b, i].astype(F32), [jnp.where(left, *rows[j : j + 2]) for j in (0, 2)]
+
+    def write(ref, state):
+        ref[:TOK] = state[0].astype(BF)
         rows = []
+        for rest in state[1]:
+            for _ in range(3):
+                rows.append(rest.astype(BF).astype(F32))
+                rest = rest - rows[-1]
+        rows.append(jnp.zeros((TAIL - len(rows), HD), F32))
+        ref[TOK:] = jnp.concatenate(rows, axis=0).astype(BF)
+
+    def read(ref):
+        rows = ref[TOK:].astype(F32)
+        sums_of = [rows[3 * j : 3 * j + 1] + rows[3 * j + 1 : 3 * j + 2] for j in range(2)]
+        return ref[:TOK].astype(F32), [v + rows[3 * j + 2 : 3 * j + 3] for j, v in enumerate(sums_of)]
+
+    def joined(one, two):
+        blocks, log_sums = [], []
         for j in range(2):
-            at = [pl.ds(b * 16 + i * 4 + 2 * j + k, 1) for k in (0, 1)]
-            factor = [jnp.exp(logs[r, :] - sums[0, r, :]) for r in at]
-            factor = jnp.broadcast_to(jnp.where(left, *factor), (2 * GROUP, HD))
-            rows.append(factor.T)
-        return jnp.concatenate(rows, axis=0) * ctx[b, i].astype(F32)
+            peak = jnp.maximum(one[1][j], two[1][j])
+            log_sum = peak + jnp.log(jnp.exp(one[1][j] - peak) + jnp.exp(two[1][j] - peak))
+            block = 0.0
+            for context, logs_of in (one, two):
+                factor = jnp.broadcast_to(jnp.exp(logs_of[j] - log_sum), (2 * GROUP, HD)).T
+                block += factor * context[j * 2 * GROUP : (j + 1) * 2 * GROUP]
+            blocks.append(block)
+            log_sums.append(log_sum)
+        return jnp.concatenate(blocks, axis=0), log_sums
+
+    def both_halves(at, row):
+        turned = pltpu.roll(row, GROUP, 1)
+        return (at, jnp.where(left, row, turned)), (at + 1, jnp.where(left, turned, row))
 
     def context_piece(i):
         def first(way, b):
-            staged[i, way] = scaled(b, i).astype(BF)
+            write(staged.at[i, way], mine(b, i))
             return staged.at[i, way]
 
         return Scatter(
             copies,
             first,
-            lambda b: scaled(b, i),
+            lambda ref, b: write(ref, joined(read(ref), mine(b, i))),
             lambda way, s: held.at[i, 4 * way + s],
             HOPS[i % 2],
             along_z,
         )
 
     def out_piece(i):
-        return Scatter(
+        return Sum(
             copies,
-            lambda way, b: part.at[i, b],
-            lambda b: part[i, b].astype(F32),
+            lambda b: part.at[i, b],
             lambda way, s: y_held.at[i, 2 * way + s],
             HOPS_Y[i % 2],
             along_y,
         )
 
-    weights = [
-        weight_piece(copies, w_ref.at[pl.ds(half + i * depth, depth)], wb, width, i, along_z)
-        for i in range(2)
-    ]
     contexts = [context_piece(i) for i in range(X)]
     outs = [out_piece(i) for i in range(X)]
     upstream = [
@@ -520,21 +554,28 @@
     ]
 
     def share(i):
-        context = contexts[i].total().astype(BF)
-        mine = ctx4.at[i, :, :, :, columns(x, HD)]
-        mine[...] = context.reshape(Y, C, slots, HD)
-        ctx_in[i] = [copies.start(mine, mine, device(xs[j], z, y, c)) for j in (1, 3, 2)]
+        state = mine(z, i)
+        for ref in contexts[i].arrived():
+            state = joined(state, read(ref))
+        at = ctx4.at[i, :, :, :, columns(x, HD)]
+        at[...] = state[0].astype(BF).reshape(Y, C, slots, HD)
+        ctx_in[i] = [copies.start(at, at, device(xs[j], z, y, c)) for j in (1, 3, 2)]
+        for j in range(2):
+            for row, value in both_halves(z * 16 + i * 4 + 2 * j, state[1][j]):
+                sums[0, pl.ds(row, 1), :] = value
 
     def inner(i):
         context = ctx4[i, :, :, :, columns(x, HD)].reshape(TOK, HD)
         product = upall[z, i].astype(F32) * context.astype(F32)
         for j in range(2):
             rows = product[j * 2 * GROUP : (j + 1) * 2 * GROUP]
-            row = jnp.sum(rows.T, axis=0, keepdims=True)
-            turned = pltpu.roll(row, GROUP, 1)
-            at = z * 16 + i * 4 + 2 * j
-            sums[1, pl.ds(at, 1), :] = jnp.where(left, row, turned)
-            sums[1, pl.ds(at + 1, 1), :] = jnp.where(left, turned, row)
+            total = jnp.sum(rows.T, axis=0, keepdims=True)
+            for row, value in both_halves(z * 16 + i * 4 + 2 * j, total):
+                sums[1, pl.ds(row, 1), :] = value
+
+    def tell():
+        ref = sums.at[:, own]
+        return [copies.start(ref, ref, device(x, zs[i], y, c)) for i in order]
 
     def swap(i):
         for copy in ctx_in[i]:
@@ -543,16 +584,12 @@
 
     def multiply(i):
         core_in[i].wait_recv()
-        terms = (
-            (ctx4[i, :, c].reshape(Y * slots, head_cols), wa, wb),
-            (ctx_other[i].reshape(Y * slots, head_cols), wo.at[0], wo.at[1]),
-        )
+        mine = ctx4[i, :, c].reshape(Y * slots, head_cols)
+        others = ctx_other[i].reshape(Y * slots, head_cols)
         for j in range(2):
             cols = pl.ds(j * (span // 2), span // 2)
-            product = 0.0
-            for rows, first, second in terms:
-                product += jnp.dot(rows[:, :half], first[:, cols], preferred_element_type=F32)
-                product += jnp.dot(rows[:, half:], second[:, cols], preferred_element_type=F32)
+            product = jnp.dot(mine, wf[:, cols], preferred_element_type=F32)
+            product += jnp.dot(others, wf_other[:, cols], preferred_element_type=F32)
             part[i, :, :, cols] = product.astype(BF).reshape(Y, slots, span // 2)
         outs[i].step(0)
 
@@ -579,71 +616,43 @@
                 device_id_type=pl.DeviceIdType.MESH,
             ).start()
 
-    logs_sent = send_logs()
-    step_all(weights, 0)
-    wa_in = copies.start(wa, wo.at[0], sibling)
-    start_local(local, kept, w_ref.at[pl.ds(half, half)], wb.at[:, columns(z, width)])
-    multiply_rows(0, wa, pl.ds(0, half))
-    multiply_rows(1, wa, pl.ds(0, half))
-    step_all(weights, 1)
-    for copy in logs_sent:
-        copy.wait_recv()
-    merge_logs()
-    logs_back = tell(sums.at[0, own])
-    multiply_rows(2, wa, pl.ds(0, half))
-    multiply_rows(3, wa, pl.ds(0, half))
-    step_all(weights, 2)
-    step_all(weights, 3)
-    for copy in logs_back:
-        copy.wait_recv()
     step_all(contexts, 0)
-    step_all(weights, 4)
-    kept[0].wait()
-    wb_in = copies.start(wb, wo.at[1], sibling)
-    multiply_rows(0, wb, pl.ds(half, half))
-    send_up(0)
-    step_all(contexts[:2], 1)
-    multiply_rows(1, wb, pl.ds(half, half))
-    send_up(1)
-    step_all(contexts[2:], 1)
-    multiply_rows(2, wb, pl.ds(half, half))
-    send_up(2)
-    step_all(contexts[:2], 2)
-    multiply_rows(3, wb, pl.ds(half, half))
-    send_up(3)
-    step_all(contexts[2:], 2)
-    step_all(contexts, 3)
-    total_up(0)
-    total_up(1)
+    weight_in = copies.start(wf, wf_other, sibling)
+    for i in range(X):
+        multiply_rows(i)
+    for s in (1, 2, 3):
+        step_all(contexts, s)
+    for i in range(X):
+        total_up(i)
     for i in range(X):
         contexts[i].step(4)
         share(i)
-    total_up(2)
-    total_up(3)
-    wa_in.wait_recv()
-    wb_in.wait_recv()
+    weight_in.wait_recv()
+    step_all(upstream[:2], 1)
     swap(0)
-    step_all(upstream, 1)
     multiply(0)
+    step_all(upstream[2:], 1)
     swap(1)
+    multiply(1)
+    step_all(upstream[:2], 2)
+    swap(2)
+    multiply(2)
+    step_all(upstream[2:], 2)
+    swap(3)
+    step_all(outs[:1], 1)
+    multiply(3)
     for i in range(X):
         inner(i)
-    inner_back = tell(sums.at[1, own])
-    multiply(1)
-    swap(2)
-    step_all(upstream, 2)
-    multiply(2)
-    swap(3)
-    multiply(3)
-    step_all(outs[:2], 1)
+    told = tell()
+    step_all(outs[1:2], 1)
     step_all(upstream, 3)
+    step_all(outs[2:], 1)
     finish_out(0)
     finish_out(1)
-    step_all(outs[2:], 1)
     step_all(upstream, 4)
     finish_out(2)
     finish_out(3)
-    for copy in inner_back:
+    for copy in told:
         copy.wait_recv()
     for i in (1, 2, 3):
         copy = pltpu.make_async_remote_copy(
@@ -659,8 +668,8 @@
     copies.finish()
 
 
-def project(logs, ctx, wa, out_weight, gfull):
-    half, span = wa.shape
+def project(logs, ctx, wf, gfull):
+    head_cols, span = wf.shape
     slots = TOK // (Y * C)
     return pl.pallas_call(
         project_kernel,
@@ -669,18 +678,16 @@
             jax.ShapeDtypeStruct(ctx.shape, BF),
             jax.ShapeDtypeStruct((slots, X * span), BF),
         ),
-        in_specs=[VMEM] * 3 + [HBM] + [VMEM],
+        in_specs=[VMEM] * 4,
         out_specs=[VMEM] * 3,
         scratch_shapes=[
-            pltpu.VMEM((half, span), BF),
-            pltpu.VMEM((2, half, span), BF),
-            pltpu.VMEM((Z - 1, 16, 2 * GROUP), F32),
-            pltpu.VMEM((X, TOK, 2 * half), BF),
+            pltpu.VMEM((head_cols, span), BF),
+            pltpu.VMEM((X, TOK, head_cols), BF),
             pltpu.VMEM((X, X - 1, TOK, HD), BF),
-            pltpu.VMEM((X, 2, TOK, HD), BF),
-            pltpu.VMEM((X, 8, TOK, HD), BF),
-            pltpu.VMEM((X, Y, C, slots, 2 * half), BF),
-            pltpu.VMEM((X, Y, slots, 2 * half), BF),
+            pltpu.VMEM((X, 2, TOK + TAIL, HD), BF),
+            pltpu.VMEM((X, 8, TOK + TAIL, HD), BF),
+            pltpu.VMEM((X, Y, C, slots, head_cols), BF),
+            pltpu.VMEM((X, Y, slots, head_cols), BF),
             pltpu.VMEM((X, Y, slots, span), BF),
             pltpu.VMEM((X, 4, slots, span), BF),
             pltpu.VMEM((X, slots, span), BF),
@@ -694,13 +701,11 @@
             collective_id=1, has_side_effects=True, vmem_limit_bytes=LIMIT
         ),
         name="project",
-    )(logs, ctx, wa, out_weight, gfull)
-
-
-def grads_kernel(
-    ids, qall, upall, ktab, vtab, sums, gq, dkey, dvalue, groups, names, dk, dv
-):
-    n = list_uses(ids, groups, names)
+    )(logs, ctx, wf, gfull)
+
+
+def grads_kernel(uses, qall, upall, ktab, vtab, sums, gq, dkey, dvalue, dk, dv):
+    n = uses[2 * LISTED]
     for ref in (gq, dk, dv):
         clear(ref)
 
@@ -710,38 +715,38 @@
     def dot(a, b):
         return jnp.dot(a, b, preferred_element_type=F32)
 
-    def pair(p, carry):
-        a, b = 2 * p, 2 * p + 1
-        ga, gb, na, nb = groups[a], groups[b], names[a], names[b]
-        qq = jnp.concatenate(pair_rows(qall, ga, gb, GROUP), axis=0)
-        uu = jnp.concatenate(pair_rows(upall, ga, gb, GROUP), axis=0)
-        keys = pair_rows(ktab, na, nb, NLEN)
-        values = pair_rows(vtab, na, nb, NLEN)
-        scores = pair_scores(*keys, qq, left) * SCALE
-        grad_probs = pair_scores(*values, uu, left)
-        log_total = jnp.where(left, sums[0, pl.ds(ga, 1), :], sums[0, pl.ds(gb, 1), :])
-        inner = jnp.where(left, sums[1, pl.ds(ga, 1), :], sums[1, pl.ds(gb, 1), :])
-        real = left | (b < n)
-        prob = jnp.where(real, jnp.exp(scores - log_total), 0.0)
-        grad_scores = prob * (grad_probs - inner)
-        grad_t = grad_scores.T.astype(BF)
-        prob, grad_scores = prob.astype(BF), grad_scores.astype(BF)
-
-        def halves(v):
-            return jnp.concatenate([jnp.where(left, v, zero), jnp.where(left, zero, v)], axis=0)
-
-        grad_q = dot(grad_t, jnp.concatenate(keys, axis=1)) * SCALE
-        grad_v = dot(halves(prob), uu)
-        grad_k = dot(halves(grad_scores), qq) * SCALE
-        add_rows(gq, ga, GROUP, grad_q[:GROUP, :HD])
-        add_rows(gq, gb, GROUP, grad_q[GROUP:, HD:])
-        add_rows(dv, na, NLEN, grad_v[:NLEN])
-        add_rows(dv, nb, NLEN, grad_v[NLEN:])
-        add_rows(dk, na, NLEN, grad_k[:NLEN])
-        add_rows(dk, nb, NLEN, grad_k[NLEN:])
+    def some(p, carry):
+        pairs = uses_at(uses, p, n, GRAD_PAIRS)
+        found = []
+        for ga, gb, na, nb, real in pairs:
+            qq = jnp.concatenate(pair_rows(qall, ga, gb, GROUP), axis=0)
+            uu = jnp.concatenate(pair_rows(upall, ga, gb, GROUP), axis=0)
+            keys = pair_rows(ktab, na, nb, NLEN)
+            values = pair_rows(vtab, na, nb, NLEN)
+            scores = pair_scores(*keys, qq, left) * SCALE
+            grad_probs = pair_scores(*values, uu, left)
+            log_total = jnp.where(left, sums[0, pl.ds(ga, 1), :], sums[0, pl.ds(gb, 1), :])
+            inner = jnp.where(left, sums[1, pl.ds(ga, 1), :], sums[1, pl.ds(gb, 1), :])
+            prob = jnp.where(real, jnp.exp(scores - log_total), 0.0)
+            grad_scores = prob * (grad_probs - inner)
+            grad_t = grad_scores.T.astype(BF)
+            grad_q = dot(grad_t, jnp.concatenate(keys, axis=1)) * SCALE
+            grad_v = dot(halves(prob.astype(BF)), uu)
+            grad_k = dot(halves(grad_scores.astype(BF)), qq) * SCALE
+            found.append((grad_q, grad_v, grad_k))
+        for (ga, gb, na, nb, _), (grad_q, grad_v, grad_k) in zip(pairs, found):
+            add_rows(gq, ga, GROUP, grad_q[:GROUP, :HD])
+            add_rows(gq, gb, GROUP, grad_q[GROUP:, HD:])
+            add_rows(dv, na, NLEN, grad_v[:NLEN])
+            add_rows(dv, nb, NLEN, grad_v[NLEN:])
+            add_rows(dk, na, NLEN, grad_k[:NLEN])
+            add_rows(dk, nb, NLEN, grad_k[NLEN:])
         return carry
 
-    lax.fori_loop(0, (n + 1) // 2, pair, 0)
+    def halves(v):
+        return jnp.concatenate([jnp.where(left, v, zero), jnp.where(left, zero, v)], axis=0)
+
+    lax.fori_loop(0, turns(n, GRAD_PAIRS), some, 0)
     for src, dst in ((dk, dkey), (dv, dvalue)):
         rows = 512
 
@@ -751,7 +756,7 @@
             dst[at, :] = src[at, :].astype(BF)
 
 
-def grads_of_uses(ids, qall, upall, ktab, vtab, sums):
+def grads_of_uses(uses, qall, upall, ktab, vtab, sums):
     tokens, rows = qall.shape[0], ktab.shape[0]
     return pl.pallas_call(
         grads_kernel,
@@ -763,14 +768,12 @@
         in_specs=[SMEM] + [VMEM] * 5,
         out_specs=[VMEM] * 3,
         scratch_shapes=[
-            pltpu.SMEM((264,), jnp.int32),
-            pltpu.SMEM((264,), jnp.int32),
             pltpu.VMEM((rows, HD), F32),
             pltpu.VMEM((rows, HD), F32),
         ],
         compiler_params=pltpu.CompilerParams(vmem_limit_bytes=LIMIT),
         name="grads",
-    )(ids, qall, upall, ktab, vtab, sums)
+    )(uses, qall, upall, ktab, vtab, sums)
 
 
 def collect_kernel(
@@ -784,10 +787,9 @@
     kept, table_in, gq_sent = [], [], []
 
     def piece(i):
-        return Scatter(
+        return Sum(
             copies,
-            lambda way, b: gq.at[b, xs[i]],
-            lambda b: gq[b, xs[i]].astype(F32),
+            lambda b: gq.at[b, xs[i]],
             lambda way, s: held.at[i, 4 * way + s],
             HOPS[i % 2],
             along_z,
@@ -845,13 +847,13 @@
 def shards(queries, keys, values, out_weight, grad_out, neighbour_owner, neighbour_local):
     ids = jnp.stack([neighbour_owner, neighbour_local], axis=-1).reshape(1, -1)
     ids = jnp.pad(ids, ((0, 0), (0, 128 - ids.shape[1])))
-    ids, qall, ktab, vtab, wa, gfull = spread(ids, queries, keys, values, out_weight, grad_out)
+    ids, qall, ktab, vtab, wf, gfull = spread(ids, queries, keys, values, out_weight, grad_out)
     qall = qall.reshape(Z * X * TOK, HD)
     ktab, vtab = (a.reshape(X * keys.shape[0], HD) for a in (ktab, vtab))
-    logs, ctx = attend(ids, qall, ktab, vtab)
-    sums, upall, out = project(logs, ctx.reshape(Z, X, TOK, HD), wa, out_weight, gfull)
+    logs, ctx, uses = attend(ids, qall, ktab, vtab)
+    sums, upall, out = project(logs, ctx.reshape(Z, X, TOK, HD), wf, gfull)
     upall = upall.reshape(Z * X * TOK, HD)
-    gq, dkey, dvalue = grads_of_uses(ids, qall, upall, ktab, vtab, sums)
+    gq, dkey, dvalue = grads_of_uses(uses, qall, upall, ktab, vtab, sums)
     dkey, dvalue = (a.reshape((X,) + keys.shape[:1] + (HD,)) for a in (dkey, dvalue))
     grad_queries, grad_keys, grad_values = collect(gq.reshape(Z, X, TOK, HD), dkey, dvalue)
     return out, grad_queries, grad_keys.astype(F32), grad_values.astype(F32)

time: 202 us -> 174 us (0.86)
  Pallas kernels: 189 us -> 161 us
    pallas_call x1, Pallas kernels: 90 us -> 66 us  [project(): pl.pallas_call(project_kernel, out_shape=(jax.ShapeDtypeStruct((2,) + log...]
    pallas_call x1, Pallas kernels: 45.1 us -> 51.1 us  [spread(): pl.pallas_call(spread_kernel, out_shape=(jax.ShapeDtypeStruct((Z, X) + id...]
    pallas_call x1, Pallas kernels: 11.9 us -> 7.35 us  [attend(): pl.pallas_call(attend_kernel, out_shape=(jax.ShapeDtypeStruct((16 * Z, 2...]
    pallas_call x1, Pallas kernels: 10.1 us -> 6.57 us  [grads_of_uses(): pl.pallas_call(grads_kernel, out_shape=(jax.ShapeDtypeStruct((tokens, HD)...]
    unnamed x14 -> x12, local copies, waits for them, and re-layouts: 6.89 us -> 6.88 us
where the time goes in v5:
time: 174 us; the launch traced here: 173 us
  Pallas kernels  161 us (93%)
  local copies, waits for them, and re-layouts  7.07 us (4%)
  other arithmetic  3.92 us (2%)
    pallas_call x1, Pallas kernels, project(): pl.pallas_call(project_kernel, out_shape=(jax.ShapeDtypeStruct((2,) + log...  66 us
    pallas_call x1, Pallas kernels, spread(): pl.pallas_call(spread_kernel, out_shape=(jax.ShapeDtypeStruct((Z, X) + id...  51.1 us
    pallas_call x1, Pallas kernels, collect(): pl.pallas_call(collect_kernel, out_shape=(jax.ShapeDtypeStruct((TOK, X *...  30.3 us
    pallas_call x1, Pallas kernels, attend(): pl.pallas_call(attend_kernel, out_shape=(jax.ShapeDtypeStruct((16 * Z, 2...  7.35 us
    unnamed x12, local copies, waits for them, and re-layouts  6.88 us
    pallas_call x1, Pallas kernels, grads_of_uses(): pl.pallas_call(grads_kernel, out_shape=(jax.ShapeDtypeStruct((tokens, HD)...  6.57 us

profile of v5, /device:TPU:6, one launch (start us, length us, event | category | flops | bytes accessed | tf_op | source)
XLA Modules:
  0.0 173.0 jit_solution(17897942426911492457)
XLA Ops:
  0.6 0.7 pad_add_fusion
  1.3 0.1 copy.12
  1.4 0.1 reshape.35
  1.5 0.0 copy-start
  1.5 1.2 copy-done
  2.8 0.0 copy-start.1
  2.8 1.2 copy-done.1
  4.0 0.0 copy-start.2
  4.0 1.0 copy-done.2
  5.0 0.0 copy-start.3
  5.0 0.9 copy-done.3
  6.0 0.0 copy-start.4
  6.0 0.9 copy-done.4
  6.9 51.1 %spread.1 = (s32[8,4,1,128]{3,2,1,0:T(1,128)S(1)}, bf16[8,4,256,128]{3,2,1,0:T(8,128)(2,1)S(1)}, bf16[4,1024,128]{2,1,0:T(8,128)(2,1)S(1)}, bf16[4,1024,128]{2,1...) custom-call(s32[1,128]{1,0:T(1,128)S(1)} %pad.4.ids_ref, ...), custom_call_target="tpu_custom_call" | custom-call | tf_op jit(solution)/shard_map/spread/pallas_call | solution.py:278
  58.0 7.3 %attend.1 = (f32[128,128]{1,0:T(8,128)S(1)}, bf16[8192,128]{1,0:T(8,128)(2,1)S(1)}, s32[640]{0:T(1024)S(1)}) custom-call(s32[8,4,1,128]{3,2,1,0:T(1,128)S(1)} %get-tuple-element.22.ids, bf16[8192,128]{1,0:T(8,128)(2,1)S(1)} %bitcast.10, bf16[4096,128]{1,0:T(8,128)(2,1)S(1)} %bitcast.12, bf16[4096,128]{1,0:T(8,128)(2,1)S(1)} %bitcast.14), custom_call_target="tpu_custom_call" | custom-call | tf_op jit(solution)/shard_map/attend/pallas_call | solution.py:425
  65.3 66.0 %project.1 = (f32[2,128,128]{2,1,0:T(8,128)S(1)}, bf16[8,4,256,128]{3,2,1,0:T(8,128)(2,1)S(1)}, bf16[32,8192]{1,0:T(8,128)(2,1)S(1)}) custom-call(f32[128,128]{1,0:T(8,128)S(1)} %get-tuple-element.26.logs, bf16[8,4,256,128]{3,2,1,0:T(8,128)(2,1)S(1)} %bitcast.18, bf16[512,2048]{1,0:T(8,128)(2,1)S(1)} %get-tuple-element.28.wf, ...), custom_call_target="tpu_custom_call" | custom-call | tf_op jit(solution)/shard_map/project/pallas_call | solution.py:674
  131.4 6.6 %grads.1 = (bf16[8192,128]{1,0:T(8,128)(2,1)S(1)}, bf16[4096,128]{1,0:T(8,128)(2,1)S(1)}, bf16[4096,128]{1,0:T(8,128)(2,1)S(1)}) custom-call(s32[640]{0:T(1024)S(1)} %get-tuple-element.31.uses, bf16[8192,128]{1,0:T(8,128)(2,1)S(1)} %bitcast.11, bf16[8192,128]{1,0:T(8,128)(2,1)S(1)} %bitcast.17, bf16[4096,128]{1,0:T(8,128)(2,1)S(1)} %bitcast.13, ...), custom_call_target="tpu_custom_call" | custom-call | tf_op jit(solution)/shard_map/grads/pallas_call | solution.py:761
  137.9 30.3 %collect.1 = (bf16[256,512]{1,0:T(8,128)(2,1)S(1)}, bf16[1024,512]{1,0:T(8,128)(2,1)S(1)}, bf16[1024,512]{1,0:T(8,128)(2,1)S(1)}) custom-call(bf16[8,4,256,128]{3,2,1,0:T(8,128)(2,1)S(1)} %bitcast.16, bf16[4,1024,128]{2,1,0:T(8,128)(2,1)S(1)} %bitcast.19, bf16[4,1024,128]{2,1,0:T(8,128)(2,1)S(1)} %bitcast.20), custom_call_target="tpu_custom_call" | custom-call | tf_op jit(solution)/shard_map/collect/pallas_call | solution.py:824
  168.3 1.6 convert_element_type.6
  169.9 1.6 convert_element_type.7
  171.5 0.8 copy.15
  172.3 0.7 copy.16
  (1 shorter events, 0.0 us)
Async XLA Ops:
  1.5 1.2 copy-start
  2.8 1.2 copy-start.1
  4.0 1.0 copy-start.2
  5.0 0.9 copy-start.3
  6.0 0.9 copy-start.4

commit v6 on v5

--- a/solution.py
+++ b/solution.py
@@ -306,14 +306,17 @@
 def list_uses(ids, uses):
     z = lax.rem(lax.axis_index("dp"), Z)
 
-    def add(i, n):
-        dp_z, dp_x = lax.shift_right_logical(i, 5), lax.shift_right_logical(i, 3) & 3
-        owner, name = (ids[dp_z, dp_x, 0, 2 * (i & 7) + j] for j in (0, 1))
-        uses[n] = lax.shift_right_logical(i, 1)
-        uses[LISTED + n] = lax.shift_right_logical(owner, 3) * NB_DEV + name
-        return n + ((owner & 7) == z).astype(jnp.int32)
-
-    n = lax.fori_loop(0, X * Z * 8, add, jnp.int32(0), unroll=8)
+    def add(dp, n):
+        dp_z, dp_x = lax.shift_right_logical(dp, 2), dp & 3
+        named = [ids[dp_z, dp_x, 0, j] for j in range(16)]
+        for j in range(8):
+            owner, name = named[2 * j : 2 * j + 2]
+            uses[n] = dp * 4 + j // 2
+            uses[LISTED + n] = lax.shift_right_logical(owner, 3) * NB_DEV + name
+            n = n + ((owner & 7) == z).astype(jnp.int32)
+        return n
+
+    n = lax.fori_loop(0, X * Z, add, jnp.int32(0), unroll=2)
     last = jnp.maximum(n - 1, 0)
     for i in range(2 * PAIRS - 1):
         uses[n + i] = uses[last]
@@ -449,19 +452,16 @@
     head_cols, span = wf.shape
     slots = TOK // (Y * C)
     xs = [step_from(x, i, X) for i in range(X)]
-    zs = [step_from(z, i, Z) for i in range(Z)]
-    order = (4, 3, 5, 2, 6, 1, 7)
     along_z, along_y = rings(x, z, y, c)
     sibling = device(x, z, y, 1 - c)
     enter(
         [device(xs[i], z, y, c) for i in (1, 2, 3)]
-        + [device(x, zs[i], y, c) for i in order]
+        + list(along_z[2])
         + list(along_y[2])
         + [sibling]
     )
     copies = Copies(send, recv)
     left = lax.broadcasted_iota(jnp.int32, (1, 2 * GROUP), 1) < GROUP
-    own = pl.ds(pl.multiple_of(z * 16, 16), 16)
     up_in, ctx_in, core_in = {}, {}, {}
 
     def multiply_rows(i):
@@ -573,10 +573,6 @@
             for row, value in both_halves(z * 16 + i * 4 + 2 * j, total):
                 sums[1, pl.ds(row, 1), :] = value
 
-    def tell():
-        ref = sums.at[:, own]
-        return [copies.start(ref, ref, device(x, zs[i], y, c)) for i in order]
-
     def swap(i):
         for copy in ctx_in[i]:
             copy.wait_recv()
@@ -615,6 +611,14 @@
                 device_id=device(i, z, y, c),
                 device_id_type=pl.DeviceIdType.MESH,
             ).start()
+
+    told = Gather(
+        copies,
+        sums.at[:, columns(z, 16)],
+        lambda b: sums.at[:, columns(b, 16)],
+        HOPS[0],
+        along_z,
+    )
 
     step_all(contexts, 0)
     weight_in = copies.start(wf, wf_other, sibling)
@@ -629,11 +633,15 @@
         share(i)
     weight_in.wait_recv()
     step_all(upstream[:2], 1)
+    for i in range(X):
+        inner(i)
+    told.step(0)
     swap(0)
     multiply(0)
     step_all(upstream[2:], 1)
     swap(1)
     multiply(1)
+    told.step(1)
     step_all(upstream[:2], 2)
     swap(2)
     multiply(2)
@@ -641,19 +649,17 @@
     swap(3)
     step_all(outs[:1], 1)
     multiply(3)
-    for i in range(X):
-        inner(i)
-    told = tell()
+    told.step(2)
     step_all(outs[1:2], 1)
     step_all(upstream, 3)
     step_all(outs[2:], 1)
+    told.step(3)
     finish_out(0)
     finish_out(1)
     step_all(upstream, 4)
+    told.step(4)
     finish_out(2)
     finish_out(3)
-    for copy in told:
-        copy.wait_recv()
     for i in (1, 2, 3):
         copy = pltpu.make_async_remote_copy(
             src_ref=done.at[0],
@@ -844,6 +850,45 @@
     )(gq, dkey, dvalue)
 
 
+def finish_kernel(out, gq, dkey, dvalue, out_to, gq_to, dk_to, dv_to, wide, sems):
+    copies = []
+
+    def send(src, dst):
+        copies.append(pltpu.make_async_copy(src, dst, sems.at[len(copies)]))
+        copies[-1].start()
+
+    rows = dkey.shape[0] // 4
+    for i, (src, dst) in enumerate(((dkey, dk_to), (dvalue, dv_to))):
+        for j in range(4):
+            at = pl.ds(j * rows, rows)
+            wide[i, at] = src[at].astype(F32)
+            send(wide.at[i, at], dst.at[at])
+    send(out, out_to)
+    send(gq, gq_to)
+    for copy in copies:
+        copy.wait()
+
+
+def finish(out, gq, dkey, dvalue):
+    return pl.pallas_call(
+        finish_kernel,
+        out_shape=(
+            jax.ShapeDtypeStruct(out.shape, BF),
+            jax.ShapeDtypeStruct(gq.shape, BF),
+            jax.ShapeDtypeStruct(dkey.shape, F32),
+            jax.ShapeDtypeStruct(dvalue.shape, F32),
+        ),
+        in_specs=[VMEM] * 4,
+        out_specs=[HBM] * 4,
+        scratch_shapes=[
+            pltpu.VMEM((2,) + dkey.shape, F32),
+            pltpu.SemaphoreType.DMA((10,)),
+        ],
+        compiler_params=pltpu.CompilerParams(vmem_limit_bytes=LIMIT),
+        name="finish",
+    )(out, gq, dkey, dvalue)
+
+
 def shards(queries, keys, values, out_weight, grad_out, neighbour_owner, neighbour_local):
     ids = jnp.stack([neighbour_owner, neighbour_local], axis=-1).reshape(1, -1)
     ids = jnp.pad(ids, ((0, 0), (0, 128 - ids.shape[1])))
@@ -856,7 +901,7 @@
     gq, dkey, dvalue = grads_of_uses(uses, qall, upall, ktab, vtab, sums)
     dkey, dvalue = (a.reshape((X,) + keys.shape[:1] + (HD,)) for a in (dkey, dvalue))
     grad_queries, grad_keys, grad_values = collect(gq.reshape(Z, X, TOK, HD), dkey, dvalue)
-    return out, grad_queries, grad_keys.astype(F32), grad_values.astype(F32)
+    return finish(out, grad_queries, grad_keys, grad_values)
 
 
 def solution(mesh):

time: 174 us -> 174 us (level); the launches traced: 173 us -> 171 us
  other arithmetic: 3.92 us -> 0.7 us
  Pallas kernels: 161 us -> 164 us
    pallas_call x1, Pallas kernels: 30.3 us -> 33.9 us  [collect(): pl.pallas_call(collect_kernel, out_shape=(jax.ShapeDtypeStruct((TOK, X *...]
    convert_element_type x2 -> x0, other arithmetic: 3.22 us -> none  [shards(): return (out, grad_queries, grad_keys.astype(F32), grad_values.astype(F32))]
    pallas_call x0 -> x1, Pallas kernels: none -> 2.36 us  [finish(): pl.pallas_call(finish_kernel, out_shape=(jax.ShapeDtypeStruct(out.shape,...]
    unnamed x12 -> x10, local copies, waits for them, and re-layouts: 6.88 us -> 5.39 us
where the time goes in v6:
time: 174 us; the launch traced here: 171 us
  Pallas kernels  164 us (94%)
  local copies, waits for them, and re-layouts  5.58 us (3%)
    pallas_call x1, Pallas kernels, project(): pl.pallas_call(project_kernel, out_shape=(jax.ShapeDtypeStruct((2,) + log...  65.2 us
    pallas_call x1, Pallas kernels, spread(): pl.pallas_call(spread_kernel, out_shape=(jax.ShapeDtypeStruct((Z, X) + id...  51.1 us
    pallas_call x1, Pallas kernels, collect(): pl.pallas_call(collect_kernel, out_shape=(jax.ShapeDtypeStruct((TOK, X *...  33.9 us
    pallas_call x1, Pallas kernels, attend(): pl.pallas_call(attend_kernel, out_shape=(jax.ShapeDtypeStruct((16 * Z, 2...  6.16 us
    unnamed x10, local copies, waits for them, and re-layouts  5.39 us
    pallas_call x1, Pallas kernels, grads_of_uses(): pl.pallas_call(grads_kernel, out_shape=(jax.ShapeDtypeStruct((tokens, HD)...  5.29 us

profile of v6, /device:TPU:6, one launch (start us, length us, event | category | flops | bytes accessed | tf_op | source)
XLA Modules:
  0.0 171.2 jit_solution(16004091830648380640)
XLA Ops:
  0.6 0.7 pad_add_fusion
  1.3 0.1 copy.12
  1.4 0.1 reshape.35
  1.5 0.0 copy-start
  1.5 1.2 copy-done
  2.8 0.0 copy-start.1
  2.8 1.2 copy-done.1
  4.0 0.0 copy-start.2
  4.0 1.0 copy-done.2
  5.0 0.0 copy-start.3
  5.0 0.9 copy-done.3
  6.0 0.0 copy-start.4
  6.0 0.9 copy-done.4
  6.9 51.1 %spread.1 = (s32[8,4,1,128]{3,2,1,0:T(1,128)S(1)}, bf16[8,4,256,128]{3,2,1,0:T(8,128)(2,1)S(1)}, bf16[4,1024,128]{2,1,0:T(8,128)(2,1)S(1)}, bf16[4,1024,128]{2,1...) custom-call(s32[1,128]{1,0:T(1,128)S(1)} %pad.4.ids_ref, ...), custom_call_target="tpu_custom_call" | custom-call | tf_op jit(solution)/shard_map/spread/pallas_call | solution.py:278
  58.0 6.2 %attend.1 = (f32[128,128]{1,0:T(8,128)S(1)}, bf16[8192,128]{1,0:T(8,128)(2,1)S(1)}, s32[640]{0:T(1024)S(1)}) custom-call(s32[8,4,1,128]{3,2,1,0:T(1,128)S(1)} %get-tuple-element.22.ids, bf16[8192,128]{1,0:T(8,128)(2,1)S(1)} %bitcast.10, bf16[4096,128]{1,0:T(8,128)(2,1)S(1)} %bitcast.12, bf16[4096,128]{1,0:T(8,128)(2,1)S(1)} %bitcast.14), custom_call_target="tpu_custom_call" | custom-call | tf_op jit(solution)/shard_map/attend/pallas_call | solution.py:428
  64.2 65.2 %project.1 = (f32[2,128,128]{2,1,0:T(8,128)S(1)}, bf16[8,4,256,128]{3,2,1,0:T(8,128)(2,1)S(1)}, bf16[32,8192]{1,0:T(8,128)(2,1)S(1)}) custom-call(f32[128,128]{1,0:T(8,128)S(1)} %get-tuple-element.26.logs, bf16[8,4,256,128]{3,2,1,0:T(8,128)(2,1)S(1)} %bitcast.18, bf16[512,2048]{1,0:T(8,128)(2,1)S(1)} %get-tuple-element.28.wf, ...), custom_call_target="tpu_custom_call" | custom-call | tf_op jit(solution)/shard_map/project/pallas_call | solution.py:680
  129.4 5.3 %grads.1 = (bf16[8192,128]{1,0:T(8,128)(2,1)S(1)}, bf16[4096,128]{1,0:T(8,128)(2,1)S(1)}, bf16[4096,128]{1,0:T(8,128)(2,1)S(1)}) custom-call(s32[640]{0:T(1024)S(1)} %get-tuple-element.31.uses, bf16[8192,128]{1,0:T(8,128)(2,1)S(1)} %bitcast.11, bf16[8192,128]{1,0:T(8,128)(2,1)S(1)} %bitcast.17, bf16[4096,128]{1,0:T(8,128)(2,1)S(1)} %bitcast.13, ...), custom_call_target="tpu_custom_call" | custom-call | tf_op jit(solution)/shard_map/grads/pallas_call | solution.py:767
  134.7 33.9 %collect.1 = (bf16[256,512]{1,0:T(8,128)(2,1)S(1)}, bf16[1024,512]{1,0:T(8,128)(2,1)S(1)}, bf16[1024,512]{1,0:T(8,128)(2,1)S(1)}) custom-call(bf16[8,4,256,128]{3,2,1,0:T(8,128)(2,1)S(1)} %bitcast.16, bf16[4,1024,128]{2,1,0:T(8,128)(2,1)S(1)} %bitcast.19, bf16[4,1024,128]{2,1,0:T(8,128)(2,1)S(1)} %bitcast.20), custom_call_target="tpu_custom_call" | custom-call | tf_op jit(solution)/shard_map/collect/pallas_call | solution.py:830
  168.6 2.4 %finish.1 = (bf16[32,8192]{1,0:T(8,128)(2,1)}, bf16[256,512]{1,0:T(8,128)(2,1)}, f32[1024,512]{1,0:T(8,128)}, f32[1024,512]{1,0:T(8,128)}) custom-call(bf16[32,8192]{1,0:T(8,128)(2,1)S(1)} %get-tuple-element.30.out, bf16[256,512]{1,0:T(8,128)(2,1)S(1)} %get-tuple-element.37.gq, bf16[1024,512]{1,0:T(8,128)(2,1)S(1)} %get-tuple-element.38.dkey, ...), custom_call_target="tpu_custom_call" | custom-call | tf_op jit(solution)/shard_map/finish/pallas_call | solution.py:873
  (1 shorter events, 0.0 us)
Async XLA Ops:
  1.5 1.2 copy-start
  2.8 1.2 copy-start.1
  4.0 1.0 copy-start.2
  5.0 0.9 copy-start.3
  6.0 0.9 copy-start.4

commit v7 on v6

--- a/solution.py
+++ b/solution.py
@@ -624,10 +624,13 @@
     weight_in = copies.start(wf, wf_other, sibling)
     for i in range(X):
         multiply_rows(i)
-    for s in (1, 2, 3):
+    for s in (1, 2):
         step_all(contexts, s)
-    for i in range(X):
-        total_up(i)
+    total_up(0)
+    total_up(1)
+    step_all(contexts, 3)
+    total_up(2)
+    total_up(3)
     for i in range(X):
         contexts[i].step(4)
         share(i)

time: 174 us -> 175 us (level)
  Pallas kernels: 164 us -> 166 us
where the time goes in v7:
time: 175 us; the launch traced here: 173 us
  Pallas kernels  166 us (95%)
  local copies, waits for them, and re-layouts  5.58 us (3%)
    pallas_call x1, Pallas kernels, project(): pl.pallas_call(project_kernel, out_shape=(jax.ShapeDtypeStruct((2,) + log...  66.7 us
    pallas_call x1, Pallas kernels, spread(): pl.pallas_call(spread_kernel, out_shape=(jax.ShapeDtypeStruct((Z, X) + id...  51.1 us
    pallas_call x1, Pallas kernels, collect(): pl.pallas_call(collect_kernel, out_shape=(jax.ShapeDtypeStruct((TOK, X *...  33.4 us
    pallas_call x1, Pallas kernels, grads_of_uses(): pl.pallas_call(grads_kernel, out_shape=(jax.ShapeDtypeStruct((tokens, HD)...  6.57 us
    pallas_call x1, Pallas kernels, attend(): pl.pallas_call(attend_kernel, out_shape=(jax.ShapeDtypeStruct((16 * Z, 2...  6.15 us
    unnamed x10, local copies, waits for them, and re-layouts  5.39 us

profile of v7, /device:TPU:6, one launch (start us, length us, event | category | flops | bytes accessed | tf_op | source)
XLA Modules:
  0.0 173.4 jit_solution(3723681902134915216)
XLA Ops:
  0.6 0.7 pad_add_fusion
  1.3 0.1 copy.12
  1.4 0.1 reshape.35
  1.5 0.0 copy-start
  1.5 1.2 copy-done
  2.8 0.0 copy-start.1
  2.8 1.2 copy-done.1
  4.0 0.0 copy-start.2
  4.0 1.0 copy-done.2
  5.0 0.0 copy-start.3
  5.0 0.9 copy-done.3
  6.0 0.0 copy-start.4
  6.0 0.9 copy-done.4
  6.9 51.1 %spread.1 = (s32[8,4,1,128]{3,2,1,0:T(1,128)S(1)}, bf16[8,4,256,128]{3,2,1,0:T(8,128)(2,1)S(1)}, bf16[4,1024,128]{2,1,0:T(8,128)(2,1)S(1)}, bf16[4,1024,128]{2,1...) custom-call(s32[1,128]{1,0:T(1,128)S(1)} %pad.4.ids_ref, ...), custom_call_target="tpu_custom_call" | custom-call | tf_op jit(solution)/shard_map/spread/pallas_call | solution.py:278
  58.0 6.1 %attend.1 = (f32[128,128]{1,0:T(8,128)S(1)}, bf16[8192,128]{1,0:T(8,128)(2,1)S(1)}, s32[640]{0:T(1024)S(1)}) custom-call(s32[8,4,1,128]{3,2,1,0:T(1,128)S(1)} %get-tuple-element.22.ids, bf16[8192,128]{1,0:T(8,128)(2,1)S(1)} %bitcast.10, bf16[4096,128]{1,0:T(8,128)(2,1)S(1)} %bitcast.12, bf16[4096,128]{1,0:T(8,128)(2,1)S(1)} %bitcast.14), custom_call_target="tpu_custom_call" | custom-call | tf_op jit(solution)/shard_map/attend/pallas_call | solution.py:428
  64.1 66.7 %project.1 = (f32[2,128,128]{2,1,0:T(8,128)S(1)}, bf16[8,4,256,128]{3,2,1,0:T(8,128)(2,1)S(1)}, bf16[32,8192]{1,0:T(8,128)(2,1)S(1)}) custom-call(f32[128,128]{1,0:T(8,128)S(1)} %get-tuple-element.26.logs, bf16[8,4,256,128]{3,2,1,0:T(8,128)(2,1)S(1)} %bitcast.18, bf16[512,2048]{1,0:T(8,128)(2,1)S(1)} %get-tuple-element.28.wf, ...), custom_call_target="tpu_custom_call" | custom-call | tf_op jit(solution)/shard_map/project/pallas_call | solution.py:683
  130.9 6.6 %grads.1 = (bf16[8192,128]{1,0:T(8,128)(2,1)S(1)}, bf16[4096,128]{1,0:T(8,128)(2,1)S(1)}, bf16[4096,128]{1,0:T(8,128)(2,1)S(1)}) custom-call(s32[640]{0:T(1024)S(1)} %get-tuple-element.31.uses, bf16[8192,128]{1,0:T(8,128)(2,1)S(1)} %bitcast.11, bf16[8192,128]{1,0:T(8,128)(2,1)S(1)} %bitcast.17, bf16[4096,128]{1,0:T(8,128)(2,1)S(1)} %bitcast.13, ...), custom_call_target="tpu_custom_call" | custom-call | tf_op jit(solution)/shard_map/grads/pallas_call | solution.py:770
  137.5 33.4 %collect.1 = (bf16[256,512]{1,0:T(8,128)(2,1)S(1)}, bf16[1024,512]{1,0:T(8,128)(2,1)S(1)}, bf16[1024,512]{1,0:T(8,128)(2,1)S(1)}) custom-call(bf16[8,4,256,128]{3,2,1,0:T(8,128)(2,1)S(1)} %bitcast.16, bf16[4,1024,128]{2,1,0:T(8,128)(2,1)S(1)} %bitcast.19, bf16[4,1024,128]{2,1,0:T(8,128)(2,1)S(1)} %bitcast.20), custom_call_target="tpu_custom_call" | custom-call | tf_op jit(solution)/shard_map/collect/pallas_call | solution.py:833
  170.9 2.4 %finish.1 = (bf16[32,8192]{1,0:T(8,128)(2,1)}, bf16[256,512]{1,0:T(8,128)(2,1)}, f32[1024,512]{1,0:T(8,128)}, f32[1024,512]{1,0:T(8,128)}) custom-call(bf16[32,8192]{1,0:T(8,128)(2,1)S(1)} %get-tuple-element.30.out, bf16[256,512]{1,0:T(8,128)(2,1)S(1)} %get-tuple-element.37.gq, bf16[1024,512]{1,0:T(8,128)(2,1)S(1)} %get-tuple-element.38.dkey, ...), custom_call_target="tpu_custom_call" | custom-call | tf_op jit(solution)/shard_map/finish/pallas_call | solution.py:876
  (1 shorter events, 0.0 us)
Async XLA Ops:
  1.5 1.2 copy-start
  2.8 1.2 copy-start.1
  4.0 1.0 copy-start.2
  5.0 0.9 copy-start.3
  6.0 0.9 copy-start.4
